TPU v7x, 32 devices: a whole 2x2x4 slice. The times are simulated.
32 devices in a mesh: dp: 8 (over z, x), mp: 4 (over y, core).
Axes of the slice: x: 2, y: 2, z: 4, core: 2. Of those that a mesh axis runs over, the one named last changes fastest.
Arguments:
- text_in: bfloat16 [12288, 768], P(('dp', 'mp')), may hold values from -6 to 6
- image_in: bfloat16 [6144, 1024], P(('dp', 'mp')), may hold values from -6 to 6
- caption_lengths: int32 [192], P('dp'), may hold values from 1 to 64, 7680 in all
- region_lengths: int32 [48, 4], P('dp'), may hold values from 1 to 80, 128 in all within a row
- image_caption: int32 [8, 24], P('dp'), may hold values from 0 to 23, each once within a row
- co_text_qkv: bfloat16 [3, 768, 1024], P(None, None, 'mp'), may hold values from -0.21875 to 0.21875
- co_image_qkv: bfloat16 [3, 1024, 1024], P(None, None, 'mp'), may hold values from -0.1875 to 0.1875
- co_text_out: bfloat16 [1024, 768], P('mp'), may hold values from -1 to 1
- co_image_out: bfloat16 [1024, 1024], P('mp'), may hold values from -1 to 1
- text_up: bfloat16 [768, 3072], P(None, 'mp'), may hold values from -0.21875 to 0.21875
- text_down: bfloat16 [3072, 768], P('mp'), may hold values from -0.109375 to 0.109375
- image_up: bfloat16 [1024, 1024], P(None, 'mp'), may hold values from -0.1875 to 0.1875
- image_down: bfloat16 [1024, 1024], P('mp'), may hold values from -0.1875 to 0.1875
- text_self_qkv: bfloat16 [3, 768, 768], P(None, None, 'mp'), may hold values from -0.21875 to 0.21875
- text_self_out: bfloat16 [768, 768], P('mp'), may hold values from -1 to 1
- image_self_qkv: bfloat16 [3, 1024, 1024], P(None, None, 'mp'), may hold values from -0.1875 to 0.1875
- image_self_out: bfloat16 [1024, 1024], P('mp'), may hold values from -1 to 1
- text_gains: float32 [3, 768], replicated, may hold values from 0.5 to 1.5
- text_shifts: float32 [3, 768], replicated, may hold values from -3 to 3
- image_gains: float32 [3, 1024], replicated, may hold values from 0.5 to 1.5
- image_shifts: float32 [3, 1024], replicated, may hold values from -3 to 3
- text_grad_out: bfloat16 [12288, 768], P(('dp', 'mp')), may hold values from -6 to 6
- image_grad_out: bfloat16 [6144, 1024], P(('dp', 'mp')), may hold values from -6 to 6
Outputs:
- text_out: bfloat16 [12288, 768], P(('dp', 'mp'))
- image_out: bfloat16 [6144, 1024], P(('dp', 'mp'))
- text_in_grad: float32 [12288, 768], P(('dp', 'mp'))
- image_in_grad: float32 [6144, 1024], P(('dp', 'mp'))
- co_text_qkv_grad: float32 [3, 768, 1024], P(None, 'dp', 'mp')
- co_image_qkv_grad: float32 [3, 1024, 1024], P(None, 'dp', 'mp')
- co_text_out_grad: float32 [1024, 768], P('mp', 'dp')
- co_image_out_grad: float32 [1024, 1024], P('mp', 'dp')
- text_up_grad: float32 [768, 3072], P('dp', 'mp')
- text_down_grad: float32 [3072, 768], P('mp', 'dp')
- image_up_grad: float32 [1024, 1024], P('dp', 'mp')
- image_down_grad: float32 [1024, 1024], P('mp', 'dp')
- text_self_qkv_grad: float32 [3, 768, 768], P(None, 'dp', 'mp')
- text_self_out_grad: float32 [768, 768], P('mp', 'dp')
- image_self_qkv_grad: float32 [3, 1024, 1024], P(None, 'dp', 'mp')
- image_self_out_grad: float32 [1024, 1024], P('mp', 'dp')
- text_gains_grad: float32 [3, 768], P(None, ('dp', 'mp'))
- text_shifts_grad: float32 [3, 768], P(None, ('dp', 'mp'))
- image_gains_grad: float32 [3, 1024], P(None, ('dp', 'mp'))
- image_shifts_grad: float32 [3, 1024], P(None, ('dp', 'mp'))
Inputs may be any that keep to these rules, and one draw needn't show every extreme that they name: `region_lengths`: each row's 4 counts sum to 128. `image_caption`: each row is a permutation.
All inputs are finite; a program needn't handle non-finite values. No bound on the sum of `caption_lengths` on one device may be relied on, other than what follows from the above.
Results may differ from a plain program's by a relative error of at most 0.04.
Values may be sent and summed in bfloat16 or wider, within the bound.
A program may use at most 192 MiB of HBM per device.

v0:
```python
import jax
import jax.numpy as jnp
from jax import lax
from jax.sharding import PartitionSpec as P

CO_HEADS = 8
TEXT_HEADS = 12
IMAGE_HEADS = 8
CAP_LEN = 64
ROW_LEN = 128
PER_ROW = 4


epsilon = 1e-05


def product(former, latter):
    return jnp.dot(former, latter, preferred_element_type=jnp.float32)


def product_tn(former, latter):
    return lax.dot_general(
        former, latter, (((0,), (0,)), ((), ())), preferred_element_type=jnp.float32
    )


def product_nt(former, latter):
    return lax.dot_general(
        former, latter, (((1,), (1,)), ((), ())), preferred_element_type=jnp.float32
    )


def layer_norm(values, norm_gain, norm_shift):
    centre = values - jnp.mean(values, axis=-1, keepdims=True)
    spread = jnp.mean(centre * centre, axis=-1, keepdims=True)
    return centre * lax.rsqrt(spread + epsilon) * norm_gain + norm_shift


def gelu_tanh(values):
    return (
        0.5
        * values
        * (1.0 + jnp.tanh(0.7978845608028654 * (values + 0.044715 * values * values * values)))
    )


def norm_back(values, norm_gain, norm_shift, gradient):
    _, pullback = jax.vjp(layer_norm, values, norm_gain, norm_shift)
    return pullback(gradient)


def layout(cap_len, reg_len, image_order):
    caption_count = image_order.shape[0]
    row_count = caption_count // PER_ROW
    places = jnp.arange(ROW_LEN, dtype=jnp.int32)
    ends = jnp.cumsum(reg_len, axis=1)
    region_slot = jnp.sum((places[None, :, None] >= ends[:, None, :]).astype(jnp.int32), axis=2)
    labels = jnp.arange(caption_count, dtype=jnp.int32)
    inverse = jnp.sum(
        labels[None, :] * (image_order[None, :] == labels[:, None]).astype(jnp.int32), axis=1
    )
    spots = jnp.arange(PER_ROW * CAP_LEN, dtype=jnp.int32)
    slot_len = jnp.take(cap_len, image_order).reshape(row_count, PER_ROW)
    text_live = (spots % CAP_LEN)[None, :] < jnp.repeat(slot_len, CAP_LEN, axis=1)
    to_image = (spots // CAP_LEN)[None, :, None] == region_slot[:, None, :]
    to_text = jnp.swapaxes(to_image, 1, 2) & text_live[:, None, :]
    among_regions = region_slot[:, :, None] == region_slot[:, None, :]
    pairs = jnp.arange(2 * CAP_LEN, dtype=jnp.int32)
    pair_live = (pairs % CAP_LEN)[None, :] < jnp.repeat(
        cap_len.reshape(caption_count // 2, 2), CAP_LEN, axis=1
    )
    same_caption = (pairs // CAP_LEN)[:, None] == (pairs // CAP_LEN)[None, :]
    among_tokens = same_caption[None] & pair_live[:, None, :]
    return (inverse, to_image, to_text, among_regions, among_tokens)


def split_heads(values, head_count):
    blocks, length, inner_width = values.shape
    return values.reshape(blocks, length, head_count, inner_width // head_count)


def score_block(split_q, split_k, key_mask):
    scaling = split_q.shape[-1] ** (-0.5)
    scores = (
        jnp.einsum("bqhd,bkhd->bhqk", split_q, split_k, preferred_element_type=jnp.float32)
        * scaling
    )
    return (jnp.where(key_mask[:, None], scores, -1000000000.0), scaling)


def attend_forward(queries, key_rows, value_rows, key_mask, head_count):
    split_q = split_heads(queries, head_count)
    split_k = split_heads(key_rows, head_count)
    split_v = split_heads(value_rows, head_count)
    scores, scaling = score_block(split_q, split_k, key_mask)
    row_max = jnp.max(scores, axis=-1, keepdims=True)
    exponent = jnp.exp(scores - row_max)
    row_sum = jnp.sum(exponent, axis=-1, keepdims=True)
    shares = (exponent / row_sum).astype(jnp.bfloat16)
    context = jnp.einsum("bhqk,bkhd->bqhd", shares, split_v, preferred_element_type=jnp.float32)
    return (context.reshape(queries.shape).astype(jnp.bfloat16), row_max + jnp.log(row_sum))


def attend_back(queries, key_rows, value_rows, key_mask, head_count, log_total, context_grad):
    split_q = split_heads(queries, head_count)
    split_k = split_heads(key_rows, head_count)
    split_v = split_heads(value_rows, head_count)
    split_g = split_heads(context_grad, head_count)
    scores, scaling = score_block(split_q, split_k, key_mask)
    shares = jnp.exp(scores - log_total)
    share_grad = jnp.einsum("bqhd,bkhd->bhqk", split_g, split_v, preferred_element_type=jnp.float32)
    inner_sum = jnp.sum(share_grad * shares, axis=-1, keepdims=True)
    score_grad = (shares * (share_grad - inner_sum) * scaling).astype(jnp.bfloat16)
    query_grad = jnp.einsum(
        "bhqk,bkhd->bqhd", score_grad, split_k, preferred_element_type=jnp.float32
    )
    key_grad = jnp.einsum(
        "bhqk,bqhd->bkhd", score_grad, split_q, preferred_element_type=jnp.float32
    )
    value_grad = jnp.einsum(
        "bhqk,bqhd->bkhd", shares.astype(jnp.bfloat16), split_g, preferred_element_type=jnp.float32
    )
    return (
        query_grad.reshape(queries.shape).astype(jnp.bfloat16),
        key_grad.reshape(key_rows.shape).astype(jnp.bfloat16),
        value_grad.reshape(value_rows.shape).astype(jnp.bfloat16),
    )


def project_three(rows_in, stacked):
    return [product(rows_in, stacked[member]).astype(jnp.bfloat16) for member in range(3)]


def project_three_back(rows_in, stacked, gradients):
    weight_grad = jnp.stack([product_tn(rows_in, gradients[member]) for member in range(3)])
    input_grad = (
        product_nt(gradients[0], stacked[0])
        + product_nt(gradients[1], stacked[1])
        + product_nt(gradients[2], stacked[2])
    )
    return (weight_grad, input_grad)


def arrange(stacked, group_count, part_count):
    height, breadth = stacked.shape
    blocked = stacked.reshape(
        height, group_count, part_count, breadth // (group_count * part_count)
    )
    return jnp.transpose(blocked, (0, 2, 1, 3)).reshape(height, breadth)


def per_device(
    text_in,
    image_in,
    caption_lengths,
    region_lengths,
    image_caption,
    co_text_qkv,
    co_image_qkv,
    co_text_out,
    co_image_out,
    text_up,
    text_down,
    image_up,
    image_down,
    text_self_qkv,
    text_self_out,
    image_self_qkv,
    image_self_out,
    text_gains,
    text_shifts,
    image_gains,
    image_shifts,
    text_grad_out,
    image_grad_out,
):
    image_order = image_caption[0]
    caption_count = image_order.shape[0]
    row_count = caption_count // PER_ROW
    text_width = text_in.shape[1]
    part_count = lax.axis_size("mp")
    group_count = lax.axis_size("dp")
    co_local = CO_HEADS // part_count
    text_local = TEXT_HEADS // part_count
    image_local = IMAGE_HEADS // part_count
    inverse, to_image, to_text, among_regions, among_tokens = layout(
        caption_lengths, region_lengths, image_order
    )

    def co_forward(text_all, image_all):
        text_order = jnp.take(
            text_all.reshape(caption_count, CAP_LEN, text_width), image_order, axis=0
        ).reshape(caption_count * CAP_LEN, text_width)
        text_side = [
            tensor.reshape(row_count, PER_ROW * CAP_LEN, -1)
            for tensor in project_three(text_order, co_text_qkv)
        ]
        image_side = [
            tensor.reshape(row_count, ROW_LEN, -1)
            for tensor in project_three(image_all, co_image_qkv)
        ]
        text_context, text_total = attend_forward(
            text_side[0], image_side[1], image_side[2], to_image, co_local
        )
        image_context, image_total = attend_forward(
            image_side[0], text_side[1], text_side[2], to_text, co_local
        )
        text_caps = jnp.take(
            text_context.reshape(caption_count, CAP_LEN, -1), inverse, axis=0
        ).reshape(caption_count * CAP_LEN, -1)
        image_flat = image_context.reshape(row_count * ROW_LEN, -1)
        return (
            image_all,
            text_order,
            text_side,
            image_side,
            text_total,
            image_total,
            text_caps,
            image_flat,
        )

    text_all, image_all = (
        lax.all_gather(text_in, "mp", axis=0, tiled=True),
        lax.all_gather(image_in, "mp", axis=0, tiled=True),
    )
    co_state = co_forward(text_all, image_all)
    text_attn, image_attn = (
        lax.psum_scatter(
            product(co_state[6], co_text_out).astype(jnp.bfloat16),
            "mp",
            scatter_dimension=0,
            tiled=True,
        ).astype(jnp.float32),
        lax.psum_scatter(
            product(co_state[7], co_image_out).astype(jnp.bfloat16),
            "mp",
            scatter_dimension=0,
            tiled=True,
        ).astype(jnp.float32),
    )
    text_zero = text_in.astype(jnp.float32) + text_attn
    image_zero = image_in.astype(jnp.float32) + image_attn
    text_first = layer_norm(text_zero, text_gains[0], text_shifts[0])
    image_first = layer_norm(image_zero, image_gains[0], image_shifts[0])
    text_mlp_in, image_mlp_in = (
        lax.all_gather(text_first.astype(jnp.bfloat16), "mp", axis=0, tiled=True),
        lax.all_gather(image_first.astype(jnp.bfloat16), "mp", axis=0, tiled=True),
    )
    text_pre = product(text_mlp_in, text_up)
    image_pre = product(image_mlp_in, image_up)
    text_act = gelu_tanh(text_pre).astype(jnp.bfloat16)
    image_act = gelu_tanh(image_pre).astype(jnp.bfloat16)
    text_mlp, image_mlp = (
        lax.psum_scatter(
            product(text_act, text_down).astype(jnp.bfloat16), "mp", scatter_dimension=0, tiled=True
        ).astype(jnp.float32),
        lax.psum_scatter(
            product(image_act, image_down).astype(jnp.bfloat16),
            "mp",
            scatter_dimension=0,
            tiled=True,
        ).astype(jnp.float32),
    )
    text_mid = text_first + text_mlp
    image_mid = image_first + image_mlp
    text_second = layer_norm(text_mid, text_gains[1], text_shifts[1])
    image_second = layer_norm(image_mid, image_gains[1], image_shifts[1])
    text_self_in, image_self_in = (
        lax.all_gather(text_second.astype(jnp.bfloat16), "mp", axis=0, tiled=True),
        lax.all_gather(image_second.astype(jnp.bfloat16), "mp", axis=0, tiled=True),
    )
    text_parts = [
        tensor.reshape(caption_count // 2, 2 * CAP_LEN, -1)
        for tensor in project_three(text_self_in, text_self_qkv)
    ]
    image_parts = [
        tensor.reshape(row_count, ROW_LEN, -1)
        for tensor in project_three(image_self_in, image_self_qkv)
    ]
    text_self_ctx, text_self_total = attend_forward(
        text_parts[0], text_parts[1], text_parts[2], among_tokens, text_local
    )
    image_self_ctx, image_self_total = attend_forward(
        image_parts[0], image_parts[1], image_parts[2], among_regions, image_local
    )
    text_self_rows = text_self_ctx.reshape(caption_count * CAP_LEN, -1)
    image_self_rows = image_self_ctx.reshape(row_count * ROW_LEN, -1)
    text_late, image_late = (
        lax.psum_scatter(
            product(text_self_rows, text_self_out).astype(jnp.bfloat16),
            "mp",
            scatter_dimension=0,
            tiled=True,
        ).astype(jnp.float32),
        lax.psum_scatter(
            product(image_self_rows, image_self_out).astype(jnp.bfloat16),
            "mp",
            scatter_dimension=0,
            tiled=True,
        ).astype(jnp.float32),
    )
    text_last = text_second + text_late
    image_last = image_second + image_late
    text_result = layer_norm(text_last, text_gains[2], text_shifts[2])
    image_result = layer_norm(image_last, image_gains[2], image_shifts[2])
    text_late_grad, text_gain_c, text_shift_c = norm_back(
        text_last, text_gains[2], text_shifts[2], text_grad_out.astype(jnp.float32)
    )
    image_late_grad, image_gain_c, image_shift_c = norm_back(
        image_last, image_gains[2], image_shifts[2], image_grad_out.astype(jnp.float32)
    )
    text_late_all, image_late_all = (
        lax.all_gather(text_late_grad.astype(jnp.bfloat16), "mp", axis=0, tiled=True),
        lax.all_gather(image_late_grad.astype(jnp.bfloat16), "mp", axis=0, tiled=True),
    )
    grad_text_self_out = product_tn(text_self_rows, text_late_all)
    grad_image_self_out = product_tn(image_self_rows, image_late_all)
    text_ctx_grad = (
        product_nt(text_late_all, text_self_out).astype(jnp.bfloat16).reshape(text_self_ctx.shape)
    )
    image_ctx_grad = (
        product_nt(image_late_all, image_self_out)
        .astype(jnp.bfloat16)
        .reshape(image_self_ctx.shape)
    )
    text_self_grads = attend_back(
        text_parts[0],
        text_parts[1],
        text_parts[2],
        among_tokens,
        text_local,
        text_self_total,
        text_ctx_grad,
    )
    image_self_grads = attend_back(
        image_parts[0],
        image_parts[1],
        image_parts[2],
        among_regions,
        image_local,
        image_self_total,
        image_ctx_grad,
    )
    grad_text_self_qkv, text_self_input_grad = project_three_back(
        text_self_in,
        text_self_qkv,
        [tensor.reshape(caption_count * CAP_LEN, -1) for tensor in text_self_grads],
    )
    grad_image_self_qkv, image_self_input_grad = project_three_back(
        image_self_in,
        image_self_qkv,
        [tensor.reshape(row_count * ROW_LEN, -1) for tensor in image_self_grads],
    )
    text_back_self, image_back_self = (
        lax.psum_scatter(
            text_self_input_grad.astype(jnp.bfloat16), "mp", scatter_dimension=0, tiled=True
        ).astype(jnp.float32),
        lax.psum_scatter(
            image_self_input_grad.astype(jnp.bfloat16), "mp", scatter_dimension=0, tiled=True
        ).astype(jnp.float32),
    )
    text_mid_grad, text_gain_b, text_shift_b = norm_back(
        text_mid, text_gains[1], text_shifts[1], text_late_grad + text_back_self
    )
    image_mid_grad, image_gain_b, image_shift_b = norm_back(
        image_mid, image_gains[1], image_shifts[1], image_late_grad + image_back_self
    )
    text_mlp_all, image_mlp_all = (
        lax.all_gather(text_mid_grad.astype(jnp.bfloat16), "mp", axis=0, tiled=True),
        lax.all_gather(image_mid_grad.astype(jnp.bfloat16), "mp", axis=0, tiled=True),
    )
    grad_text_down = product_tn(text_act, text_mlp_all)
    grad_image_down = product_tn(image_act, image_mlp_all)
    _, text_gelu_pull = jax.vjp(gelu_tanh, text_pre)
    _, image_gelu_pull = jax.vjp(gelu_tanh, image_pre)
    text_pre_grad = text_gelu_pull(product_nt(text_mlp_all, text_down))[0].astype(jnp.bfloat16)
    image_pre_grad = image_gelu_pull(product_nt(image_mlp_all, image_down))[0].astype(jnp.bfloat16)
    grad_text_up = product_tn(text_mlp_in, text_pre_grad)
    grad_image_up = product_tn(image_mlp_in, image_pre_grad)
    text_back_mlp, image_back_mlp = (
        lax.psum_scatter(
            product_nt(text_pre_grad, text_up).astype(jnp.bfloat16),
            "mp",
            scatter_dimension=0,
            tiled=True,
        ).astype(jnp.float32),
        lax.psum_scatter(
            product_nt(image_pre_grad, image_up).astype(jnp.bfloat16),
            "mp",
            scatter_dimension=0,
            tiled=True,
        ).astype(jnp.float32),
    )
    text_zero_grad, text_gain_a, text_shift_a = norm_back(
        text_zero, text_gains[0], text_shifts[0], text_mid_grad + text_back_mlp
    )
    image_zero_grad, image_gain_a, image_shift_a = norm_back(
        image_zero, image_gains[0], image_shifts[0], image_mid_grad + image_back_mlp
    )
    text_norm_stack = arrange(
        jnp.stack(
            [text_gain_a, text_gain_b, text_gain_c, text_shift_a, text_shift_b, text_shift_c]
        ),
        group_count,
        part_count,
    )
    image_norm_stack = arrange(
        jnp.stack(
            [image_gain_a, image_gain_b, image_gain_c, image_shift_a, image_shift_b, image_shift_c]
        ),
        group_count,
        part_count,
    )
    text_co_all, image_co_all = (
        lax.all_gather(text_zero_grad.astype(jnp.bfloat16), "mp", axis=0, tiled=True),
        lax.all_gather(image_zero_grad.astype(jnp.bfloat16), "mp", axis=0, tiled=True),
    )
    text_again, image_again = (
        lax.all_gather(text_in, "mp", axis=0, tiled=True),
        lax.all_gather(image_in, "mp", axis=0, tiled=True),
    )
    back_state = co_forward(text_again, image_again)
    (
        image_rows_all,
        text_order,
        text_side,
        image_side,
        text_total,
        image_total,
        text_caps,
        image_flat,
    ) = back_state
    grad_co_text_out = product_tn(text_caps, text_co_all)
    grad_co_image_out = product_tn(image_flat, image_co_all)
    text_caps_grad = product_nt(text_co_all, co_text_out).astype(jnp.bfloat16)
    text_co_ctx_grad = jnp.take(
        text_caps_grad.reshape(caption_count, CAP_LEN, -1), image_order, axis=0
    ).reshape(text_side[0].shape)
    image_co_ctx_grad = (
        product_nt(image_co_all, co_image_out).astype(jnp.bfloat16).reshape(image_side[0].shape)
    )
    text_query_grad, image_key_grad, image_value_grad = attend_back(
        text_side[0], image_side[1], image_side[2], to_image, co_local, text_total, text_co_ctx_grad
    )
    image_query_grad, text_key_grad, text_value_grad = attend_back(
        image_side[0], text_side[1], text_side[2], to_text, co_local, image_total, image_co_ctx_grad
    )
    text_flat_grads = [
        tensor.reshape(caption_count * CAP_LEN, -1)
        for tensor in (text_query_grad, text_key_grad, text_value_grad)
    ]
    image_flat_grads = [
        tensor.reshape(row_count * ROW_LEN, -1)
        for tensor in (image_query_grad, image_key_grad, image_value_grad)
    ]
    grad_co_text_qkv, text_order_grad = project_three_back(text_order, co_text_qkv, text_flat_grads)
    grad_co_image_qkv, image_input_grad = project_three_back(
        image_rows_all, co_image_qkv, image_flat_grads
    )
    text_input_grad = jnp.take(
        text_order_grad.reshape(caption_count, CAP_LEN, -1), inverse, axis=0
    ).reshape(caption_count * CAP_LEN, -1)
    text_back_co, image_back_co, text_norm_part, image_norm_part = (
        lax.psum_scatter(
            text_input_grad.astype(jnp.bfloat16), "mp", scatter_dimension=0, tiled=True
        ).astype(jnp.float32),
        lax.psum_scatter(
            image_input_grad.astype(jnp.bfloat16), "mp", scatter_dimension=0, tiled=True
        ).astype(jnp.float32),
        lax.psum_scatter(
            text_norm_stack.astype(jnp.bfloat16), "mp", scatter_dimension=1, tiled=True
        ).astype(jnp.float32),
        lax.psum_scatter(
            image_norm_stack.astype(jnp.bfloat16), "mp", scatter_dimension=1, tiled=True
        ).astype(jnp.float32),
    )
    text_in_grad = text_zero_grad + text_back_co
    image_in_grad = image_zero_grad + image_back_co
    summed = (
        lax.psum_scatter(grad_co_text_qkv, "dp", scatter_dimension=1, tiled=True),
        lax.psum_scatter(grad_co_image_qkv, "dp", scatter_dimension=1, tiled=True),
        lax.psum_scatter(grad_co_text_out, "dp", scatter_dimension=1, tiled=True),
        lax.psum_scatter(grad_co_image_out, "dp", scatter_dimension=1, tiled=True),
        lax.psum_scatter(grad_text_up, "dp", scatter_dimension=0, tiled=True),
        lax.psum_scatter(grad_text_down, "dp", scatter_dimension=1, tiled=True),
        lax.psum_scatter(grad_image_up, "dp", scatter_dimension=0, tiled=True),
        lax.psum_scatter(grad_image_down, "dp", scatter_dimension=1, tiled=True),
        lax.psum_scatter(grad_text_self_qkv, "dp", scatter_dimension=1, tiled=True),
        lax.psum_scatter(grad_text_self_out, "dp", scatter_dimension=1, tiled=True),
        lax.psum_scatter(grad_image_self_qkv, "dp", scatter_dimension=1, tiled=True),
        lax.psum_scatter(grad_image_self_out, "dp", scatter_dimension=1, tiled=True),
        lax.psum_scatter(text_norm_part, "dp", scatter_dimension=1, tiled=True),
        lax.psum_scatter(image_norm_part, "dp", scatter_dimension=1, tiled=True),
    )
    return (
        text_result.astype(jnp.bfloat16),
        image_result.astype(jnp.bfloat16),
        text_in_grad,
        image_in_grad,
        summed[0],
        summed[1],
        summed[2],
        summed[3],
        summed[4],
        summed[5],
        summed[6],
        summed[7],
        summed[8],
        summed[9],
        summed[10],
        summed[11],
        summed[12][:3],
        summed[12][3:],
        summed[13][:3],
        summed[13][3:],
    )


def solution(mesh):
    in_specs = (
        P(("dp", "mp"), None),
        P(("dp", "mp"), None),
        P("dp"),
        P("dp", None),
        P("dp", None),
        P(None, None, "mp"),
        P(None, None, "mp"),
        P("mp", None),
        P("mp", None),
        P(None, "mp"),
        P("mp", None),
        P(None, "mp"),
        P("mp", None),
        P(None, None, "mp"),
        P("mp", None),
        P(None, None, "mp"),
        P("mp", None),
        P(),
        P(),
        P(),
        P(),
        P(("dp", "mp"), None),
        P(("dp", "mp"), None),
    )
    out_specs = (
        P(("dp", "mp"), None),
        P(("dp", "mp"), None),
        P(("dp", "mp"), None),
        P(("dp", "mp"), None),
        P(None, "dp", "mp"),
        P(None, "dp", "mp"),
        P("mp", "dp"),
        P("mp", "dp"),
        P("dp", "mp"),
        P("mp", "dp"),
        P("dp", "mp"),
        P("mp", "dp"),
        P(None, "dp", "mp"),
        P("mp", "dp"),
        P(None, "dp", "mp"),
        P("mp", "dp"),
        P(None, ("dp", "mp")),
        P(None, ("dp", "mp")),
        P(None, ("dp", "mp")),
        P(None, ("dp", "mp")),
    )
    return jax.shard_map(
        per_device, mesh=mesh, in_specs=in_specs, out_specs=out_specs, check_vma=False
    )
```

profile of v0, /device:TPU:0, one launch (start us, length us, event | category | flops | bytes accessed | tf_op | source)
XLA Modules:
  0.0 1671.0 jit_solution(11098915400663737033)
XLA Ops:
  16.2 15.8 all-gather.13.cloned.1.call-done
  35.2 22.4 %all-gather.15.cloned.1.call-done = bf16[1536,768]{1,0:T(8,128)(2,1)} async-done(((bf16[384,768]{1,0:T(8,128)(2,1)}), bf16[1536,768]{1,0:T(8,128)(2,1)}) %all-gather.15.cloned.1.call-update) | async-done | bytes 2359312 | tf_op jit(solution)/shard_map/all_gather | solution.py:224
  105.6 31.4 %reduce-scatter.37.cloned.1.call-done = bf16[384,768]{1,0:T(8,128)(2,1)} async-done(((bf16[1536,768]{1,0:T(8,128)(2,1)}), bf16[384,768]{1,0:T(8,128)(2,1)}) %reduce-scatter.37.cloned.1.call-update) | async-done | bytes 589840 | tf_op jit(solution)/shard_map/reduce_scatter | solution.py:229
  140.0 18.7 %all-gather.21.cloned.1.call-done = bf16[768,1024]{1,0:T(8,128)(2,1)} async-done(((bf16[192,1024]{1,0:T(8,128)(2,1)}), bf16[768,1024]{1,0:T(8,128)(2,1)}) %all-gather.21.cloned.1.call-update) | async-done | bytes 1572880 | tf_op jit(solution)/shard_map/all_gather | solution.py:248
  163.8 21.0 %all-gather.17.cloned.1.call-done = bf16[1536,768]{1,0:T(8,128)(2,1)} async-done(((bf16[384,768]{1,0:T(8,128)(2,1)}), bf16[1536,768]{1,0:T(8,128)(2,1)}) %all-gather.17.cloned.1.call-update) | async-done | bytes 2359312 | tf_op jit(solution)/shard_map/all_gather | solution.py:247
  195.4 20.1 %reduce-scatter.45.cloned.1.call-done = bf16[192,1024]{1,0:T(8,128)(2,1)} async-done(((bf16[768,1024]{1,0:T(8,128)(2,1)}), bf16[192,1024]{1,0:T(8,128)(2,1)}) %reduce-scatter.45.cloned.1.call-update) | async-done | bytes 393232 | tf_op jit(solution)/shard_map/reduce_scatter | solution.py:258
  218.9 32.5 %reduce-scatter.39.cloned.1.call-done = bf16[384,768]{1,0:T(8,128)(2,1)} async-done(((bf16[1536,768]{1,0:T(8,128)(2,1)}), bf16[384,768]{1,0:T(8,128)(2,1)}) %reduce-scatter.39.cloned.1.call-update) | async-done | bytes 589840 | tf_op jit(solution)/shard_map/reduce_scatter | solution.py:255
  257.0 16.2 all-gather.23.cloned.1.call-done
  337.4 28.3 %reduce-scatter.41.cloned.1.call-done = bf16[384,768]{1,0:T(8,128)(2,1)} async-done(((bf16[1536,768]{1,0:T(8,128)(2,1)}), bf16[384,768]{1,0:T(8,128)(2,1)}) %reduce-scatter.41.cloned.1.call-update) | async-done | bytes 589840 | tf_op jit(solution)/shard_map/reduce_scatter | solution.py:290
  373.4 13.5 all-gather.31.cloned.1.call-done
  456.4 28.2 %reduce-scatter.49.cloned.1.call-done = bf16[384,768]{1,0:T(8,128)(2,1)} async-done(((bf16[1536,768]{1,0:T(8,128)(2,1)}), bf16[384,768]{1,0:T(8,128)(2,1)}) %reduce-scatter.49.cloned.1.call-update) | async-done | bytes 589840 | tf_op jit(solution)/shard_map/reduce_scatter | solution.py:356
  490.4 15.9 all-gather.33.cloned.1.call-done
  511.7 20.1 %all-gather.27.cloned.1.call-done = bf16[1536,768]{1,0:T(8,128)(2,1)} async-done(((bf16[384,768]{1,0:T(8,128)(2,1)}), bf16[1536,768]{1,0:T(8,128)(2,1)}) %all-gather.27.cloned.1.call-update) | async-done | bytes 2359312 | tf_op jit(solution)/shard_map/all_gather | solution.py:370
  545.6 17.0 %reduce-scatter.55.cloned.1.call-done = bf16[192,1024]{1,0:T(8,128)(2,1)} async-done(((bf16[768,1024]{1,0:T(8,128)(2,1)}), bf16[192,1024]{1,0:T(8,128)(2,1)}) %reduce-scatter.55.cloned.1.call-update) | async-done | bytes 393232 | tf_op jit(solution)/shard_map/reduce_scatter | solution.py:388
  569.9 28.3 %reduce-scatter.51.cloned.1.call-done = bf16[384,768]{1,0:T(8,128)(2,1)} async-done(((bf16[1536,768]{1,0:T(8,128)(2,1)}), bf16[384,768]{1,0:T(8,128)(2,1)}) %reduce-scatter.51.cloned.1.call-update) | async-done | bytes 589840 | tf_op jit(solution)/shard_map/reduce_scatter | solution.py:382
  603.8 16.7 reduce-scatter.81.cloned.1.call-done
  694.0 11.6 fusion.65
  781.5 17.4 %reduce-scatter.85.cloned.1.call-done = f32[96,192]{1,0:T(8,128)} async-done(((f32[768,192]{1,0:T(8,128)}), f32[96,192]{1,0:T(8,128)}) %reduce-scatter.85.cloned.1.call-update) | async-done | bytes 73744
  800.6 67.5 %reduce-scatter.83.cloned.1.call-done = f32[96,576]{1,0:T(8,128)} async-done(((f32[768,576]{1,0:T(8,128)}), f32[96,576]{1,0:T(8,128)}) %reduce-scatter.83.cloned.1.call-update) | async-done | bytes 221200
  870.0 19.1 %reduce-scatter.87.cloned.1.call-done = bf16[192,6]{1,0:T(8,128)(2,1)} async-done(((bf16[768,6]{1,0:T(8,128)(2,1)}), bf16[192,6]{1,0:T(8,128)(2,1)}) %reduce-scatter.87.cloned.1.call-update) | async-done | bytes 2320
  890.0 21.6 %all-reduce = f32[6,192]{1,0:T(8,128)S(1)} all-reduce(bf16[6,192]{1,0:T(8,128)(2,1)S(1)} %copy.364), channel_id=27, replica_groups=mesh['dp'=8,'mp'=4] {'dp'}, use_global_device_ids=true, to_apply=%region_70.73.clone | all-reduce | flops 1152 | bytes 6912
  922.2 33.5 %reduce-scatter.57.cloned.1.call-done = bf16[384,768]{1,0:T(8,128)(2,1)} async-done(((bf16[1536,768]{1,0:T(8,128)(2,1)}), bf16[384,768]{1,0:T(8,128)(2,1)}) %reduce-scatter.57.cloned.1.call-update) | async-done | bytes 589840 | tf_op jit(solution)/shard_map/reduce_scatter | solution.py:465
  958.0 76.6 %reduce-scatter.63.cloned.1.call-done = f32[3,128,256]{1,2,0:T(8,128)} async-done(((f32[3,1024,256]{1,2,0:T(8,128)}), f32[3,128,256]{1,2,0:T(8,128)}) %reduce-scatter.63.cloned.1.call-update) | async-done | bytes 393232 | tf_op jit(solution)/shard_map/reduce_scatter | solution.py:482
  1036.5 65.7 %reduce-scatter.79.cloned.1.call-done = f32[256,128]{1,0:T(8,128)} async-done(((f32[256,1024]{1,0:T(8,128)}), f32[256,128]{1,0:T(8,128)}) %reduce-scatter.79.cloned.1.call-update) | async-done | bytes 131088 | tf_op jit(solution)/shard_map/reduce_scatter | solution.py:492
  1102.2 78.1 %reduce-scatter.77.cloned.1.call-done = f32[3,128,256]{2,1,0:T(8,128)} async-done(((f32[3,1024,256]{2,1,0:T(8,128)}), f32[3,128,256]{2,1,0:T(8,128)}) %reduce-scatter.77.cloned.1.call-update) | async-done | bytes 393232 | tf_op jit(solution)/shard_map/reduce_scatter | solution.py:491
  1180.3 66.6 %reduce-scatter.73.cloned.1.call-done = f32[128,256]{1,0:T(8,128)} async-done(((f32[1024,256]{1,0:T(8,128)}), f32[128,256]{1,0:T(8,128)}) %reduce-scatter.73.cloned.1.call-update) | async-done | bytes 131088 | tf_op jit(solution)/shard_map/reduce_scatter | solution.py:487
  1246.9 67.4 %reduce-scatter.75.cloned.1.call-done = f32[256,128]{1,0:T(8,128)} async-done(((f32[256,1024]{1,0:T(8,128)}), f32[256,128]{1,0:T(8,128)}) %reduce-scatter.75.cloned.1.call-update) | async-done | bytes 131088 | tf_op jit(solution)/shard_map/reduce_scatter | solution.py:488
  1314.3 66.9 %reduce-scatter.67.cloned.1.call-done = f32[256,128]{1,0:T(8,128)} async-done(((f32[256,1024]{1,0:T(8,128)}), f32[256,128]{1,0:T(8,128)}) %reduce-scatter.67.cloned.1.call-update) | async-done | bytes 131088 | tf_op jit(solution)/shard_map/reduce_scatter | solution.py:484
  1381.2 72.6 %reduce-scatter.69.cloned.1.call-done = f32[96,768]{1,0:T(8,128)} async-done(((f32[768,768]{1,0:T(8,128)}), f32[96,768]{1,0:T(8,128)}) %reduce-scatter.69.cloned.1.call-update) | async-done | bytes 294928 | tf_op jit(solution)/shard_map/reduce_scatter | solution.py:485
  1453.7 72.6 %reduce-scatter.71.cloned.1.call-done = f32[768,96]{0,1:T(8,128)} async-done(((f32[768,768]{0,1:T(8,128)}), f32[768,96]{0,1:T(8,128)}) %reduce-scatter.71.cloned.1.call-update) | async-done | bytes 294928 | tf_op jit(solution)/shard_map/reduce_scatter | solution.py:486
  1526.3 65.7 %reduce-scatter.65.cloned.1.call-done = f32[256,96]{0,1:T(8,128)} async-done(((f32[256,768]{0,1:T(8,128)}), f32[256,96]{0,1:T(8,128)}) %reduce-scatter.65.cloned.1.call-update) | async-done | bytes 98320 | tf_op jit(solution)/shard_map/reduce_scatter | solution.py:483
  1592.1 71.8 %reduce-scatter.61.cloned.1.call-done = f32[3,96,256]{2,1,0:T(8,128)} async-done(((f32[3,768,256]{2,1,0:T(8,128)}), f32[3,96,256]{2,1,0:T(8,128)}) %reduce-scatter.61.cloned.1.call-update) | async-done | bytes 294928 | tf_op jit(solution)/shard_map/reduce_scatter | solution.py:481
  (750 shorter events, 432.2 us)
Async XLA Ops:
  8.7 92.7 %reduce-scatter.43.cloned.1.call-start = ((), (), s32[]{:S(2)}) async-start(), calls=%async_computation.34 | async-start | bytes 1966080 | tf_op jit(solution)/shard_map/reduce_scatter | solution.py:235
  104.9 79.9 %all-gather.17.cloned.1.call-start = ((), (), s32[]{:S(2)}) async-start(), calls=%async_computation.30 | async-start | bytes 2949120 | tf_op jit(solution)/shard_map/all_gather | solution.py:247
  140.0 75.6 %reduce-scatter.45.cloned.1.call-start = ((), (), s32[]{:S(2)}) async-start(), calls=%async_computation.36 | async-start | bytes 1966080 | tf_op jit(solution)/shard_map/reduce_scatter | solution.py:258
  163.7 87.6 %reduce-scatter.39.cloned.1.call-start = ((), (), s32[]{:S(2)}) async-start(), calls=%async_computation.31 | async-start | bytes 2949120 | tf_op jit(solution)/shard_map/reduce_scatter | solution.py:255
  195.1 78.0 %all-gather.23.cloned.1.call-start = ((), (), s32[]{:S(2)}) async-start(), calls=%async_computation.37 | async-start | bytes 1966080 | tf_op jit(solution)/shard_map/all_gather | solution.py:271
  218.8 86.8 %all-gather.19.cloned.1.call-start = ((), (), s32[]{:S(2)}) async-start(), calls=%async_computation.32 | async-start | bytes 2949120 | tf_op jit(solution)/shard_map/all_gather | solution.py:270
  256.1 75.3 %reduce-scatter.47.cloned.1.call-start = ((), (), s32[]{:S(2)}) async-start(), calls=%async_computation.38 | async-start | bytes 1966080 | tf_op jit(solution)/shard_map/reduce_scatter | solution.py:296
  337.4 80.1 %all-gather.25.cloned.1.call-start = ((), (), s32[]{:S(2)}) async-start(), calls=%async_computation.39 | async-start | bytes 2949120 | tf_op jit(solution)/shard_map/all_gather | solution.py:314
  372.0 79.3 %reduce-scatter.53.cloned.1.call-start = ((), (), s32[]{:S(2)}) async-start(), calls=%async_computation.45 | async-start | bytes 1966080 | tf_op jit(solution)/shard_map/reduce_scatter | solution.py:359
  415.8 68.8 %reduce-scatter.49.cloned.1.call-start = ((), (), s32[]{:S(2)}) async-start(), calls=%async_computation.40 | async-start | bytes 2949120 | tf_op jit(solution)/shard_map/reduce_scatter | solution.py:356
  456.4 75.4 %all-gather.27.cloned.1.call-start = ((), (), s32[]{:S(2)}) async-start(), calls=%async_computation.41 | async-start | bytes 2949120 | tf_op jit(solution)/shard_map/all_gather | solution.py:370
  490.2 72.4 %reduce-scatter.55.cloned.1.call-start = ((), (), s32[]{:S(2)}) async-start(), calls=%async_computation.47 | async-start | bytes 1966080 | tf_op jit(solution)/shard_map/reduce_scatter | solution.py:388
  511.6 86.6 %reduce-scatter.51.cloned.1.call-start = ((), (), s32[]{:S(2)}) async-start(), calls=%async_computation.42 | async-start | bytes 2949120 | tf_op jit(solution)/shard_map/reduce_scatter | solution.py:382
  544.3 76.2 %reduce-scatter.81.cloned.1.call-start = ((), (), s32[]{:S(2)}) async-start(), calls=%async_computation.61 | async-start | bytes 20480 | tf_op jit(solution)/shard_map/reduce_scatter | solution.py:474
  567.8 74.6 %all-gather.35.cloned.1.call-start = ((), (), s32[]{:S(2)}) async-start(), calls=%async_computation.48 | async-start | bytes 1966080 | tf_op jit(solution)/shard_map/all_gather | solution.py:417
  569.9 98.9 %all-gather.29.cloned.1.call-start = ((), (), s32[]{:S(2)}) async-start(), calls=%async_computation.43 | async-start | bytes 2949120 | tf_op jit(solution)/shard_map/all_gather | solution.py:416
  603.8 175.6 %reduce-scatter.89.cloned.1.call-start = ((), (), s32[]{:S(2)}) async-start(), calls=%async_computation.65 | async-start | bytes 147456
  622.0 177.0 %reduce-scatter.85.cloned.1.call-start = ((), (), s32[]{:S(2)}) async-start(), calls=%async_computation.63 | async-start | bytes 884736
  626.0 242.1 %reduce-scatter.83.cloned.1.call-start = ((), (), s32[]{:S(2)}) async-start(), calls=%async_computation.62 | async-start | bytes 2211840
  637.8 251.3 %reduce-scatter.87.cloned.1.call-start = ((), (), s32[]{:S(2)}) async-start(), calls=%async_computation.64 | async-start | bytes 245760
  663.8 256.2 %reduce-scatter.59.cloned.1.call-start = ((), (), s32[]{:S(2)}) async-start(), calls=%async_computation.50 | async-start | bytes 1966080 | tf_op jit(solution)/shard_map/reduce_scatter | solution.py:468
  692.2 263.5 %reduce-scatter.57.cloned.1.call-start = ((), (), s32[]{:S(2)}) async-start(), calls=%async_computation.49 | async-start | bytes 2949120 | tf_op jit(solution)/shard_map/reduce_scatter | solution.py:465
  729.5 305.1 %reduce-scatter.63.cloned.1.call-start = ((), (), s32[]{:S(2)}) async-start(), calls=%async_computation.52 | async-start | bytes 3538944 | tf_op jit(solution)/shard_map/reduce_scatter | solution.py:482
  734.7 367.5 %reduce-scatter.79.cloned.1.call-start = ((), (), s32[]{:S(2)}) async-start(), calls=%async_computation.60 | async-start | bytes 1179648 | tf_op jit(solution)/shard_map/reduce_scatter | solution.py:492
  737.8 442.5 %reduce-scatter.77.cloned.1.call-start = ((), (), s32[]{:S(2)}) async-start(), calls=%async_computation.59 | async-start | bytes 3538944 | tf_op jit(solution)/shard_map/reduce_scatter | solution.py:491
  743.6 503.3 %reduce-scatter.73.cloned.1.call-start = ((), (), s32[]{:S(2)}) async-start(), calls=%async_computation.57 | async-start | bytes 1179648 | tf_op jit(solution)/shard_map/reduce_scatter | solution.py:487
  746.6 567.6 %reduce-scatter.75.cloned.1.call-start = ((), (), s32[]{:S(2)}) async-start(), calls=%async_computation.58 | async-start | bytes 1179648 | tf_op jit(solution)/shard_map/reduce_scatter | solution.py:488
  749.8 631.3 %reduce-scatter.67.cloned.1.call-start = ((), (), s32[]{:S(2)}) async-start(), calls=%async_computation.54 | async-start | bytes 1179648 | tf_op jit(solution)/shard_map/reduce_scatter | solution.py:484
  753.1 700.7 %reduce-scatter.69.cloned.1.call-start = ((), (), s32[]{:S(2)}) async-start(), calls=%async_computation.55 | async-start | bytes 2654208 | tf_op jit(solution)/shard_map/reduce_scatter | solution.py:485
  758.3 768.0 %reduce-scatter.71.cloned.1.call-start = ((), (), s32[]{:S(2)}) async-start(), calls=%async_computation.56 | async-start | bytes 2654208 | tf_op jit(solution)/shard_map/reduce_scatter | solution.py:486
  766.1 825.9 %reduce-scatter.65.cloned.1.call-start = ((), (), s32[]{:S(2)}) async-start(), calls=%async_computation.53 | async-start | bytes 884736 | tf_op jit(solution)/shard_map/reduce_scatter | solution.py:483
  770.9 893.0 %reduce-scatter.61.cloned.1.call-start = ((), (), s32[]{:S(2)}) async-start(), calls=%async_computation.51 | async-start | bytes 2654208 | tf_op jit(solution)/shard_map/reduce_scatter | solution.py:481
  (194 other events, 3560.9 us)
Sparse Core Ops, SparseCore 0:
  9.6 22.3 all-gather.12
  33.6 24.0 all-gather.14
  73.2 28.1 reduce-scatter.42
  103.9 33.0 reduce-scatter.36
  160.7 24.0 all-gather.16
  187.3 28.1 reduce-scatter.44
  218.2 33.0 reduce-scatter.38
  275.1 24.0 all-gather.18
  301.8 28.1 reduce-scatter.46
  332.5 33.0 reduce-scatter.40
  388.3 24.0 all-gather.24
  415.9 28.1 reduce-scatter.52
  451.4 33.1 reduce-scatter.48
  507.7 24.0 all-gather.26
  534.4 28.1 reduce-scatter.54
  565.1 33.0 reduce-scatter.50
  644.6 24.0 all-gather.28
  672.9 60.7 reduce-scatter.88
  737.4 61.5 reduce-scatter.84
  802.3 65.7 reduce-scatter.82
  891.8 28.1 reduce-scatter.58
  922.6 33.0 reduce-scatter.56
  959.6 74.9 reduce-scatter.62
  1039.0 63.1 reduce-scatter.78
  1106.4 73.9 reduce-scatter.76
  1184.1 62.6 reduce-scatter.72
  1251.2 62.9 reduce-scatter.74
  1318.2 62.8 reduce-scatter.66
  1385.5 68.1 reduce-scatter.68
  1458.1 68.2 reduce-scatter.70
  1530.6 61.4 reduce-scatter.64
  1596.0 67.8 reduce-scatter.60
  (7 shorter events, 135.7 us)
where the time goes:
time: 1680 us; the launch traced here: 1670 us
  waiting for transfers between devices  1210 us (72%)
  matrix products  222 us (13%)
  local copies, waits for them, and re-layouts  125 us (7%)
  other arithmetic  69.7 us (4%)
  blocking collectives  21.6 us (1%)
  between operations  18 us (1%)
    unnamed x43, waiting for transfers between devices  106 us
    reduce_scatter x1, waiting for transfers between devices, per_device(): lax.psum_scatter(grad_image_self_qkv, 'dp', scatter_dimension=1, tiled=True)  78.1 us
    reduce_scatter x1, waiting for transfers between devices, per_device(): lax.psum_scatter(grad_co_image_qkv, 'dp', scatter_dimension=1, tiled=True)  76.6 us
    reduce_scatter x1, waiting for transfers between devices, per_device(): lax.psum_scatter(grad_text_down, 'dp', scatter_dimension=1, tiled=True)  72.6 us
    reduce_scatter x1, waiting for transfers between devices, per_device(): lax.psum_scatter(grad_text_up, 'dp', scatter_dimension=0, tiled=True)  72.6 us
    reduce_scatter x1, waiting for transfers between devices, per_device(): lax.psum_scatter(grad_co_text_qkv, 'dp', scatter_dimension=1, tiled=True)  71.8 us
    reduce_scatter x1, waiting for transfers between devices, per_device(): lax.psum_scatter(grad_image_down, 'dp', scatter_dimension=1, tiled=True)  67.4 us
    reduce_scatter x1, waiting for transfers between devices, per_device(): lax.psum_scatter(grad_co_image_out, 'dp', scatter_dimension=1, tiled=True)  66.9 us
  transfers between devices with their start and end apart: 39, of which 34 were waited for; matrix products, arithmetic and copies ran while one was open for 22% of the time, Pallas kernels for 0%

commit v1 on v0

v1 whole, which is shorter than its diff:
```python
import functools

import jax
import jax.numpy as jnp
from jax import lax
from jax.experimental import pallas as pl
from jax.experimental.pallas import tpu as pltpu
from jax.sharding import PartitionSpec as P

CO_HEADS = 8
TEXT_HEADS = 12
IMAGE_HEADS = 8
CAP_LEN = 64
ROW_LEN = 128
PER_ROW = 4

epsilon = 1e-05
BF = jnp.bfloat16
F32 = jnp.float32
VMEM_LIMIT = 48 * 1024 * 1024


def product(former, latter):
    return jnp.dot(former, latter, preferred_element_type=F32)


def product_tn(former, latter):
    return lax.dot_general(former, latter, (((0,), (0,)), ((), ())), preferred_element_type=F32)


def product_nt(former, latter):
    return lax.dot_general(former, latter, (((1,), (1,)), ((), ())), preferred_element_type=F32)


def layer_norm(values, norm_gain, norm_shift):
    centre = values - jnp.mean(values, axis=-1, keepdims=True)
    spread = jnp.mean(centre * centre, axis=-1, keepdims=True)
    return centre * lax.rsqrt(spread + epsilon) * norm_gain + norm_shift


def norm_back(values, norm_gain, gradient):
    centre = values - jnp.mean(values, axis=-1, keepdims=True)
    spread = jnp.mean(centre * centre, axis=-1, keepdims=True)
    inverse = lax.rsqrt(spread + epsilon)
    unit = centre * inverse
    scaled = gradient * norm_gain
    back = inverse * (
        scaled
        - jnp.mean(scaled, axis=-1, keepdims=True)
        - unit * jnp.mean(scaled * unit, axis=-1, keepdims=True)
    )
    return back, jnp.sum(gradient * unit, axis=0), jnp.sum(gradient, axis=0)


GELU_A = 0.7978845608028654
GELU_B = 0.044715


def gelu_tanh(values):
    return 0.5 * values * (1.0 + jnp.tanh(GELU_A * (values + GELU_B * values * values * values)))


def gelu_slope(values):
    bent = jnp.tanh(GELU_A * (values + GELU_B * values * values * values))
    return 0.5 * (1.0 + bent) + 0.5 * values * (1.0 - bent * bent) * GELU_A * (
        1.0 + 3.0 * GELU_B * values * values
    )


def softmax_block(scores, mask):
    scores = jnp.where(mask, scores, -1000000000.0)
    exponent = jnp.exp(scores - jnp.max(scores, axis=-1, keepdims=True))
    return (exponent / jnp.sum(exponent, axis=-1, keepdims=True)).astype(BF)


def attend_back(shares, scaling, queries, keys, values, context_grad):
    wide = shares.astype(F32)
    share_grad = product_nt(context_grad, values)
    inner = jnp.sum(share_grad * wide, axis=-1, keepdims=True)
    score_grad = (wide * (share_grad - inner) * scaling).astype(BF)
    return (
        product(score_grad, keys).astype(BF),
        product_tn(score_grad, queries).astype(BF),
        product_tn(shares, context_grad).astype(BF),
    )


def row_ends(region_ref, row):
    ends = [region_ref[row * PER_ROW]]
    for slot in range(1, PER_ROW):
        ends.append(ends[-1] + region_ref[row * PER_ROW + slot])
    return ends


def slot_of(places, ends):
    slot = (places >= ends[0]).astype(jnp.int32)
    for end in ends[1:]:
        slot = slot + (places >= end).astype(jnp.int32)
    return slot


def caption_rows(ref, captions, start, width):
    return jnp.concatenate(
        [
            ref[pl.ds(pl.multiple_of(caption * CAP_LEN, CAP_LEN), CAP_LEN), start : start + width]
            for caption in captions
        ],
        axis=0,
    )


def co_forward_kernel(
    heads, per_step, order_ref, region_ref, length_ref, text_ref, image_ref,
    text_out, image_out, text_shares, image_shares,
):
    inner = text_ref.shape[1] // 3
    size = inner // heads
    scaling = size ** (-0.5)
    span = PER_ROW * CAP_LEN
    for member in range(per_step):
        row = pl.program_id(0) * per_step + member
        captions = [order_ref[row * PER_ROW + slot] for slot in range(PER_ROW)]
        ends = row_ends(region_ref, row)
        token_slot = lax.broadcasted_iota(jnp.int32, (span, ROW_LEN), 0) // CAP_LEN
        to_image = token_slot == slot_of(
            lax.broadcasted_iota(jnp.int32, (span, ROW_LEN), 1), ends
        )
        spots = lax.broadcasted_iota(jnp.int32, (ROW_LEN, span), 1)
        length = jnp.full((ROW_LEN, span), length_ref[captions[0]], jnp.int32)
        for slot in range(1, PER_ROW):
            length = jnp.where(spots >= slot * CAP_LEN, length_ref[captions[slot]], length)
        to_text = (
            slot_of(lax.broadcasted_iota(jnp.int32, (ROW_LEN, span), 0), ends) == spots // CAP_LEN
        ) & (spots % CAP_LEN < length)
        rows = slice(member * ROW_LEN, (member + 1) * ROW_LEN)
        for head in range(heads):
            text = [
                caption_rows(text_ref, captions, part * inner + head * size, size)
                for part in range(3)
            ]
            image = [
                image_ref[rows, part * inner + head * size : part * inner + (head + 1) * size]
                for part in range(3)
            ]
            lanes = slice(head * size, (head + 1) * size)
            shares = softmax_block(product_nt(text[0], image[1]) * scaling, to_image)
            text_shares[member, head] = shares
            context = product(shares, image[2]).astype(BF)
            for slot, caption in enumerate(captions):
                text_out[
                    pl.ds(pl.multiple_of(caption * CAP_LEN, CAP_LEN), CAP_LEN), lanes
                ] = context[slot * CAP_LEN : (slot + 1) * CAP_LEN]
            shares = softmax_block(product_nt(image[0], text[1]) * scaling, to_text)
            image_shares[member, head] = shares
            image_out[rows, lanes] = product(shares, text[2]).astype(BF)


def co_backward_kernel(
    heads, per_step, order_ref, text_ref, image_ref, text_shares, image_shares,
    text_grad, image_grad, text_out, image_out,
):
    inner = text_ref.shape[1] // 3
    size = inner // heads
    scaling = size ** (-0.5)
    for member in range(per_step):
        row = pl.program_id(0) * per_step + member
        captions = [order_ref[row * PER_ROW + slot] for slot in range(PER_ROW)]
        rows = slice(member * ROW_LEN, (member + 1) * ROW_LEN)
        for head in range(heads):
            text = [
                caption_rows(text_ref, captions, part * inner + head * size, size)
                for part in range(3)
            ]
            image = [
                image_ref[rows, part * inner + head * size : part * inner + (head + 1) * size]
                for part in range(3)
            ]
            lanes = slice(head * size, (head + 1) * size)
            from_text = caption_rows(text_grad, captions, head * size, size)
            text_q, image_k, image_v = attend_back(
                text_shares[member, head], scaling, text[0], image[1], image[2], from_text
            )
            image_q, text_k, text_v = attend_back(
                image_shares[member, head], scaling, image[0], text[1], text[2],
                image_grad[rows, lanes],
            )
            for part, grad in enumerate((text_q, text_k, text_v)):
                for slot, caption in enumerate(captions):
                    text_out[
                        pl.ds(pl.multiple_of(caption * CAP_LEN, CAP_LEN), CAP_LEN),
                        part * inner + head * size : part * inner + (head + 1) * size,
                    ] = grad[slot * CAP_LEN : (slot + 1) * CAP_LEN]
            for part, grad in enumerate((image_q, image_k, image_v)):
                image_out[
                    rows, part * inner + head * size : part * inner + (head + 1) * size
                ] = grad


def self_mask_text(length_ref, block):
    shape = (2 * CAP_LEN, 2 * CAP_LEN)
    queries = lax.broadcasted_iota(jnp.int32, shape, 0)
    spots = lax.broadcasted_iota(jnp.int32, shape, 1)
    length = jnp.where(
        spots >= CAP_LEN, length_ref[block * 2 + 1] + CAP_LEN, length_ref[block * 2]
    )
    return (queries // CAP_LEN == spots // CAP_LEN) & (spots < length)


def self_mask_image(region_ref, row):
    ends = row_ends(region_ref, row)
    shape = (ROW_LEN, ROW_LEN)
    return slot_of(lax.broadcasted_iota(jnp.int32, shape, 0), ends) == slot_of(
        lax.broadcasted_iota(jnp.int32, shape, 1), ends
    )


def self_forward_kernel(heads, per_step, masker, count_ref, rows_ref, context_out, shares_out):
    inner = rows_ref.shape[1] // 3
    size = inner // heads
    scaling = size ** (-0.5)
    for member in range(per_step):
        mask = masker(count_ref, pl.program_id(0) * per_step + member)
        rows = slice(member * ROW_LEN, (member + 1) * ROW_LEN)
        contexts = []
        for head in range(heads):
            pieces = [
                rows_ref[rows, part * inner + head * size : part * inner + (head + 1) * size]
                for part in range(3)
            ]
            shares = softmax_block(product_nt(pieces[0], pieces[1]) * scaling, mask)
            shares_out[member, head] = shares
            contexts.append(product(shares, pieces[2]).astype(BF))
        context_out[rows, :] = jnp.concatenate(contexts, axis=1)


def self_backward_kernel(heads, per_step, rows_ref, shares_ref, grad_ref, rows_out):
    inner = rows_ref.shape[1] // 3
    size = inner // heads
    scaling = size ** (-0.5)
    for member in range(per_step):
        rows = slice(member * ROW_LEN, (member + 1) * ROW_LEN)
        grads = []
        for head in range(heads):
            pieces = [
                rows_ref[rows, part * inner + head * size : part * inner + (head + 1) * size]
                for part in range(3)
            ]
            grads.append(
                attend_back(
                    shares_ref[member, head], scaling, *pieces,
                    grad_ref[rows, head * size : (head + 1) * size],
                )
            )
        rows_out[rows, :] = jnp.concatenate(
            [grads[head][part] for part in range(3) for head in range(heads)], axis=1
        )


def shape_of(shape, dtype=BF):
    return jax.ShapeDtypeStruct(shape, dtype)


def cost(flops, moved, exps):
    return pl.CostEstimate(flops=int(flops), bytes_accessed=int(moved), transcendentals=int(exps))


def co_forward(text, image, order, regions, lengths, heads):
    tokens, width = text.shape
    slots = image.shape[0]
    inner = width // 3
    rows = slots // ROW_LEN
    per_step = 2
    span = PER_ROW * CAP_LEN
    whole = lambda i, *_: (0, 0)
    strip = lambda i, *_: (i, 0)
    block = lambda i, *_: (i, 0, 0, 0)
    return pl.pallas_call(
        functools.partial(co_forward_kernel, heads, per_step),
        grid_spec=pltpu.PrefetchScalarGridSpec(
            num_scalar_prefetch=3,
            grid=(rows // per_step,),
            in_specs=[
                pl.BlockSpec((tokens, width), whole),
                pl.BlockSpec((per_step * ROW_LEN, width), strip),
            ],
            out_specs=[
                pl.BlockSpec((tokens, inner), whole),
                pl.BlockSpec((per_step * ROW_LEN, inner), strip),
                pl.BlockSpec((per_step, heads, span, ROW_LEN), block),
                pl.BlockSpec((per_step, heads, ROW_LEN, span), block),
            ],
        ),
        out_shape=[
            shape_of((tokens, inner)),
            shape_of((slots, inner)),
            shape_of((rows, heads, span, ROW_LEN)),
            shape_of((rows, heads, ROW_LEN, span)),
        ],
        compiler_params=pltpu.CompilerParams(vmem_limit_bytes=VMEM_LIMIT),
        cost_estimate=cost(
            8 * rows * inner * span * ROW_LEN, 8e6, 2 * rows * heads * span * ROW_LEN
        ),
        name="co_forward",
    )(order, regions, lengths, text, image)


def co_backward(text, image, text_shares, image_shares, text_grad, image_grad, order, heads):
    tokens, width = text.shape
    slots = image.shape[0]
    inner = width // 3
    rows = slots // ROW_LEN
    per_step = 2
    span = PER_ROW * CAP_LEN
    whole = lambda i, *_: (0, 0)
    strip = lambda i, *_: (i, 0)
    block = lambda i, *_: (i, 0, 0, 0)
    return pl.pallas_call(
        functools.partial(co_backward_kernel, heads, per_step),
        grid_spec=pltpu.PrefetchScalarGridSpec(
            num_scalar_prefetch=1,
            grid=(rows // per_step,),
            in_specs=[
                pl.BlockSpec((tokens, width), whole),
                pl.BlockSpec((per_step * ROW_LEN, width), strip),
                pl.BlockSpec((per_step, heads, span, ROW_LEN), block),
                pl.BlockSpec((per_step, heads, ROW_LEN, span), block),
                pl.BlockSpec((tokens, inner), whole),
                pl.BlockSpec((per_step * ROW_LEN, inner), strip),
            ],
            out_specs=[
                pl.BlockSpec((tokens, width), whole),
                pl.BlockSpec((per_step * ROW_LEN, width), strip),
            ],
        ),
        out_shape=[shape_of((tokens, width)), shape_of((slots, width))],
        compiler_params=pltpu.CompilerParams(vmem_limit_bytes=VMEM_LIMIT),
        cost_estimate=cost(16 * rows * inner * span * ROW_LEN, 12e6, 0),
        name="co_backward",
    )(order, text, image, text_shares, image_shares, text_grad, image_grad)


def self_forward(rows_in, counts, heads, per_step, masker):
    tokens, width = rows_in.shape
    inner = width // 3
    blocks = tokens // ROW_LEN
    strip = lambda i, *_: (i, 0)
    block = lambda i, *_: (i, 0, 0, 0)
    return pl.pallas_call(
        functools.partial(self_forward_kernel, heads, per_step, masker),
        grid_spec=pltpu.PrefetchScalarGridSpec(
            num_scalar_prefetch=1,
            grid=(blocks // per_step,),
            in_specs=[pl.BlockSpec((per_step * ROW_LEN, width), strip)],
            out_specs=[
                pl.BlockSpec((per_step * ROW_LEN, inner), strip),
                pl.BlockSpec((per_step, heads, ROW_LEN, ROW_LEN), block),
            ],
        ),
        out_shape=[
            shape_of((tokens, inner)),
            shape_of((blocks, heads, ROW_LEN, ROW_LEN)),
        ],
        compiler_params=pltpu.CompilerParams(vmem_limit_bytes=VMEM_LIMIT),
        cost_estimate=cost(4 * tokens * inner * ROW_LEN, 6e6, tokens * heads * ROW_LEN),
        name="self_forward",
    )(counts, rows_in)


def self_backward(rows_in, shares, grad, heads, per_step):
    tokens, width = rows_in.shape
    inner = width // 3
    blocks = tokens // ROW_LEN
    strip = lambda i: (i, 0)
    block = lambda i: (i, 0, 0, 0)
    return pl.pallas_call(
        functools.partial(self_backward_kernel, heads, per_step),
        grid=(blocks // per_step,),
        in_specs=[
            pl.BlockSpec((per_step * ROW_LEN, width), strip),
            pl.BlockSpec((per_step, heads, ROW_LEN, ROW_LEN), block),
            pl.BlockSpec((per_step * ROW_LEN, inner), strip),
        ],
        out_specs=pl.BlockSpec((per_step * ROW_LEN, width), strip),
        out_shape=shape_of((tokens, width)),
        compiler_params=pltpu.CompilerParams(vmem_limit_bytes=VMEM_LIMIT),
        cost_estimate=cost(10 * tokens * inner * ROW_LEN, 9e6, 0),
        name="self_backward",
    )(rows_in, shares, grad)


def swap(values, axis, flip):
    return lax.ppermute(values, axis, [(i, i ^ flip) for i in range(lax.axis_size(axis))])


def gather(shard, core):
    other = swap(shard, "mp", 2)
    near = swap(shard, "mp", 1)
    far = swap(other, "mp", 1)
    first = core == 0
    return jnp.concatenate(
        [
            jnp.where(first, shard, near),
            jnp.where(first, near, shard),
            jnp.where(first, other, far),
            jnp.where(first, far, other),
        ],
        axis=0,
    )


def scatter_sum(left, right, core):
    first = core == 0

    def over_cores(half):
        upper, lower = jnp.split(half, 2, axis=0)
        kept = jnp.where(first, upper, lower)
        given = jnp.where(first, lower, upper).astype(BF)
        return kept + swap(given, "mp", 1).astype(F32)

    sent = swap(over_cores(right).astype(BF), "mp", 2)
    return over_cores(left) + sent.astype(F32)


def halves(rows):
    return jnp.split(rows, 2, axis=0)


def blocked(grads, group_count):
    pieces = []
    for grad in grads:
        rows, columns = grad.shape
        for start in range(0, columns, 256):
            pieces.append(
                grad[:, start : start + 256].astype(BF).reshape(group_count, rows // group_count, 256)
            )
    return jnp.concatenate(pieces, axis=1)


def unblocked(summed, shapes, group_count):
    outs = []
    at = 0
    for rows, columns in shapes:
        part = rows // group_count
        pieces = []
        for _ in range(columns // 256):
            pieces.append(summed[at : at + part])
            at += part
        outs.append(jnp.concatenate(pieces, axis=1).astype(F32))
    return outs


def reduce_groups(grads, group_count):
    stacked = blocked(grads, group_count)
    flat = stacked.reshape(-1, 256)
    summed = lax.psum_scatter(flat, "dp", scatter_dimension=0, tiled=True)
    return unblocked(summed, [grad.shape for grad in grads], group_count)


def reduce_halving(grads, group_count, bits):
    current = blocked(grads, group_count)
    tail = current.shape[1:]
    place = lax.axis_index("dp")
    names = list(range(group_count.bit_length() - 1))[::-1]
    current = current.reshape((2,) * len(names) + tail)
    for bit in bits:
        axis = names.index(bit)
        lower = lax.index_in_dim(current, 0, axis, keepdims=False)
        upper = lax.index_in_dim(current, 1, axis, keepdims=False)
        mine = (place >> bit) & 1
        kept = jnp.where(mine == 0, lower, upper)
        given = jnp.where(mine == 0, upper, lower)
        current = (kept.astype(F32) + swap(given, "dp", 1 << bit).astype(F32)).astype(BF)
        names.pop(axis)
    return unblocked(current, [grad.shape for grad in grads], group_count)


def side_by_side(stacked):
    members, height, breadth = stacked.shape
    return jnp.transpose(stacked, (1, 0, 2)).reshape(height, members * breadth)


def apart(grad):
    rows, columns = grad.shape
    return jnp.transpose(grad.reshape(rows, 3, columns // 3), (1, 0, 2))


def per_device(
    text_in,
    image_in,
    caption_lengths,
    region_lengths,
    image_caption,
    co_text_qkv,
    co_image_qkv,
    co_text_out,
    co_image_out,
    text_up,
    text_down,
    image_up,
    image_down,
    text_self_qkv,
    text_self_out,
    image_self_qkv,
    image_self_out,
    text_gains,
    text_shifts,
    image_gains,
    image_shifts,
    text_grad_out,
    image_grad_out,
):
    captions = image_caption.shape[1]
    part_count = lax.axis_size("mp")
    group_count = lax.axis_size("dp")
    spot = lax.axis_index("mp")
    core = spot % 2
    chip = spot // 2
    co_local = CO_HEADS // part_count
    text_local = TEXT_HEADS // part_count
    image_local = IMAGE_HEADS // part_count

    half = captions // 2
    turned = chip == 1
    flip = lambda values: jnp.where(turned, jnp.roll(values, half), values)
    lengths = flip(caption_lengths)
    regions = flip(region_lengths.reshape(-1))
    order = flip(image_caption[0])
    order = jnp.where(turned, (order + half) % captions, order)

    w_co_text = side_by_side(co_text_qkv)
    w_co_image = side_by_side(co_image_qkv)
    w_self_text = side_by_side(text_self_qkv)
    w_self_image = side_by_side(image_self_qkv)

    text_all = gather(text_in, core)
    image_all = gather(image_in, core)
    text_co = product(text_all, w_co_text).astype(BF)
    image_co = product(image_all, w_co_image).astype(BF)
    text_ctx, image_ctx, text_share, image_share = co_forward(
        text_co, image_co, order, regions, lengths, co_local
    )
    text_zero = text_in.astype(F32) + scatter_sum(
        *[product(rows, co_text_out) for rows in halves(text_ctx)], core
    )
    image_zero = image_in.astype(F32) + scatter_sum(
        *[product(rows, co_image_out) for rows in halves(image_ctx)], core
    )
    text_first = layer_norm(text_zero, text_gains[0], text_shifts[0])
    image_first = layer_norm(image_zero, image_gains[0], image_shifts[0])

    text_mlp_in = gather(text_first.astype(BF), core)
    image_mlp_in = gather(image_first.astype(BF), core)
    text_pre = product(text_mlp_in, text_up)
    image_pre = product(image_mlp_in, image_up)
    text_act = gelu_tanh(text_pre).astype(BF)
    image_act = gelu_tanh(image_pre).astype(BF)
    text_mid = text_first + scatter_sum(
        *[product(rows, text_down) for rows in halves(text_act)], core
    )
    image_mid = image_first + scatter_sum(
        *[product(rows, image_down) for rows in halves(image_act)], core
    )
    text_second = layer_norm(text_mid, text_gains[1], text_shifts[1])
    image_second = layer_norm(image_mid, image_gains[1], image_shifts[1])

    text_self_in = gather(text_second.astype(BF), core)
    image_self_in = gather(image_second.astype(BF), core)
    text_parts = product(text_self_in, w_self_text).astype(BF)
    image_parts = product(image_self_in, w_self_image).astype(BF)
    text_self_ctx, text_self_share = self_forward(
        text_parts, lengths, text_local, 3, self_mask_text
    )
    image_self_ctx, image_self_share = self_forward(
        image_parts, regions, image_local, 2, self_mask_image
    )
    text_last = text_second + scatter_sum(
        *[product(rows, text_self_out) for rows in halves(text_self_ctx)], core
    )
    image_last = image_second + scatter_sum(
        *[product(rows, image_self_out) for rows in halves(image_self_ctx)], core
    )
    text_result = layer_norm(text_last, text_gains[2], text_shifts[2]).astype(BF)
    image_result = layer_norm(image_last, image_gains[2], image_shifts[2]).astype(BF)

    text_late_grad, text_gain_c, text_shift_c = norm_back(
        text_last, text_gains[2], text_grad_out.astype(F32)
    )
    image_late_grad, image_gain_c, image_shift_c = norm_back(
        image_last, image_gains[2], image_grad_out.astype(F32)
    )
    text_late_all = gather(text_late_grad.astype(BF), core)
    image_late_all = gather(image_late_grad.astype(BF), core)
    text_parts_grad = self_backward(
        text_parts, text_self_share, product_nt(text_late_all, text_self_out).astype(BF),
        text_local, 3,
    )
    image_parts_grad = self_backward(
        image_parts, image_self_share, product_nt(image_late_all, image_self_out).astype(BF),
        image_local, 2,
    )
    text_back_self = scatter_sum(
        *[product_nt(rows, w_self_text) for rows in halves(text_parts_grad)], core
    )
    image_back_self = scatter_sum(
        *[product_nt(rows, w_self_image) for rows in halves(image_parts_grad)], core
    )
    grads_self = reduce_groups(
        [
            jnp.concatenate(
                [
                    product_tn(text_self_in, text_parts_grad),
                    product_tn(text_late_all, text_self_ctx),
                ],
                axis=1,
            ),
            product_tn(image_self_in, image_parts_grad),
            product_tn(image_late_all, image_self_ctx),
        ],
        group_count,
    )
    text_mid_grad, text_gain_b, text_shift_b = norm_back(
        text_mid, text_gains[1], text_late_grad + text_back_self
    )
    image_mid_grad, image_gain_b, image_shift_b = norm_back(
        image_mid, image_gains[1], image_late_grad + image_back_self
    )

    text_mlp_all = gather(text_mid_grad.astype(BF), core)
    image_mlp_all = gather(image_mid_grad.astype(BF), core)
    text_pre_grad = (product_nt(text_mlp_all, text_down) * gelu_slope(text_pre)).astype(BF)
    image_pre_grad = (product_nt(image_mlp_all, image_down) * gelu_slope(image_pre)).astype(BF)
    text_back_mlp = scatter_sum(
        *[product_nt(rows, text_up) for rows in halves(text_pre_grad)], core
    )
    image_back_mlp = scatter_sum(
        *[product_nt(rows, image_up) for rows in halves(image_pre_grad)], core
    )
    grads_mlp = reduce_groups(
        [
            product_tn(text_mlp_in, text_pre_grad),
            product_tn(text_mlp_all, text_act),
            product_tn(image_mlp_in, image_pre_grad),
            product_tn(image_mlp_all, image_act),
        ],
        group_count,
    )
    text_zero_grad, text_gain_a, text_shift_a = norm_back(
        text_zero, text_gains[0], text_mid_grad + text_back_mlp
    )
    image_zero_grad, image_gain_a, image_shift_a = norm_back(
        image_zero, image_gains[0], image_mid_grad + image_back_mlp
    )

    def norm_columns(*vectors):
        stacked = jnp.stack(vectors)
        for step in (1, 2):
            stacked = stacked + swap(stacked, "mp", step)
        return jnp.pad(stacked.T, ((0, 0), (0, 256 - len(vectors))))

    text_norm = norm_columns(
        text_gain_a, text_gain_b, text_gain_c, text_shift_a, text_shift_b, text_shift_c
    )
    image_norm = norm_columns(
        image_gain_a, image_gain_b, image_gain_c, image_shift_a, image_shift_b, image_shift_c
    )

    text_co_all = gather(text_zero_grad.astype(BF), core)
    image_co_all = gather(image_zero_grad.astype(BF), core)
    text_ctx_grad = product_nt(text_co_all, co_text_out).astype(BF)
    image_ctx_grad = product_nt(image_co_all, co_image_out).astype(BF)
    text_co_grad, image_co_grad = co_backward(
        text_co, image_co, text_share, image_share, text_ctx_grad, image_ctx_grad, order, co_local
    )
    text_in_grad = text_zero_grad + scatter_sum(
        *[product_nt(rows, w_co_text) for rows in halves(text_co_grad)], core
    )
    image_in_grad = image_zero_grad + scatter_sum(
        *[product_nt(rows, w_co_image) for rows in halves(image_co_grad)], core
    )
    bits = list(range(group_count.bit_length() - 1))
    grads_text_co = reduce_halving(
        [product_tn(text_all, text_co_grad), product_tn(text_co_all, text_ctx), text_norm],
        group_count,
        bits,
    )
    grads_image_co = reduce_halving(
        [product_tn(image_all, image_co_grad), product_tn(image_co_all, image_ctx), image_norm],
        group_count,
        bits[1:2] + bits[:1] + bits[2:],
    )

    def norm_part(columns):
        rows = columns.shape[0] // part_count
        mine = lax.dynamic_slice_in_dim(columns, spot * rows, rows, axis=0)[:, :6].T
        return mine[:3], mine[3:]

    text_gain_grad, text_shift_grad = norm_part(grads_text_co[2])
    image_gain_grad, image_shift_grad = norm_part(grads_image_co[2])
    text_self_columns = 3 * text_self_qkv.shape[2]
    return (
        text_result,
        image_result,
        text_in_grad,
        image_in_grad,
        apart(grads_text_co[0]),
        apart(grads_image_co[0]),
        grads_text_co[1].T,
        grads_image_co[1].T,
        grads_mlp[0],
        grads_mlp[1].T,
        grads_mlp[2],
        grads_mlp[3].T,
        apart(grads_self[0][:, :text_self_columns]),
        grads_self[0][:, text_self_columns:].T,
        apart(grads_self[1]),
        grads_self[2].T,
        text_gain_grad,
        text_shift_grad,
        image_gain_grad,
        image_shift_grad,
    )


def solution(mesh):
    tokens = P(("dp", "mp"), None)
    stack_in = P(None, None, "mp")
    rows_in = P("mp", None)
    columns_in = P(None, "mp")
    in_specs = (
        tokens, tokens, P("dp"), P("dp", None), P("dp", None),
        stack_in, stack_in, rows_in, rows_in,
        columns_in, rows_in, columns_in, rows_in,
        stack_in, rows_in, stack_in, rows_in,
        P(), P(), P(), P(),
        tokens, tokens,
    )
    stack_out = P(None, "dp", "mp")
    rows_out = P("mp", "dp")
    columns_out = P("dp", "mp")
    norm_out = P(None, ("dp", "mp"))
    out_specs = (
        tokens, tokens, tokens, tokens,
        stack_out, stack_out, rows_out, rows_out,
        columns_out, rows_out, columns_out, rows_out,
        stack_out, rows_out, stack_out, rows_out,
        norm_out, norm_out, norm_out, norm_out,
    )
    return jax.shard_map(
        per_device, mesh=mesh, in_specs=in_specs, out_specs=out_specs, check_vma=False
    )
```

time: 1680 us -> 556 us (0.33)
  waiting for transfers between devices: 1210 us -> 208 us
  matrix products: 222 us -> 67 us
  local copies, waits for them, and re-layouts: 125 us -> 70.9 us
  Pallas kernels: 0 us -> 51.6 us
  starting transfers between devices: 3.83 us -> 51.5 us
  blocking collectives: 21.6 us -> 0 us
    reduce_scatter x23 -> x2, waiting for transfers between devices: 954 us -> 0.01 us  [reduce_groups(): summed = lax.psum_scatter(flat, 'dp', scatter_dimension=0, tiled=True)]
    ppermute x0 -> x82, waiting for transfers between devices: none -> 208 us  [swap(): lax.ppermute(values, axis, [(i, i ^ flip) for i in range(lax.axis_size(ax...]
    all_gather x12 -> x0, waiting for transfers between devices: 151 us -> none  [the longest x1 22.4 us: per_device(): lax.all_gather(text_in, 'mp', axis=0, tiled=True)]
    unnamed x43 -> x2, waiting for transfers between devices: 106 us -> 0.03 us
    dot_general x44 -> x18, matrix products: 127 us -> 22 us  [product(): return jnp.dot(former, latter, preferred_element_type=F32)]
    pallas_call x0 -> x6, Pallas kernels: none -> 51.6 us  [the longest x2 18 us: self_forward(): pl.pallas_call(functools.partial(self_forward_kernel, heads, per_step, ma...]
    ppermute x0 -> x82, starting transfers between devices: none -> 51.4 us  [swap(): lax.ppermute(values, axis, [(i, i ^ flip) for i in range(lax.axis_size(ax...]
    another operation x40 -> x8, local copies, waits for them, and re-layouts: 35.5 us -> 1.27 us  [norm_columns(): stacked = jnp.stack(vectors)]
  transfers between devices with their start and end apart: 39 -> 84, of which waited for: 34 -> 26; matrix products, arithmetic and copies ran while one was open for 22% -> 35% of each run, Pallas kernels for 0% -> 8%
where the time goes in v1:
time: 556 us; the launch traced here: 549 us
  waiting for transfers between devices  208 us (37%)
  other arithmetic  82.3 us (15%)
  local copies, waits for them, and re-layouts  70.9 us (13%)
  matrix products  67 us (12%)
  Pallas kernels  51.6 us (9%)
  starting transfers between devices  51.5 us (9%)
  between operations  17.9 us (3%)
    ppermute x82, waiting for transfers between devices, swap(): lax.ppermute(values, axis, [(i, i ^ flip) for i in range(lax.axis_size(ax...  208 us
    unnamed x460, local copies, waits for them, and re-layouts  53.1 us
    ppermute x82, starting transfers between devices, swap(): lax.ppermute(values, axis, [(i, i ^ flip) for i in range(lax.axis_size(ax...  51.4 us
    dot_general x18, matrix products, product_nt(): lax.dot_general(former, latter, (((1,), (1,)), ((), ())), preferred_eleme...  25.3 us
    dot_general x18, matrix products, product(): return jnp.dot(former, latter, preferred_element_type=F32)  22 us
    dot_general x12, matrix products, product_tn(): lax.dot_general(former, latter, (((0,), (0,)), ((), ())), preferred_eleme...  19.7 us
    pallas_call x2, Pallas kernels, self_forward(): pl.pallas_call(functools.partial(self_forward_kernel, heads, per_step, ma...  18 us
    pallas_call x2, Pallas kernels, self_backward(): pl.pallas_call(functools.partial(self_backward_kernel, heads, per_step),...  16.1 us
  transfers between devices with their start and end apart: 84, of which 26 were waited for; matrix products, arithmetic and copies ran while one was open for 35% of the time, Pallas kernels for 8%

profile of v1, /device:TPU:0, one launch (start us, length us, event | category | flops | bytes accessed | tf_op | source)
XLA Modules:
  0.0 548.9 jit_solution(15128049976934999283)
XLA Ops:
  25.7 7.3 %collective-permute-done.1 = bf16[384,768]{0,1:T(8,128)(2,1)} collective-permute-done((bf16[384,768]{0,1:T(8,128)(2,1)S(1)}, bf16[384,768]{0,1:T(8,128)(2,1)}, u32[]{:S(2)}, u32[]{:S(2)}) %collective-permute-start.1) | collective-permute-done | bytes 589856 | tf_op jit(solution)/shard_map/ppermute | solution.py:392
  42.6 5.8 %co_forward.1 = (bf16[1536,256]{1,0:T(8,128)(2,1)S(1)}, bf16[768,256]{1,0:T(8,128)(2,1)S(1)}, bf16[6,2,256,128]{3,2,1,0:T(8,128)(2,1)S(1)}, bf16[6,2,128,256]{3,2,1,0:T(8,128)(2,1)S(1)}) custom-call(s32[24]{0:T(128)S(1)} %broadcast_select_fusion.50.order_ref, s32[24]{0:T(128)S(1)} %get-tuple-element.284.region_ref.count_ref, ...), custom_call_target="tpu_custom_call" | custom-call | flops 402653184 | bytes 8000000 | tf_op jit(solution)/shard_map/co_forward/pallas_call | solution.py:277
  56.0 9.3 %collective-permute-done.23 = bf16[192,1024]{1,0:T(8,128)(2,1)S(1)} collective-permute-done((bf16[192,1024]{1,0:T(8,128)(2,1)S(1)}, bf16[192,1024]{1,0:T(8,128)(2,1)S(1)}, u32[]{:S(2)}, u32[]{:S(2)}) %collective-permute-start.23) | collective-permute-done | bytes 393248 | tf_op jit(solution)/shard_map/ppermute | solution.py:392
  68.0 10.0 %collective-permute-done.8 = bf16[384,768]{0,1:T(8,128)(2,1)S(1)} collective-permute-done((bf16[384,768]{0,1:T(8,128)(2,1)S(1)}, bf16[384,768]{0,1:T(8,128)(2,1)S(1)}, u32[]{:S(2)}, u32[]{:S(2)}) %collective-permute-start.8) | collective-permute-done | bytes 589856 | tf_op jit(solution)/shard_map/ppermute | solution.py:392
  78.5 7.4 %collective-permute-done.25 = bf16[192,1024]{1,0:T(8,128)(2,1)S(1)} collective-permute-done((bf16[192,1024]{1,0:T(8,128)(2,1)S(1)}, bf16[192,1024]{1,0:T(8,128)(2,1)S(1)}, u32[]{:S(2)}, u32[]{:S(2)}) %collective-permute-start.25) | collective-permute-done | bytes 393248 | tf_op jit(solution)/shard_map/ppermute | solution.py:392
  98.5 4.9 collective-permute-done.10
  105.0 6.5 %collective-permute-done.29 = bf16[192,1024]{1,0:T(8,128)(2,1)} collective-permute-done((bf16[192,1024]{1,0:T(8,128)(2,1)}, bf16[192,1024]{1,0:T(8,128)(2,1)}, u32[]{:S(2)}, u32[]{:S(2)}) %collective-permute-start.29) | collective-permute-done | bytes 393248 | tf_op jit(solution)/shard_map/ppermute | solution.py:392
  116.6 5.4 multiply_convert_fusion
  129.4 4.8 self_forward.3
  136.0 5.7 %collective-permute-done.14 = bf16[384,768]{0,1:T(8,128)(2,1)S(1)} collective-permute-done((bf16[384,768]{0,1:T(8,128)(2,1)S(1)}, bf16[384,768]{0,1:T(8,128)(2,1)S(1)}, u32[]{:S(2)}, u32[]{:S(2)}) %collective-permute-start.14) | collective-permute-done | bytes 589856 | tf_op jit(solution)/shard_map/ppermute | solution.py:392
  145.8 8.9 %collective-permute-done.35 = bf16[192,1024]{1,0:T(8,128)(2,1)S(1)} collective-permute-done((bf16[192,1024]{1,0:T(8,128)(2,1)S(1)}, bf16[192,1024]{1,0:T(8,128)(2,1)S(1)}, u32[]{:S(2)}, u32[]{:S(2)}) %collective-permute-start.35) | collective-permute-done | bytes 393248 | tf_op jit(solution)/shard_map/ppermute | solution.py:392
  157.7 9.7 %collective-permute-done.16 = bf16[384,768]{0,1:T(8,128)(2,1)} collective-permute-done((bf16[384,768]{0,1:T(8,128)(2,1)}, bf16[384,768]{0,1:T(8,128)(2,1)}, u32[]{:S(2)}, u32[]{:S(2)}) %collective-permute-start.16) | collective-permute-done | bytes 589856 | tf_op jit(solution)/shard_map/ppermute | solution.py:392
  178.7 13.1 %self_forward.2 = (bf16[1536,192]{1,0:T(8,128)(2,1)S(1)}, bf16[12,3,128,128]{3,2,1,0:T(8,128)(2,1)S(1)}) custom-call(s32[24]{0:T(128)S(1)} %get-tuple-element.283.length_ref.count_ref, bf16[1536,576]{1,0:T(8,128)(2,1)S(1)} %convolution_convert_fusion.1.rows_ref), custom_call_target="tpu_custom_call" | custom-call | flops 150994944 | bytes 6000000 | tf_op jit(solution)/shard_map/self_forward/pallas_call | solution.py:348
  199.1 4.1 self_backward.3
  213.6 7.2 %collective-permute-done.56 = bf16[192,1024]{1,0:T(8,128)(2,1)S(1)} collective-permute-done((bf16[192,1024]{1,0:T(8,128)(2,1)S(1)}, bf16[192,1024]{1,0:T(8,128)(2,1)S(1)}, u32[]{:S(2)}, u32[]{:S(2)}) %collective-permute-start.56) | collective-permute-done | bytes 393248 | tf_op jit(solution)/shard_map/ppermute | solution.py:392
  225.6 7.9 %collective-permute-done.20 = bf16[384,768]{0,1:T(8,128)(2,1)S(1)} collective-permute-done((bf16[384,768]{0,1:T(8,128)(2,1)S(1)}, bf16[384,768]{0,1:T(8,128)(2,1)S(1)}, u32[]{:S(2)}, u32[]{:S(2)}) %collective-permute-start.20) | collective-permute-done | bytes 589856 | tf_op jit(solution)/shard_map/ppermute | solution.py:392
  237.2 4.2 collective-permute-done.58
  251.2 6.4 %collective-permute-done.37 = bf16[384,768]{0,1:T(8,128)(2,1)S(1)} collective-permute-done((bf16[384,768]{0,1:T(8,128)(2,1)S(1)}, bf16[384,768]{0,1:T(8,128)(2,1)S(1)}, u32[]{:S(2)}, u32[]{:S(2)}) %collective-permute-start.37) | collective-permute-done | bytes 589856 | tf_op jit(solution)/shard_map/ppermute | solution.py:392
  269.1 12.0 %self_backward.2 = bf16[1536,576]{1,0:T(8,128)(2,1)S(1)} custom-call(bf16[1536,576]{1,0:T(8,128)(2,1)S(1)} %convolution_convert_fusion.1.rows_ref, bf16[12,3,128,128]{3,2,1,0:T(8,128)(2,1)S(1)} %copy-done.7, bf16[1536,192]{1,0:T(8,128)(2,1)S(1)} %copy-done.5), custom_call_target="tpu_custom_call" | custom-call | flops 377487360 | bytes 9000000 | tf_op jit(solution)/shard_map/self_backward/pallas_call | solution.py:375
  312.1 18.9 %collective-permute-done.78 = f32[6,1024]{1,0:T(8,128)S(1)} collective-permute-done((f32[6,1024]{1,0:T(8,128)S(1)}, f32[6,1024]{1,0:T(8,128)S(1)}, u32[]{:S(2)}, u32[]{:S(2)}) %collective-permute-start.78) | collective-permute-done | bytes 24608 | tf_op jit(solution)/shard_map/ppermute | solution.py:392
  333.9 3.8 multiply_reduce_fusion
  342.9 11.1 %collective-permute-done.43 = bf16[384,768]{0,1:T(8,128)(2,1)} collective-permute-done((bf16[384,768]{0,1:T(8,128)(2,1)S(1)}, bf16[384,768]{0,1:T(8,128)(2,1)}, u32[]{:S(2)}, u32[]{:S(2)}) %collective-permute-start.43) | collective-permute-done | bytes 589856 | tf_op jit(solution)/shard_map/ppermute | solution.py:392
  358.6 7.4 %fusion.6 = bf16[1536,768]{1,0:T(8,128)(2,1)S(1)} fusion(f32[1536,768]{1,0:T(8,128)} %get-tuple-element.280, bf16[768,768]{1,0:T(8,128)(2,1)S(1)} %copy-done.204, bf16[384,768]{0,1:T(8,128)(2,1)S(1)} %get-tuple-element.193, bf16[384,768]{0,1:T(8,128)(2,1)S(1)} %get-tuple-element.192, bf16[384,768]{0,1:T(8,128)(2,1)S(1)} %get-tuple-element.191, ...), kind=kOutput, calls=%fused_computation.8 | convolution fusion | flops 1843789824 | bytes 10616832 | tf_op jit(solution)/shard_map/dot_general | solution.py:32
  377.2 13.4 %collective-permute-done.47 = bf16[384,768]{0,1:T(8,128)(2,1)S(1)} collective-permute-done((bf16[384,768]{0,1:T(8,128)(2,1)S(1)}, bf16[384,768]{0,1:T(8,128)(2,1)S(1)}, u32[]{:S(2)}, u32[]{:S(2)}) %collective-permute-start.47) | collective-permute-done | bytes 589856 | tf_op jit(solution)/shard_map/ppermute | solution.py:392
  399.9 7.5 %collective-permute-done.49 = bf16[384,768]{0,1:T(8,128)(2,1)} collective-permute-done((bf16[384,768]{0,1:T(8,128)(2,1)S(1)}, bf16[384,768]{0,1:T(8,128)(2,1)}, u32[]{:S(2)}, u32[]{:S(2)}) %collective-permute-start.49) | collective-permute-done | bytes 589856 | tf_op jit(solution)/shard_map/ppermute | solution.py:392
  416.2 11.8 %co_backward.1 = (bf16[1536,768]{1,0:T(8,128)(2,1)}, bf16[768,768]{1,0:T(8,128)(2,1)S(1)}) custom-call(s32[24]{0:T(128)S(1)} %copy-done.19, bf16[1536,768]{1,0:T(8,128)(2,1)} %convolution_convert_fusion.text_ref, bf16[768,768]{1,0:T(8,128)(2,1)S(1)} %copy-done.4, bf16[6,2,256,128]{3,2,1,0:T(8,128)(2,1)S(1)} %copy-done.9, ...), custom_call_target="tpu_custom_call" | custom-call | flops 805306368 | bytes 12000000 | tf_op jit(solution)/shard_map/co_backward/pallas_call | solution.py:317
  447.4 6.8 %collective-permute-done.71 = bf16[192,1024]{1,0:T(8,128)(2,1)S(1)} collective-permute-done((bf16[192,1024]{1,0:T(8,128)(2,1)S(1)}, bf16[192,1024]{1,0:T(8,128)(2,1)S(1)}, u32[]{:S(2)}, u32[]{:S(2)}) %collective-permute-start.71) | collective-permute-done | bytes 393248 | tf_op jit(solution)/shard_map/ppermute | solution.py:392
  455.4 16.2 %collective-permute-done.74 = bf16[2,2,480,256]{3,2,1,0:T(8,128)(2,1)S(1)} collective-permute-done((bf16[2,2,480,256]{3,2,1,0:T(8,128)(2,1)S(1)}, bf16[2,2,480,256]{3,2,1,0:T(8,128)(2,1)S(1)}, u32[]{:S(2)}, u32[]{:S(2)}) %collective-permute-start.74) | collective-permute-done | bytes 983072 | tf_op jit(solution)/shard_map/ppermute | solution.py:392
  482.5 14.9 %collective-permute-done.75 = bf16[2,480,256]{2,1,0:T(8,128)(2,1)S(1)} collective-permute-done((bf16[2,480,256]{2,1,0:T(8,128)(2,1)}, bf16[2,480,256]{2,1,0:T(8,128)(2,1)S(1)}, u32[]{:S(2)}, u32[]{:S(2)}) %collective-permute-start.75) | collective-permute-done | bytes 491552 | tf_op jit(solution)/shard_map/ppermute | solution.py:392
  497.6 5.2 collective-permute-start.76
  504.3 7.7 %collective-permute-done.76 = bf16[480,256]{1,0:T(8,128)(2,1)S(1)} collective-permute-done((bf16[480,256]{1,0:T(8,128)(2,1)S(1)}, bf16[480,256]{1,0:T(8,128)(2,1)S(1)}, u32[]{:S(2)}, u32[]{:S(2)}) %collective-permute-start.76) | collective-permute-done | bytes 245792 | tf_op jit(solution)/shard_map/ppermute | solution.py:392
  523.1 10.9 %collective-permute-done.81 = bf16[640,256]{1,0:T(8,128)(2,1)S(1)} collective-permute-done((bf16[640,256]{1,0:T(8,128)(2,1)S(1)}, bf16[640,256]{1,0:T(8,128)(2,1)S(1)}, u32[]{:S(2)}, u32[]{:S(2)}) %collective-permute-start.81) | collective-permute-done | bytes 327712 | tf_op jit(solution)/shard_map/ppermute | solution.py:392
  (838 shorter events, 255.1 us)
Async XLA Ops:
  7.2 507.7 %reduce-scatter.5.cloned.1.call-start = ((), (), s32[]{:S(2)}) async-start(), calls=%async_computation.3 | async-start | bytes 3686400 | tf_op jit(solution)/shard_map/reduce_scatter | solution.py:455
  7.3 17.3 %collective-permute-start.3 = (bf16[192,1024]{1,0:T(8,128)(2,1)}, bf16[192,1024]{1,0:T(8,128)(2,1)}, u32[]{:S(2)}, u32[]{:S(2)}) collective-permute-start(bf16[192,1024]{1,0:T(8,128)(2,1)} %param.24), channel_id=1, source_target_pairs={{0,1},{1,0},{2,3},{3,2},{4,5},{5,4},{6,7},{7,6},{8,9},{9,8},{10,11... | collective-permute-start | bytes 1179656 | tf_op jit(solution)/shard_map/ppermute | solution.py:392
  7.8 16.3 %collective-permute-start.4 = (bf16[192,1024]{1,0:T(8,128)(2,1)}, bf16[192,1024]{1,0:T(8,128)(2,1)}, u32[]{:S(2)}, u32[]{:S(2)}) collective-permute-start(bf16[192,1024]{1,0:T(8,128)(2,1)} %param.24), channel_id=1, source_target_pairs={{0,2},{1,3},{2,0},{3,1},{4,6},{5,7},{6,4},{7,5},{8,10},{9,11},{10,... | collective-permute-start | bytes 1179656 | tf_op jit(solution)/shard_map/ppermute | solution.py:392
  11.8 21.3 %collective-permute-start.1 = (bf16[384,768]{0,1:T(8,128)(2,1)S(1)}, bf16[384,768]{0,1:T(8,128)(2,1)}, u32[]{:S(2)}, u32[]{:S(2)}) collective-permute-start(bf16[384,768]{0,1:T(8,128)(2,1)S(1)} %copy.234), channel_id=1, source_target_pairs={{0,2},{1,3},{2,0},{3,1},{4,6},{5,7},{6,4},{7,5},{8,10},{9,11},{10,... | collective-permute-start | bytes 1769480 | tf_op jit(solution)/shard_map/ppermute | solution.py:392
  12.0 21.0 %collective-permute-start = (bf16[384,768]{0,1:T(8,128)(2,1)S(1)}, bf16[384,768]{0,1:T(8,128)(2,1)}, u32[]{:S(2)}, u32[]{:S(2)}) collective-permute-start(bf16[384,768]{0,1:T(8,128)(2,1)S(1)} %copy.234), channel_id=1, source_target_pairs={{0,1},{1,0},{2,3},{3,2},{4,5},{5,4},{6,7},{7,6},{8,9},{9,8},{10,11... | collective-permute-start | bytes 1769480 | tf_op jit(solution)/shard_map/ppermute | solution.py:392
  55.6 22.4 %collective-permute-start.8 = (bf16[384,768]{0,1:T(8,128)(2,1)S(1)}, bf16[384,768]{0,1:T(8,128)(2,1)S(1)}, u32[]{:S(2)}, u32[]{:S(2)}) collective-permute-start(bf16[384,768]{0,1:T(8,128)(2,1)S(1)} %add_convert_fusion.6), channel_id=1, source_target_pairs={{0,2},{1,3},{2,0},{3,1},{4,6},{5,7},{6,4},{7,5},{8,10},{9,11},{10,... | collective-permute-start | bytes 1769480 | tf_op jit(solution)/shard_map/ppermute | solution.py:392
  66.2 19.7 %collective-permute-start.25 = (bf16[192,1024]{1,0:T(8,128)(2,1)S(1)}, bf16[192,1024]{1,0:T(8,128)(2,1)S(1)}, u32[]{:S(2)}, u32[]{:S(2)}) collective-permute-start(bf16[192,1024]{1,0:T(8,128)(2,1)S(1)} %fusion.53), channel_id=1, source_target_pairs={{0,2},{1,3},{2,0},{3,1},{4,6},{5,7},{6,4},{7,5},{8,10},{9,11},{10,... | collective-permute-start | bytes 1179656 | tf_op jit(solution)/shard_map/ppermute | solution.py:392
  68.0 21.0 %collective-permute-start.24 = (bf16[192,1024]{1,0:T(8,128)(2,1)S(1)}, bf16[192,1024]{1,0:T(8,128)(2,1)S(1)}, u32[]{:S(2)}, u32[]{:S(2)}) collective-permute-start(bf16[192,1024]{1,0:T(8,128)(2,1)S(1)} %fusion.53), channel_id=1, source_target_pairs={{0,1},{1,0},{2,3},{3,2},{4,5},{5,4},{6,7},{7,6},{8,9},{9,8},{10,11... | collective-permute-start | bytes 1179656 | tf_op jit(solution)/shard_map/ppermute | solution.py:392
  87.0 16.4 %collective-permute-start.10 = (bf16[384,768]{0,1:T(8,128)(2,1)}, bf16[384,768]{0,1:T(8,128)(2,1)}, u32[]{:S(2)}, u32[]{:S(2)}) collective-permute-start(bf16[384,768]{0,1:T(8,128)(2,1)} %fusion.35), channel_id=1, source_target_pairs={{0,2},{1,3},{2,0},{3,1},{4,6},{5,7},{6,4},{7,5},{8,10},{9,11},{10,... | collective-permute-start | bytes 1769480 | tf_op jit(solution)/shard_map/ppermute | solution.py:392
  144.6 22.9 %collective-permute-start.16 = (bf16[384,768]{0,1:T(8,128)(2,1)}, bf16[384,768]{0,1:T(8,128)(2,1)}, u32[]{:S(2)}, u32[]{:S(2)}) collective-permute-start(bf16[384,768]{0,1:T(8,128)(2,1)} %fusion.36), channel_id=1, source_target_pairs={{0,2},{1,3},{2,0},{3,1},{4,6},{5,7},{6,4},{7,5},{8,10},{9,11},{10,... | collective-permute-start | bytes 1769480 | tf_op jit(solution)/shard_map/ppermute | solution.py:392
  145.8 23.8 %collective-permute-start.15 = (bf16[384,768]{0,1:T(8,128)(2,1)}, bf16[384,768]{0,1:T(8,128)(2,1)}, u32[]{:S(2)}, u32[]{:S(2)}) collective-permute-start(bf16[384,768]{0,1:T(8,128)(2,1)} %fusion.36), channel_id=1, source_target_pairs={{0,1},{1,0},{2,3},{3,2},{4,5},{5,4},{6,7},{7,6},{8,9},{9,8},{10,11... | collective-permute-start | bytes 1769480 | tf_op jit(solution)/shard_map/ppermute | solution.py:392
  157.0 17.1 %collective-permute-start.52 = (bf16[192,1024]{1,0:T(8,128)(2,1)S(1)}, bf16[192,1024]{1,0:T(8,128)(2,1)}, u32[]{:S(2)}, u32[]{:S(2)}) collective-permute-start(bf16[192,1024]{1,0:T(8,128)(2,1)S(1)} %fusion.124), channel_id=1, source_target_pairs={{0,2},{1,3},{2,0},{3,1},{4,6},{5,7},{6,4},{7,5},{8,10},{9,11},{10,... | collective-permute-start | bytes 1179656 | tf_op jit(solution)/shard_map/ppermute | solution.py:392
  157.7 16.3 %collective-permute-start.51 = (bf16[192,1024]{1,0:T(8,128)(2,1)S(1)}, bf16[192,1024]{1,0:T(8,128)(2,1)S(1)}, u32[]{:S(2)}, u32[]{:S(2)}) collective-permute-start(bf16[192,1024]{1,0:T(8,128)(2,1)S(1)} %fusion.124), channel_id=1, source_target_pairs={{0,1},{1,0},{2,3},{3,2},{4,5},{5,4},{6,7},{7,6},{8,9},{9,8},{10,11... | collective-permute-start | bytes 1179656 | tf_op jit(solution)/shard_map/ppermute | solution.py:392
  174.1 21.2 %collective-permute-start.53 = (bf16[192,1024]{1,0:T(8,128)(2,1)}, bf16[192,1024]{1,0:T(8,128)(2,1)S(1)}, u32[]{:S(2)}, u32[]{:S(2)}) collective-permute-start(bf16[192,1024]{1,0:T(8,128)(2,1)} %collective-permute-done.52), channel_id=1, source_target_pairs={{0,1},{1,0},{2,3},{3,2},{4,5},{5,4},{6,7},{7,6},{8,9},{9,8},{10,11... | collective-permute-start | bytes 1179656 | tf_op jit(solution)/shard_map/ppermute | solution.py:392
  193.8 17.6 %collective-permute-start.19 = (bf16[384,768]{0,1:T(8,128)(2,1)}, bf16[384,768]{0,1:T(8,128)(2,1)}, u32[]{:S(2)}, u32[]{:S(2)}) collective-permute-start(bf16[384,768]{0,1:T(8,128)(2,1)} %select_convert_fusion.6), channel_id=1, source_target_pairs={{0,1},{1,0},{2,3},{3,2},{4,5},{5,4},{6,7},{7,6},{8,9},{9,8},{10,11... | collective-permute-start | bytes 1769480 | tf_op jit(solution)/shard_map/ppermute | solution.py:392
  195.3 30.3 %collective-permute-start.18 = (bf16[384,768]{0,1:T(8,128)(2,1)}, bf16[384,768]{0,1:T(8,128)(2,1)}, u32[]{:S(2)}, u32[]{:S(2)}) collective-permute-start(bf16[384,768]{0,1:T(8,128)(2,1)} %select_convert_fusion.7), channel_id=1, source_target_pairs={{0,1},{1,0},{2,3},{3,2},{4,5},{5,4},{6,7},{7,6},{8,9},{9,8},{10,11... | collective-permute-start | bytes 1769480 | tf_op jit(solution)/shard_map/ppermute | solution.py:392
  212.8 20.7 %collective-permute-start.20 = (bf16[384,768]{0,1:T(8,128)(2,1)S(1)}, bf16[384,768]{0,1:T(8,128)(2,1)S(1)}, u32[]{:S(2)}, u32[]{:S(2)}) collective-permute-start(bf16[384,768]{0,1:T(8,128)(2,1)S(1)} %add_convert_fusion.4), channel_id=1, source_target_pairs={{0,2},{1,3},{2,0},{3,1},{4,6},{5,7},{6,4},{7,5},{8,10},{9,11},{10,... | collective-permute-start | bytes 1769480 | tf_op jit(solution)/shard_map/ppermute | solution.py:392
  224.3 17.0 %collective-permute-start.58 = (bf16[192,1024]{1,0:T(8,128)(2,1)S(1)}, bf16[192,1024]{1,0:T(8,128)(2,1)S(1)}, u32[]{:S(2)}, u32[]{:S(2)}) collective-permute-start(bf16[192,1024]{1,0:T(8,128)(2,1)S(1)} %get-tuple-element.153), channel_id=1, source_target_pairs={{0,2},{1,3},{2,0},{3,1},{4,6},{5,7},{6,4},{7,5},{8,10},{9,11},{10,... | collective-permute-start | bytes 1179656 | tf_op jit(solution)/shard_map/ppermute | solution.py:392
  225.6 18.9 %collective-permute-start.57 = (bf16[192,1024]{1,0:T(8,128)(2,1)S(1)}, bf16[192,1024]{1,0:T(8,128)(2,1)S(1)}, u32[]{:S(2)}, u32[]{:S(2)}) collective-permute-start(bf16[192,1024]{1,0:T(8,128)(2,1)S(1)} %get-tuple-element.153), channel_id=1, source_target_pairs={{0,1},{1,0},{2,3},{3,2},{4,5},{5,4},{6,7},{7,6},{8,9},{9,8},{10,11... | collective-permute-start | bytes 1179656 | tf_op jit(solution)/shard_map/ppermute | solution.py:392
  258.4 42.0 %collective-permute-start.60 = (bf16[192,1024]{1,0:T(8,128)(2,1)}, bf16[192,1024]{1,0:T(8,128)(2,1)}, u32[]{:S(2)}, u32[]{:S(2)}) collective-permute-start(bf16[192,1024]{1,0:T(8,128)(2,1)} %select_convert_fusion.15), channel_id=1, source_target_pairs={{0,1},{1,0},{2,3},{3,2},{4,5},{5,4},{6,7},{7,6},{8,9},{9,8},{10,11... | collective-permute-start | bytes 1179656 | tf_op jit(solution)/shard_map/ppermute | solution.py:392
  259.9 40.4 %collective-permute-start.62 = (bf16[192,1024]{1,0:T(8,128)(2,1)}, bf16[192,1024]{1,0:T(8,128)(2,1)}, u32[]{:S(2)}, u32[]{:S(2)}) collective-permute-start(bf16[192,1024]{1,0:T(8,128)(2,1)} %add_convert_fusion.8), channel_id=1, source_target_pairs={{0,2},{1,3},{2,0},{3,1},{4,6},{5,7},{6,4},{7,5},{8,10},{9,11},{10,... | collective-permute-start | bytes 1179656 | tf_op jit(solution)/shard_map/ppermute | solution.py:392
  293.4 40.4 %collective-permute-start.39 = (bf16[384,768]{0,1:T(8,128)(2,1)}, bf16[384,768]{0,1:T(8,128)(2,1)}, u32[]{:S(2)}, u32[]{:S(2)}) collective-permute-start(bf16[384,768]{0,1:T(8,128)(2,1)} %select_convert_fusion.5), channel_id=1, source_target_pairs={{0,1},{1,0},{2,3},{3,2},{4,5},{5,4},{6,7},{7,6},{8,9},{9,8},{10,11... | collective-permute-start | bytes 1769480 | tf_op jit(solution)/shard_map/ppermute | solution.py:392
  306.0 27.7 %collective-permute-start.41 = (bf16[384,768]{0,1:T(8,128)(2,1)}, bf16[384,768]{0,1:T(8,128)(2,1)}, u32[]{:S(2)}, u32[]{:S(2)}) collective-permute-start(bf16[384,768]{0,1:T(8,128)(2,1)} %add_convert_fusion.2), channel_id=1, source_target_pairs={{0,2},{1,3},{2,0},{3,1},{4,6},{5,7},{6,4},{7,5},{8,10},{9,11},{10,... | collective-permute-start | bytes 1769480 | tf_op jit(solution)/shard_map/ppermute | solution.py:392
  308.1 25.7 %collective-permute-start.64 = (bf16[192,1024]{1,0:T(8,128)(2,1)}, bf16[192,1024]{1,0:T(8,128)(2,1)}, u32[]{:S(2)}, u32[]{:S(2)}) collective-permute-start(bf16[192,1024]{1,0:T(8,128)(2,1)} %get-tuple-element.150), channel_id=1, source_target_pairs={{0,2},{1,3},{2,0},{3,1},{4,6},{5,7},{6,4},{7,5},{8,10},{9,11},{10,... | collective-permute-start | bytes 1179656 | tf_op jit(solution)/shard_map/ppermute | solution.py:392
  310.2 20.8 %collective-permute-start.78 = (f32[6,1024]{1,0:T(8,128)S(1)}, f32[6,1024]{1,0:T(8,128)S(1)}, u32[]{:S(2)}, u32[]{:S(2)}) collective-permute-start(f32[6,1024]{1,0:T(8,128)S(1)} %add.432), channel_id=1, source_target_pairs={{0,2},{1,3},{2,0},{3,1},{4,6},{5,7},{6,4},{7,5},{8,10},{9,11},{10,... | collective-permute-start | bytes 73736 | tf_op jit(solution)/shard_map/ppermute | solution.py:392
  312.0 225.2 %reduce-scatter.3.cloned.1.call-start = ((), (), s32[]{:S(2)}) async-start(), calls=%async_computation.2 | async-start | bytes 3833856 | tf_op jit(solution)/shard_map/reduce_scatter | solution.py:455
  312.0 26.8 %collective-permute-start.63 = (bf16[192,1024]{1,0:T(8,128)(2,1)}, bf16[192,1024]{1,0:T(8,128)(2,1)}, u32[]{:S(2)}, u32[]{:S(2)}) collective-permute-start(bf16[192,1024]{1,0:T(8,128)(2,1)} %get-tuple-element.150), channel_id=1, source_target_pairs={{0,1},{1,0},{2,3},{3,2},{4,5},{5,4},{6,7},{7,6},{8,9},{9,8},{10,11... | collective-permute-start | bytes 1179656 | tf_op jit(solution)/shard_map/ppermute | solution.py:392
  438.3 33.3 %collective-permute-start.74 = (bf16[2,2,480,256]{3,2,1,0:T(8,128)(2,1)S(1)}, bf16[2,2,480,256]{3,2,1,0:T(8,128)(2,1)S(1)}, u32[]{:S(2)}, u32[]{:S(2)}) collective-permute-start(bf16[2,2,480,256]{3,2,1,0:T(8,128)(2,1)S(1)} %fusion.37), channel_id=1, source_target_pairs={{0,4},{4,0},{8,12},{12,8},{16,20},{20,16},{24,28},{28,24},{1,5},{5... | collective-permute-start | bytes 2949128 | tf_op jit(solution)/shard_map/ppermute | solution.py:392
  440.4 35.1 %collective-permute-start.66 = (bf16[384,768]{0,1:T(8,128)(2,1)S(1)}, bf16[384,768]{0,1:T(8,128)(2,1)S(1)}, u32[]{:S(2)}, u32[]{:S(2)}) collective-permute-start(bf16[384,768]{0,1:T(8,128)(2,1)S(1)} %select_convert_fusion.1), channel_id=1, source_target_pairs={{0,1},{1,0},{2,3},{3,2},{4,5},{5,4},{6,7},{7,6},{8,9},{9,8},{10,11... | collective-permute-start | bytes 1769480 | tf_op jit(solution)/shard_map/ppermute | solution.py:392
  444.2 35.6 %collective-permute-start.79 = (bf16[2,2,640,256]{3,2,1,0:T(8,128)(2,1)}, bf16[2,2,640,256]{3,2,1,0:T(8,128)(2,1)}, u32[]{:S(2)}, u32[]{:S(2)}) collective-permute-start(bf16[2,2,640,256]{3,2,1,0:T(8,128)(2,1)} %fusion.12), channel_id=1, source_target_pairs={{0,8},{4,12},{8,0},{12,4},{16,24},{20,28},{24,16},{28,20},{1,9},{5... | collective-permute-start | bytes 3932168 | tf_op jit(solution)/shard_map/ppermute | solution.py:392
  446.1 29.4 %collective-permute-start.68 = (bf16[384,768]{0,1:T(8,128)(2,1)S(1)}, bf16[384,768]{0,1:T(8,128)(2,1)S(1)}, u32[]{:S(2)}, u32[]{:S(2)}) collective-permute-start(bf16[384,768]{0,1:T(8,128)(2,1)S(1)} %add_convert_fusion), channel_id=1, source_target_pairs={{0,2},{1,3},{2,0},{3,1},{4,6},{5,7},{6,4},{7,5},{8,10},{9,11},{10,... | collective-permute-start | bytes 1769480 | tf_op jit(solution)/shard_map/ppermute | solution.py:392
  473.8 23.5 %collective-permute-start.75 = (bf16[2,480,256]{2,1,0:T(8,128)(2,1)}, bf16[2,480,256]{2,1,0:T(8,128)(2,1)S(1)}, u32[]{:S(2)}, u32[]{:S(2)}) collective-permute-start(bf16[2,480,256]{2,1,0:T(8,128)(2,1)} %fusion.66), channel_id=1, source_target_pairs={{0,8},{4,12},{8,0},{12,4},{16,24},{20,28},{24,16},{28,20},{1,9},{5... | collective-permute-start | bytes 1474568 | tf_op jit(solution)/shard_map/ppermute | solution.py:392
  (262 other events, 2296.7 us)
Sparse Core Ops, SparseCore 0:
  312.1 76.9 reduce-scatter.4
  409.4 96.8 reduce-scatter.2

commit v2 on v1

--- a/solution.py
+++ b/solution.py
@@ -388,6 +388,437 @@
     )(rows_in, shares, grad)
 
 
+MESH = pl.DeviceIdType.MESH
+BIG_LIMIT = 60 * 1024 * 1024
+
+
+class Bench:
+    def __init__(self, refs, fetched, flushed, counts):
+        self.refs = refs
+        self.fetches = {}
+        self.flushes = []
+        self.flush_index = {name: i for i, name in enumerate(flushed)}
+        self.copies = 0
+        for index, name in enumerate(fetched):
+            copy = pltpu.make_async_copy(
+                refs["in_" + name], refs[name], refs["fetch_sems"].at[index]
+            )
+            copy.start()
+            self.fetches[name] = copy
+
+    def __getattr__(self, name):
+        fetches = self.__dict__["fetches"]
+        if name in fetches:
+            fetches.pop(name).wait()
+        return self.__dict__["refs"][name]
+
+    def flush(self, *names):
+        for name in names:
+            copy = pltpu.make_async_copy(
+                self.refs[name],
+                self.refs["out_" + name],
+                self.refs["flush_sems"].at[self.flush_index.pop(name)],
+            )
+            copy.start()
+            self.flushes.append(copy)
+
+    def remote(self, source, target, peer):
+        index = self.copies
+        self.copies += 1
+        return pltpu.make_async_remote_copy(
+            src_ref=source,
+            dst_ref=target,
+            send_sem=self.refs["send_sems"].at[index],
+            recv_sem=self.refs["recv_sems"].at[index],
+            device_id=peer,
+            device_id_type=MESH,
+        )
+
+    def close(self):
+        for name in list(self.flush_index):
+            self.flush(name)
+        for copy in self.flushes:
+            copy.wait()
+
+
+def exchange_kernel(body, name, collective, peers, inputs, outputs, scratch, copies, work):
+    fetched = [key for key, (_, kind) in inputs.items() if kind == "hbm"]
+    flushed = [key for key, (_, _, kind) in outputs.items() if kind == "hbm"]
+    spaces = {"hbm": pl.ANY, "vmem": pltpu.VMEM, "smem": pltpu.SMEM}
+    names = [("in_" + key if kind == "hbm" else key) for key, (_, kind) in inputs.items()]
+    names += [("out_" + key if kind == "hbm" else key) for key, (_, _, kind) in outputs.items()]
+    shapes = []
+    for key in fetched:
+        names.append(key)
+        shapes.append(pltpu.VMEM(inputs[key][0].shape, inputs[key][0].dtype))
+    for key in flushed:
+        names.append(key)
+        shapes.append(pltpu.VMEM(outputs[key][0], outputs[key][1]))
+    for key, (shape, dtype) in scratch.items():
+        names.append(key)
+        shapes.append(pltpu.VMEM(shape, dtype))
+    for key, count in (
+        ("fetch_sems", len(fetched)), ("flush_sems", len(flushed)),
+        ("send_sems", copies), ("recv_sems", copies),
+    ):
+        names.append(key)
+        shapes.append(pltpu.SemaphoreType.DMA((max(count, 1),)))
+
+    def kernel(*refs):
+        bench = Bench(dict(zip(names, refs)), fetched, flushed, copies)
+        barrier = pltpu.get_barrier_semaphore()
+        partners = peers()
+        for partner in partners:
+            pl.semaphore_signal(barrier, inc=1, device_id=partner, device_id_type=MESH)
+        pl.semaphore_wait(barrier, len(partners))
+        body(bench)
+        bench.close()
+
+    flops, moved, exps = work
+    results = pl.pallas_call(
+        kernel,
+        in_specs=[pl.BlockSpec(memory_space=spaces[kind]) for _, kind in inputs.values()],
+        out_specs=[pl.BlockSpec(memory_space=spaces[kind]) for _, _, kind in outputs.values()],
+        out_shape=[shape_of(shape, dtype) for shape, dtype, _ in outputs.values()],
+        scratch_shapes=shapes,
+        compiler_params=pltpu.CompilerParams(
+            collective_id=collective, has_side_effects=True, vmem_limit_bytes=BIG_LIMIT
+        ),
+        cost_estimate=cost(flops, moved, exps),
+        name=name,
+    )(*[array for array, _ in inputs.values()])
+    return dict(zip(outputs, results))
+
+
+def group_peers():
+    spot = lax.axis_index("mp")
+    core = lax.rem(spot, 2)
+    chip = lax.div(spot, 2)
+    return core, {"mp": spot + 1 - 2 * core}, {"mp": spot + 2 - 4 * chip}
+
+
+class Stream:
+    def __init__(self, bench, tag, rows):
+        self.bench = bench
+        self.rows = rows
+        self.core, self.core_peer, self.chip_peer = group_peers()
+        self.other = 1 - self.core
+        for key in ("give", "got", "send", "recv", "acc"):
+            setattr(self, key, getattr(bench, tag + "_" + key))
+
+    def place(self, half, core):
+        step = self.rows & -self.rows
+        return pl.ds(pl.multiple_of((2 * half + core) * self.rows, step), self.rows)
+
+    def gather(self, full):
+        own = full.at[self.place(0, self.core)]
+        far = full.at[self.place(1, self.core)]
+        self.across = self.bench.remote(own, far, self.chip_peer)
+        self.near = self.bench.remote(own, own, self.core_peer)
+        self.relay = self.bench.remote(far, far, self.core_peer)
+        self.across.start()
+        self.near.start()
+
+    def arrive(self, half, project):
+        if half == 0:
+            project(0, self.core)
+            self.near.wait_recv()
+            project(0, self.other)
+        else:
+            self.across.wait_recv()
+            self.relay.start()
+            project(1, self.core)
+            self.relay.wait_recv()
+            project(1, self.other)
+
+    def open_sum(self):
+        self.hand = [
+            self.bench.remote(self.give.at[half], self.got.at[half], self.core_peer)
+            for half in (0, 1)
+        ]
+        self.post = self.bench.remote(self.send, self.recv, self.chip_peer)
+
+    def partial(self, half, output):
+        self.give[half] = output(half, self.other).astype(BF)
+        self.hand[half].start()
+        self.acc[half] = output(half, self.core)
+        if half == 1:
+            self.hand[1].wait_recv()
+            self.send[...] = (self.acc[1] + self.got[1].astype(F32)).astype(BF)
+            self.post.start()
+
+    def settle(self, gathered=True):
+        self.hand[0].wait_recv()
+        self.post.wait_recv()
+        self.hand[0].wait_send()
+        self.hand[1].wait_send()
+        self.post.wait_send()
+        if gathered:
+            self.finish_gather()
+
+    def finish_gather(self):
+        self.across.wait_send()
+        self.near.wait_send()
+        self.relay.wait_send()
+
+    def piece(self, rows):
+        return self.acc[0, rows] + self.got[0, rows].astype(F32) + self.recv[rows].astype(F32)
+
+
+CHUNK = 32
+
+
+def chunks(count, step, start):
+    def once(index, carry):
+        return step(pl.ds(pl.multiple_of(index * CHUNK, CHUNK), CHUNK), carry)
+
+    return lax.fori_loop(0, count // CHUNK, once, start)
+
+
+def folded(values):
+    return jnp.sum(values.reshape(CHUNK // 8, 8, values.shape[-1]), axis=0)
+
+
+def stream_scratch(tag, rows, width):
+    return {
+        tag + "_give": ((2, rows, width), BF),
+        tag + "_got": ((2, rows, width), BF),
+        tag + "_send": ((rows, width), BF),
+        tag + "_recv": ((rows, width), BF),
+        tag + "_acc": ((2, rows, width), F32),
+    }
+
+
+def at_offset(ref, offset, rows):
+    return ref.at[pl.ds(pl.multiple_of(offset + rows.start, CHUNK), rows.size)]
+
+
+def attend_many(parts_ref, share_ref, context_ref, base, first_block, blocks, heads, masker):
+    inner = parts_ref.shape[1] // 3
+    size = inner // heads
+    scaling = size ** (-0.5)
+    rows = [
+        pl.ds(pl.multiple_of(base + block * ROW_LEN, CHUNK), ROW_LEN) for block in range(blocks)
+    ]
+    masks = [masker(first_block + block) for block in range(blocks)]
+    scores = []
+    for block in range(blocks):
+        for head in range(heads):
+            queries = parts_ref[rows[block], head * size : (head + 1) * size]
+            keys = parts_ref[rows[block], inner + head * size : inner + (head + 1) * size]
+            scores.append(jnp.where(masks[block], product_nt(queries, keys) * scaling, -1e9))
+    scores = jnp.concatenate(scores, axis=0)
+    exponent = jnp.exp(scores - jnp.max(scores, axis=-1, keepdims=True))
+    shares = (exponent / jnp.sum(exponent, axis=-1, keepdims=True)).astype(BF)
+    for block in range(blocks):
+        contexts = []
+        for head in range(heads):
+            at = (block * heads + head) * ROW_LEN
+            piece = shares[at : at + ROW_LEN]
+            share_ref[first_block + block, head] = piece
+            values = parts_ref[rows[block], 2 * inner + head * size : 2 * inner + (head + 1) * size]
+            contexts.append(product(piece, values).astype(BF))
+        context_ref[rows[block], :] = jnp.concatenate(contexts, axis=1)
+
+
+def norm_chunk(values, gain, shift):
+    centre = values - jnp.mean(values, axis=-1, keepdims=True)
+    spread = jnp.mean(centre * centre, axis=-1, keepdims=True)
+    return centre * lax.rsqrt(spread + epsilon) * gain + shift
+
+
+def forward_kernel(ctx_t, ctx_i, text_in, image_in, weights, norms, text_g, image_g, lengths, regions,
+                   text_local, image_local):
+    (co_text_out, co_image_out, text_up, text_down, image_up, image_down,
+     w_self_text, text_self_out, w_self_image, image_self_out) = weights
+    n_t, d_t = text_in.shape
+    n_i, d_i = image_in.shape
+    ff_t, ff_i = text_up.shape[1], image_up.shape[1]
+    in_t, in_i = text_self_out.shape[0], image_self_out.shape[0]
+    inputs = {
+        "lengths": (lengths, "smem"), "regions": (regions, "smem"),
+        "gains_t": (norms[0], "vmem"), "shifts_t": (norms[1], "vmem"),
+        "gains_i": (norms[2], "vmem"), "shifts_i": (norms[3], "vmem"),
+        "ctx_i": (ctx_i, "hbm"), "w_co_i": (co_image_out, "hbm"),
+        "ctx_t": (ctx_t, "hbm"), "w_co_t": (co_text_out, "hbm"),
+        "x_i": (image_in, "hbm"), "x_t": (text_in, "hbm"),
+        "up_i": (image_up, "hbm"), "down_i": (image_down, "hbm"),
+        "up_t": (text_up, "hbm"), "down_t": (text_down, "hbm"),
+        "qkv_i": (w_self_image, "hbm"), "so_i": (image_self_out, "hbm"),
+        "qkv_t": (w_self_text, "hbm"), "so_t": (text_self_out, "hbm"),
+        "g_i": (image_g, "hbm"), "g_t": (text_g, "hbm"),
+    }
+    outputs = {}
+    scratch = {}
+    for tag, n, d, ff, inner, heads in (
+        ("t", n_t, d_t, ff_t, in_t, text_local), ("i", n_i, d_i, ff_i, in_i, image_local),
+    ):
+        outputs.update({
+            "zero_" + tag: ((n, d), F32, "hbm"),
+            "mid_" + tag: ((n, d), F32, "hbm"),
+            "mlp_" + tag: ((4 * n, d), BF, "hbm"),
+            "act_" + tag: ((4 * n, ff), BF, "hbm"),
+            "slope_" + tag: ((4 * n, ff), BF, "hbm"),
+            "self_" + tag: ((4 * n, d), BF, "hbm"),
+            "parts_" + tag: ((4 * n, 3 * inner), BF, "hbm"),
+            "share_" + tag: ((4 * n // ROW_LEN, heads, ROW_LEN, ROW_LEN), BF, "hbm"),
+            "ctx2_" + tag: ((4 * n, inner), BF, "hbm"),
+            "late_" + tag: ((n, d), F32, "hbm"),
+            "result_" + tag: ((n, d), BF, "hbm"),
+            "gain_" + tag: ((8, d), F32, "vmem"),
+            "shift_" + tag: ((8, d), F32, "vmem"),
+        })
+        scratch.update(stream_scratch(tag, n, d))
+        scratch["first_" + tag] = ((n, d), F32)
+
+    def body(bench):
+        streams = {tag: Stream(bench, tag, n) for tag, n in (("i", n_i), ("t", n_t))}
+        get = lambda key, tag: getattr(bench, key + "_" + tag)
+
+        for tag, stream in streams.items():
+            context, weight = get("ctx", tag), get("w_co", tag)
+            output = lambda half, core: product(context[stream.place(half, core)], weight[...])
+            stream.open_sum()
+            stream.partial(1, output)
+            stream.partial(0, output)
+
+        def settle(tag, stage, source, kept, resid, full):
+            stream = streams[tag]
+            stream.settle(gathered=stage > 0)
+            gain = get("gains", tag)[stage : stage + 1]
+            shift = get("shifts", tag)[stage : stage + 1]
+            base = stream.core * stream.rows
+
+            def step(rows, carry):
+                values = source[rows].astype(F32) + stream.piece(rows)
+                kept[rows] = values
+                normed = norm_chunk(values, gain, shift)
+                resid[rows] = normed
+                at_offset(full, base, rows)[...] = normed.astype(BF)
+                return carry
+
+            chunks(stream.rows, step, 0)
+            bench.flush({"zero": "zero_", "mid": "mid_"}["zero" if stage == 0 else "mid"] + tag)
+            stream.gather(full)
+
+        for tag in streams:
+            settle(tag, 0, get("x", tag), get("zero", tag), get("first", tag), get("mlp", tag))
+
+        def feeds(tag):
+            stream = streams[tag]
+            full, up, down = get("mlp", tag), get("up", tag), get("down", tag)
+            act, slope = get("act", tag), get("slope", tag)
+
+            def project(half, core):
+                place = stream.place(half, core)
+                pre = product(full[place], up[...])
+                cube = GELU_A * (pre + GELU_B * pre * pre * pre)
+                bent = jnp.tanh(cube)
+                act[place] = (0.5 * pre * (1.0 + bent)).astype(BF)
+                slope[place] = (
+                    0.5 * (1.0 + bent)
+                    + 0.5 * pre * (1.0 - bent * bent) * GELU_A * (1.0 + 3.0 * GELU_B * pre * pre)
+                ).astype(BF)
+
+            def output(half, core):
+                return product(act[stream.place(half, core)], down[...])
+
+            return project, output
+
+        def layer(work):
+            for half in (0, 1):
+                for tag, stream in streams.items():
+                    hooks = work[tag]
+                    if half == 0:
+                        stream.open_sum()
+                    stream.arrive(half, hooks[0])
+                    if len(hooks) > 2:
+                        hooks[2](half)
+                    stream.partial(half, hooks[1])
+
+        layer({tag: feeds(tag) for tag in streams})
+        for tag in streams:
+            settle(tag, 1, get("first", tag), get("mid", tag), get("first", tag), get("self", tag))
+            bench.flush("mlp_" + tag, "act_" + tag, "slope_" + tag)
+
+        def attends(tag):
+            stream = streams[tag]
+            full, qkv, out = get("self", tag), get("qkv", tag), get("so", tag)
+            parts, share, context = get("parts", tag), get("share", tag), get("ctx2", tag)
+
+            def output(half, core):
+                return product(context[stream.place(half, core)], out[...])
+
+            if tag == "t":
+
+                def project(half, core):
+                    place = stream.place(half, core)
+                    parts[place] = product(full[place], qkv[...]).astype(BF)
+                    quad = 2 * half + core
+                    attend_many(
+                        parts, share, context, quad * n_t, quad * (n_t // ROW_LEN),
+                        n_t // ROW_LEN, text_local,
+                        functools.partial(self_mask_text, bench.lengths),
+                    )
+
+                return project, output
+
+            def project_image(half, core):
+                place = stream.place(half, core)
+                parts[place] = product(full[place], qkv[...]).astype(BF)
+
+            def middle(half):
+                blocks = 2 * n_i // ROW_LEN
+                attend_many(
+                    parts, share, context, 2 * half * n_i, half * blocks, blocks, image_local,
+                    functools.partial(self_mask_image, bench.regions),
+                )
+
+            return project_image, output, middle
+
+        layer({tag: attends(tag) for tag in streams})
+        for tag, stream in streams.items():
+            stream.settle()
+            bench.flush("self_" + tag, "parts_" + tag, "share_" + tag, "ctx2_" + tag)
+            gain, shift = get("gains", tag)[2:3], get("shifts", tag)[2:3]
+            second, result, late, grad = (
+                get("first", tag), get("result", tag), get("late", tag), get("g", tag)
+            )
+            width = second.shape[1]
+
+            def step(rows, carry):
+                values = second[rows] + stream.piece(rows)
+                back, normed, gains, shifts = norm_pull(values, gain, shift, grad[rows].astype(F32))
+                result[rows] = normed.astype(BF)
+                late[rows] = back
+                return carry[0] + gains, carry[1] + shifts
+
+            start = jnp.zeros((8, width), F32)
+            gains, shifts = chunks(stream.rows, step, (start, start))
+            get("gain", tag)[...] = gains
+            get("shift", tag)[...] = shifts
+            bench.flush("result_" + tag, "late_" + tag)
+
+    return exchange_kernel(
+        body, "forward_tail", 1, lambda: list(group_peers()[1:]), inputs, outputs, scratch, 32,
+        (15e9, 40e6, 1e6),
+    )
+
+
+def norm_pull(values, gain, shift, gradient):
+    centre = values - jnp.mean(values, axis=-1, keepdims=True)
+    spread = jnp.mean(centre * centre, axis=-1, keepdims=True)
+    inverse = lax.rsqrt(spread + epsilon)
+    unit = centre * inverse
+    scaled = gradient * gain
+    back = inverse * (
+        scaled
+        - jnp.mean(scaled, axis=-1, keepdims=True)
+        - unit * jnp.mean(scaled * unit, axis=-1, keepdims=True)
+    )
+    return back, unit * gain + shift, folded(gradient * unit), folded(gradient)
+
+
 def swap(values, axis, flip):
     return lax.ppermute(values, axis, [(i, i ^ flip) for i in range(lax.axis_size(axis))])
 
@@ -539,55 +970,27 @@
     text_ctx, image_ctx, text_share, image_share = co_forward(
         text_co, image_co, order, regions, lengths, co_local
     )
-    text_zero = text_in.astype(F32) + scatter_sum(
-        *[product(rows, co_text_out) for rows in halves(text_ctx)], core
-    )
-    image_zero = image_in.astype(F32) + scatter_sum(
-        *[product(rows, co_image_out) for rows in halves(image_ctx)], core
-    )
-    text_first = layer_norm(text_zero, text_gains[0], text_shifts[0])
-    image_first = layer_norm(image_zero, image_gains[0], image_shifts[0])
-
-    text_mlp_in = gather(text_first.astype(BF), core)
-    image_mlp_in = gather(image_first.astype(BF), core)
-    text_pre = product(text_mlp_in, text_up)
-    image_pre = product(image_mlp_in, image_up)
-    text_act = gelu_tanh(text_pre).astype(BF)
-    image_act = gelu_tanh(image_pre).astype(BF)
-    text_mid = text_first + scatter_sum(
-        *[product(rows, text_down) for rows in halves(text_act)], core
-    )
-    image_mid = image_first + scatter_sum(
-        *[product(rows, image_down) for rows in halves(image_act)], core
-    )
-    text_second = layer_norm(text_mid, text_gains[1], text_shifts[1])
-    image_second = layer_norm(image_mid, image_gains[1], image_shifts[1])
-
-    text_self_in = gather(text_second.astype(BF), core)
-    image_self_in = gather(image_second.astype(BF), core)
-    text_parts = product(text_self_in, w_self_text).astype(BF)
-    image_parts = product(image_self_in, w_self_image).astype(BF)
-    text_self_ctx, text_self_share = self_forward(
-        text_parts, lengths, text_local, 3, self_mask_text
-    )
-    image_self_ctx, image_self_share = self_forward(
-        image_parts, regions, image_local, 2, self_mask_image
-    )
-    text_last = text_second + scatter_sum(
-        *[product(rows, text_self_out) for rows in halves(text_self_ctx)], core
-    )
-    image_last = image_second + scatter_sum(
-        *[product(rows, image_self_out) for rows in halves(image_self_ctx)], core
-    )
-    text_result = layer_norm(text_last, text_gains[2], text_shifts[2]).astype(BF)
-    image_result = layer_norm(image_last, image_gains[2], image_shifts[2]).astype(BF)
-
-    text_late_grad, text_gain_c, text_shift_c = norm_back(
-        text_last, text_gains[2], text_grad_out.astype(F32)
-    )
-    image_late_grad, image_gain_c, image_shift_c = norm_back(
-        image_last, image_gains[2], image_grad_out.astype(F32)
-    )
+    ahead = forward_kernel(
+        text_ctx, image_ctx, text_in, image_in,
+        (co_text_out, co_image_out, text_up, text_down, image_up, image_down,
+         w_self_text, text_self_out, w_self_image, image_self_out),
+        (text_gains, text_shifts, image_gains, image_shifts),
+        text_grad_out, image_grad_out, lengths, regions, text_local, image_local,
+    )
+    text_result, image_result = ahead["result_t"], ahead["result_i"]
+    text_zero, image_zero = ahead["zero_t"], ahead["zero_i"]
+    text_mid, image_mid = ahead["mid_t"], ahead["mid_i"]
+    text_mlp_in, image_mlp_in = ahead["mlp_t"], ahead["mlp_i"]
+    text_act, image_act = ahead["act_t"], ahead["act_i"]
+    text_slope, image_slope = ahead["slope_t"], ahead["slope_i"]
+    text_self_in, image_self_in = ahead["self_t"], ahead["self_i"]
+    text_parts, image_parts = ahead["parts_t"], ahead["parts_i"]
+    text_self_share, image_self_share = ahead["share_t"], ahead["share_i"]
+    text_self_ctx, image_self_ctx = ahead["ctx2_t"], ahead["ctx2_i"]
+    text_late_grad, image_late_grad = ahead["late_t"], ahead["late_i"]
+    text_gain_c, text_shift_c = [jnp.sum(ahead[key], axis=0) for key in ("gain_t", "shift_t")]
+    image_gain_c, image_shift_c = [jnp.sum(ahead[key], axis=0) for key in ("gain_i", "shift_i")]
+
     text_late_all = gather(text_late_grad.astype(BF), core)
     image_late_all = gather(image_late_grad.astype(BF), core)
     text_parts_grad = self_backward(
@@ -627,8 +1030,8 @@
 
     text_mlp_all = gather(text_mid_grad.astype(BF), core)
     image_mlp_all = gather(image_mid_grad.astype(BF), core)
-    text_pre_grad = (product_nt(text_mlp_all, text_down) * gelu_slope(text_pre)).astype(BF)
-    image_pre_grad = (product_nt(image_mlp_all, image_down) * gelu_slope(image_pre)).astype(BF)
+    text_pre_grad = (product_nt(text_mlp_all, text_down) * text_slope.astype(F32)).astype(BF)
+    image_pre_grad = (product_nt(image_mlp_all, image_down) * image_slope.astype(F32)).astype(BF)
     text_back_mlp = scatter_sum(
         *[product_nt(rows, text_up) for rows in halves(text_pre_grad)], core
     )

time: 556 us -> 527 us (0.948)
  Pallas kernels: 51.6 us -> 152 us
  waiting for transfers between devices: 208 us -> 116 us
  starting transfers between devices: 51.5 us -> 32.9 us
  matrix products: 67 us -> 48.5 us
    pallas_call x2 -> x1, Pallas kernels: 18 us -> 118 us  [exchange_kernel(): pl.pallas_call(kernel, in_specs=[pl.BlockSpec(memory_space=spaces[kind])...]
    ppermute x82 -> x52, waiting for transfers between devices: 208 us -> 116 us  [swap(): lax.ppermute(values, axis, [(i, i ^ flip) for i in range(lax.axis_size(ax...]
    ppermute x82 -> x52, starting transfers between devices: 51.4 us -> 32.6 us  [swap(): lax.ppermute(values, axis, [(i, i ^ flip) for i in range(lax.axis_size(ax...]
    dot_general x18 -> x2, matrix products: 22 us -> 4.97 us  [product(): return jnp.dot(former, latter, preferred_element_type=F32)]
    unnamed x460 -> x268, local copies, waits for them, and re-layouts: 53.1 us -> 41.3 us
    reduce_sum x12, other arithmetic: 5.82 us -> 12.2 us  [the longest x4 5.39 us: per_device(): jnp.sum(ahead[key], axis=0)]
    another operation x8, local copies, waits for them, and re-layouts: 1.27 us -> 7.02 us  [norm_columns(): stacked = jnp.stack(vectors)]
  transfers between devices with their start and end apart: 84 -> 54, of which waited for: 26 -> 15; matrix products, arithmetic and copies ran while one was open for 35% -> 34% of each run, Pallas kernels for 8% -> 5%
where the time goes in v2:
time: 527 us; the launch traced here: 518 us
  Pallas kernels  152 us (29%)
  waiting for transfers between devices  116 us (22%)
  other arithmetic  84.5 us (16%)
  local copies, waits for them, and re-layouts  68.3 us (13%)
  matrix products  48.5 us (9%)
  starting transfers between devices  32.9 us (6%)
  between operations  16.2 us (3%)
    pallas_call x1, Pallas kernels, exchange_kernel(): pl.pallas_call(kernel, in_specs=[pl.BlockSpec(memory_space=spaces[kind])...  118 us
    ppermute x52, waiting for transfers between devices, swap(): lax.ppermute(values, axis, [(i, i ^ flip) for i in range(lax.axis_size(ax...  116 us
    unnamed x268, local copies, waits for them, and re-layouts  41.3 us
    ppermute x52, starting transfers between devices, swap(): lax.ppermute(values, axis, [(i, i ^ flip) for i in range(lax.axis_size(ax...  32.6 us
    dot_general x18, matrix products, product_nt(): lax.dot_general(former, latter, (((1,), (1,)), ((), ())), preferred_eleme...  23.5 us
    dot_general x12, matrix products, product_tn(): lax.dot_general(former, latter, (((0,), (0,)), ((), ())), preferred_eleme...  20 us
    pallas_call x2, Pallas kernels, self_backward(): pl.pallas_call(functools.partial(self_backward_kernel, heads, per_step),...  16.3 us
    pallas_call x1, Pallas kernels, co_backward(): pl.pallas_call(functools.partial(co_backward_kernel, heads, per_step), gr...  11.8 us
  transfers between devices with their start and end apart: 54, of which 15 were waited for; matrix products, arithmetic and copies ran while one was open for 34% of the time, Pallas kernels for 5%

profile of v2, /device:TPU:0, one launch (start us, length us, event | category | flops | bytes accessed | tf_op | source)
XLA Modules:
  0.0 518.2 jit_solution(8672237821833515272)
XLA Ops:
  7.8 2.6 collective-permute-start.4
  15.9 2.4 copy.154.refs_18_
  26.7 6.3 %collective-permute-done.1 = bf16[384,768]{1,0:T(8,128)(2,1)} collective-permute-done((bf16[384,768]{1,0:T(8,128)(2,1)}, bf16[384,768]{1,0:T(8,128)(2,1)}, u32[]{:S(2)}, u32[]{:S(2)}) %collective-permute-start.1) | collective-permute-done | bytes 589856 | tf_op jit(solution)/shard_map/ppermute | solution.py:823
  38.5 3.5 convolution_convert_fusion.text_ref
  42.1 5.6 %co_forward.1 = (bf16[1536,256]{1,0:T(8,128)(2,1)S(1)}, bf16[768,256]{1,0:T(8,128)(2,1)S(1)}, bf16[6,2,256,128]{3,2,1,0:T(8,128)(2,1)S(1)}, bf16[6,2,128,256]{3,2,1,0:T(8,128)(2,1)S(1)}) custom-call(s32[24]{0:T(128)S(1)} %get-tuple-element.281.order_ref, s32[24]{0:T(128)S(1)} %get-tuple-element.282.region_ref.refs_1_, ...), custom_call_target="tpu_custom_call" | custom-call | flops 402653184 | bytes 8000000 | tf_op jit(solution)/shard_map/co_forward/pallas_call | solution.py:277
  51.1 118.3 %forward_tail.1 = (f32[384,768]{1,0:T(8,128)}, f32[384,768]{1,0:T(8,128)}, bf16[1536,768]{1,0:T(8,128)(2,1)}, bf16[1536,768]{1,0:T(8,128)(2,1)}, bf16[1536,768]{...) custom-call(s32[24]{0:T(128)} %copy-done.11, ...), custom_call_target="tpu_custom_call" | custom-call | flops 15000000512 | bytes 40000000 | tf_op jit(solution)/shard_map/forward_tail/pallas_call | solution.py:478
  172.3 2.1 convert_element_type.295
  202.3 4.3 self_backward.3
  223.6 12.0 %self_backward.2 = bf16[1536,576]{1,0:T(8,128)(2,1)S(1)} custom-call(bf16[1536,576]{1,0:T(8,128)(2,1)S(1)} %copy-done, bf16[12,3,128,128]{3,2,1,0:T(8,128)(2,1)S(1)} %copy-done.4, bf16[1536,192]{1,0:T(8,128)(2,1)S(1)} %copy.155.grad_ref), custom_call_target="tpu_custom_call" | custom-call | flops 377487360 | bytes 9000000 | tf_op jit(solution)/shard_map/self_backward/pallas_call | solution.py:375
  235.6 2.5 fusion.15
  244.2 2.4 fusion.17
  246.7 2.4 add_convert_fusion.5
  260.7 2.4 multiply_reduce_fusion.8
  271.3 5.5 %collective-permute-done.28 = bf16[192,1024]{1,0:T(8,128)(2,1)} collective-permute-done((bf16[192,1024]{1,0:T(8,128)(2,1)}, bf16[192,1024]{1,0:T(8,128)(2,1)}, u32[]{:S(2)}, u32[]{:S(2)}) %collective-permute-start.28) | collective-permute-done | bytes 393248 | tf_op jit(solution)/shard_map/ppermute | solution.py:823
  278.0 9.9 %collective-permute-done.11 = bf16[384,768]{1,0:T(8,128)(2,1)} collective-permute-done((bf16[384,768]{1,0:T(8,128)(2,1)}, bf16[384,768]{1,0:T(8,128)(2,1)}, u32[]{:S(2)}, u32[]{:S(2)}) %collective-permute-start.11) | collective-permute-done | bytes 589856 | tf_op jit(solution)/shard_map/ppermute | solution.py:823
  287.9 2.9 multiply_reduce_fusion
  302.3 5.4 %collective-permute-done.13 = bf16[384,768]{1,0:T(8,128)(2,1)} collective-permute-done((bf16[384,768]{1,0:T(8,128)(2,1)S(1)}, bf16[384,768]{1,0:T(8,128)(2,1)}, u32[]{:S(2)}, u32[]{:S(2)}) %collective-permute-start.13) | collective-permute-done | bytes 589856 | tf_op jit(solution)/shard_map/ppermute | solution.py:823
  308.9 4.7 collective-permute-done.32
  318.8 2.4 fusion.57
  324.9 6.0 %multiply_convert_fusion = bf16[1536,768]{1,0:T(8,128)(2,1)S(1)} fusion(bf16[1536,768]{1,0:T(8,128)(2,1)} %get-tuple-element.61, bf16[768,768]{1,0:T(8,128)(2,1)S(1)} %copy-done.99, bf16[384,768]{1,0:T(8,128)(2,1)S(1)} %get-tuple-element.216, bf16[384,768]{1,0:T(8,128)(2,1)S(1)} %get-tuple-element.215, bf16[384,768]{1,0:T(8,128)(2,1)S(1)} %copy-done.61, ...), kind=kOutput, calls=%fused_computation | convolution fusion | flops 1824915456 | bytes 8257536 | tf_op jit(solution)/shard_map/dot_general | solution.py:32
  349.5 10.8 %collective-permute-done.17 = bf16[384,768]{1,0:T(8,128)(2,1)} collective-permute-done((bf16[384,768]{1,0:T(8,128)(2,1)}, bf16[384,768]{1,0:T(8,128)(2,1)}, u32[]{:S(2)}, u32[]{:S(2)}) %collective-permute-start.17) | collective-permute-done | bytes 589856 | tf_op jit(solution)/shard_map/ppermute | solution.py:823
  360.3 2.9 multiply_reduce_fusion.1
  371.6 2.7 convolution_convert_fusion.13
  375.5 4.5 collective-permute-done.19
  386.1 11.8 %co_backward.1 = (bf16[1536,768]{1,0:T(8,128)(2,1)}, bf16[768,768]{1,0:T(8,128)(2,1)S(1)}) custom-call(s32[24]{0:T(128)S(1)} %get-tuple-element.281.order_ref, bf16[1536,768]{1,0:T(8,128)(2,1)} %convolution_convert_fusion.text_ref, bf16[768,768]{1,0:T(8,128)(2,1)S(1)} %convolution_convert_fusion.5.image_ref, bf16[6,2,256,128]{3,2,1,0:T(8,128)(2,1)S(1)} %copy-done.6, ...), custom_call_target="tpu_custom_call" | custom-call | flops 805306368 | bytes 12000000 | tf_op jit(solution)/shard_map/co_backward/pallas_call | solution.py:317
  416.2 7.8 %collective-permute-done.41 = bf16[192,1024]{1,0:T(8,128)(2,1)S(1)} collective-permute-done((bf16[192,1024]{1,0:T(8,128)(2,1)S(1)}, bf16[192,1024]{1,0:T(8,128)(2,1)S(1)}, u32[]{:S(2)}, u32[]{:S(2)}) %collective-permute-start.41) | collective-permute-done | bytes 393248 | tf_op jit(solution)/shard_map/ppermute | solution.py:823
  425.2 11.8 %collective-permute-done.44 = bf16[2,2,480,256]{3,2,1,0:T(8,128)(2,1)S(1)} collective-permute-done((bf16[2,2,480,256]{3,2,1,0:T(8,128)(2,1)S(1)}, bf16[2,2,480,256]{3,2,1,0:T(8,128)(2,1)S(1)}, u32[]{:S(2)}, u32[]{:S(2)}) %collective-permute-start.44) | collective-permute-done | bytes 983072 | tf_op jit(solution)/shard_map/ppermute | solution.py:823
  440.4 14.5 %collective-permute-done.49 = bf16[2,2,640,256]{3,2,1,0:T(8,128)(2,1)S(1)} collective-permute-done((bf16[2,2,640,256]{3,2,1,0:T(8,128)(2,1)S(1)}, bf16[2,2,640,256]{3,2,1,0:T(8,128)(2,1)S(1)}, u32[]{:S(2)}, u32[]{:S(2)}) %collective-permute-start.49) | collective-permute-done | bytes 1310752 | tf_op jit(solution)/shard_map/ppermute | solution.py:823
  455.6 9.8 %collective-permute-done.45 = bf16[2,480,256]{2,1,0:T(8,128)(2,1)S(1)} collective-permute-done((bf16[2,480,256]{2,1,0:T(8,128)(2,1)S(1)}, bf16[2,480,256]{2,1,0:T(8,128)(2,1)S(1)}, u32[]{:S(2)}, u32[]{:S(2)}) %collective-permute-start.45) | collective-permute-done | bytes 491552 | tf_op jit(solution)/shard_map/ppermute | solution.py:823
  465.6 2.5 collective-permute-start.46
  469.7 9.5 %collective-permute-done.46 = bf16[480,256]{1,0:T(8,128)(2,1)S(1)} collective-permute-done((bf16[480,256]{1,0:T(8,128)(2,1)S(1)}, bf16[480,256]{1,0:T(8,128)(2,1)S(1)}, u32[]{:S(2)}, u32[]{:S(2)}) %collective-permute-start.46) | collective-permute-done | bytes 245792 | tf_op jit(solution)/shard_map/ppermute | solution.py:823
  488.1 13.5 %collective-permute-done.51 = bf16[640,256]{1,0:T(8,128)(2,1)S(1)} collective-permute-done((bf16[640,256]{1,0:T(8,128)(2,1)S(1)}, bf16[640,256]{1,0:T(8,128)(2,1)S(1)}, u32[]{:S(2)}, u32[]{:S(2)}) %collective-permute-start.51) | collective-permute-done | bytes 327712 | tf_op jit(solution)/shard_map/ppermute | solution.py:823
  (530 shorter events, 196.5 us)
Async XLA Ops:
  7.2 474.9 %reduce-scatter.5.cloned.1.call-start = ((), (), s32[]{:S(2)}) async-start(), calls=%async_computation.3 | async-start | bytes 3686400 | tf_op jit(solution)/shard_map/reduce_scatter | solution.py:886
  7.2 18.4 %collective-permute-start.3 = (bf16[192,1024]{1,0:T(8,128)(2,1)}, bf16[192,1024]{1,0:T(8,128)(2,1)}, u32[]{:S(2)}, u32[]{:S(2)}) collective-permute-start(bf16[192,1024]{1,0:T(8,128)(2,1)} %refs_10_.1), channel_id=1, source_target_pairs={{0,1},{1,0},{2,3},{3,2},{4,5},{5,4},{6,7},{7,6},{8,9},{9,8},{10,11... | collective-permute-start | bytes 1179656 | tf_op jit(solution)/shard_map/ppermute | solution.py:823
  7.8 17.8 %collective-permute-start.4 = (bf16[192,1024]{1,0:T(8,128)(2,1)}, bf16[192,1024]{1,0:T(8,128)(2,1)}, u32[]{:S(2)}, u32[]{:S(2)}) collective-permute-start(bf16[192,1024]{1,0:T(8,128)(2,1)} %refs_10_.1), channel_id=1, source_target_pairs={{0,2},{1,3},{2,0},{3,1},{4,6},{5,7},{6,4},{7,5},{8,10},{9,11},{10,... | collective-permute-start | bytes 1179656 | tf_op jit(solution)/shard_map/ppermute | solution.py:823
  10.4 22.7 %collective-permute-start = (bf16[384,768]{1,0:T(8,128)(2,1)}, bf16[384,768]{1,0:T(8,128)(2,1)}, u32[]{:S(2)}, u32[]{:S(2)}) collective-permute-start(bf16[384,768]{1,0:T(8,128)(2,1)} %refs_11_.1), channel_id=1, source_target_pairs={{0,1},{1,0},{2,3},{3,2},{4,5},{5,4},{6,7},{7,6},{8,9},{9,8},{10,11... | collective-permute-start | bytes 1769480 | tf_op jit(solution)/shard_map/ppermute | solution.py:823
  10.5 22.5 %collective-permute-start.1 = (bf16[384,768]{1,0:T(8,128)(2,1)}, bf16[384,768]{1,0:T(8,128)(2,1)}, u32[]{:S(2)}, u32[]{:S(2)}) collective-permute-start(bf16[384,768]{1,0:T(8,128)(2,1)} %refs_11_.1), channel_id=1, source_target_pairs={{0,2},{1,3},{2,0},{3,1},{4,6},{5,7},{6,4},{7,5},{8,10},{9,11},{10,... | collective-permute-start | bytes 1769480 | tf_op jit(solution)/shard_map/ppermute | solution.py:823
  171.4 25.4 %collective-permute-start.22 = (bf16[192,1024]{1,0:T(8,128)(2,1)}, bf16[192,1024]{1,0:T(8,128)(2,1)}, u32[]{:S(2)}, u32[]{:S(2)}) collective-permute-start(bf16[192,1024]{1,0:T(8,128)(2,1)} %convert_element_type.314), channel_id=1, source_target_pairs={{0,2},{1,3},{2,0},{3,1},{4,6},{5,7},{6,4},{7,5},{8,10},{9,11},{10,... | collective-permute-start | bytes 1179656 | tf_op jit(solution)/shard_map/ppermute | solution.py:823
  172.3 24.8 %collective-permute-start.21 = (bf16[192,1024]{1,0:T(8,128)(2,1)}, bf16[192,1024]{1,0:T(8,128)(2,1)}, u32[]{:S(2)}, u32[]{:S(2)}) collective-permute-start(bf16[192,1024]{1,0:T(8,128)(2,1)} %convert_element_type.314), channel_id=1, source_target_pairs={{0,1},{1,0},{2,3},{3,2},{4,5},{5,4},{6,7},{7,6},{8,9},{9,8},{10,11... | collective-permute-start | bytes 1179656 | tf_op jit(solution)/shard_map/ppermute | solution.py:823
  174.4 24.0 %collective-permute-start.7 = (bf16[384,768]{1,0:T(8,128)(2,1)}, bf16[384,768]{1,0:T(8,128)(2,1)}, u32[]{:S(2)}, u32[]{:S(2)}) collective-permute-start(bf16[384,768]{1,0:T(8,128)(2,1)} %convert_element_type.295), channel_id=1, source_target_pairs={{0,2},{1,3},{2,0},{3,1},{4,6},{5,7},{6,4},{7,5},{8,10},{9,11},{10,... | collective-permute-start | bytes 1769480 | tf_op jit(solution)/shard_map/ppermute | solution.py:823
  175.6 23.2 %collective-permute-start.6 = (bf16[384,768]{1,0:T(8,128)(2,1)}, bf16[384,768]{1,0:T(8,128)(2,1)}, u32[]{:S(2)}, u32[]{:S(2)}) collective-permute-start(bf16[384,768]{1,0:T(8,128)(2,1)} %convert_element_type.295), channel_id=1, source_target_pairs={{0,1},{1,0},{2,3},{3,2},{4,5},{5,4},{6,7},{7,6},{8,9},{9,8},{10,11... | collective-permute-start | bytes 1769480 | tf_op jit(solution)/shard_map/ppermute | solution.py:823
  198.4 17.8 %collective-permute-start.8 = (bf16[384,768]{1,0:T(8,128)(2,1)}, bf16[384,768]{1,0:T(8,128)(2,1)S(1)}, u32[]{:S(2)}, u32[]{:S(2)}) collective-permute-start(bf16[384,768]{1,0:T(8,128)(2,1)} %collective-permute-done.7), channel_id=1, source_target_pairs={{0,1},{1,0},{2,3},{3,2},{4,5},{5,4},{6,7},{7,6},{8,9},{9,8},{10,11... | collective-permute-start | bytes 1769480 | tf_op jit(solution)/shard_map/ppermute | solution.py:823
  213.1 33.5 %collective-permute-start.25 = (bf16[192,1024]{1,0:T(8,128)(2,1)}, bf16[192,1024]{1,0:T(8,128)(2,1)}, u32[]{:S(2)}, u32[]{:S(2)}) collective-permute-start(bf16[192,1024]{1,0:T(8,128)(2,1)} %select_convert_fusion.10), channel_id=1, source_target_pairs={{0,1},{1,0},{2,3},{3,2},{4,5},{5,4},{6,7},{7,6},{8,9},{9,8},{10,11... | collective-permute-start | bytes 1179656 | tf_op jit(solution)/shard_map/ppermute | solution.py:823
  213.4 46.2 %collective-permute-start.24 = (bf16[192,1024]{1,0:T(8,128)(2,1)}, bf16[192,1024]{1,0:T(8,128)(2,1)}, u32[]{:S(2)}, u32[]{:S(2)}) collective-permute-start(bf16[192,1024]{1,0:T(8,128)(2,1)} %select_convert_fusion.11), channel_id=1, source_target_pairs={{0,1},{1,0},{2,3},{3,2},{4,5},{5,4},{6,7},{7,6},{8,9},{9,8},{10,11... | collective-permute-start | bytes 1179656 | tf_op jit(solution)/shard_map/ppermute | solution.py:823
  251.9 26.1 %collective-permute-start.9 = (bf16[384,768]{1,0:T(8,128)(2,1)}, bf16[384,768]{1,0:T(8,128)(2,1)}, u32[]{:S(2)}, u32[]{:S(2)}) collective-permute-start(bf16[384,768]{1,0:T(8,128)(2,1)} %select_convert_fusion.5), channel_id=1, source_target_pairs={{0,1},{1,0},{2,3},{3,2},{4,5},{5,4},{6,7},{7,6},{8,9},{9,8},{10,11... | collective-permute-start | bytes 1769480 | tf_op jit(solution)/shard_map/ppermute | solution.py:823
  267.4 20.5 %collective-permute-start.11 = (bf16[384,768]{1,0:T(8,128)(2,1)}, bf16[384,768]{1,0:T(8,128)(2,1)}, u32[]{:S(2)}, u32[]{:S(2)}) collective-permute-start(bf16[384,768]{1,0:T(8,128)(2,1)} %add_convert_fusion.2), channel_id=1, source_target_pairs={{0,2},{1,3},{2,0},{3,1},{4,6},{5,7},{6,4},{7,5},{8,10},{9,11},{10,... | collective-permute-start | bytes 1769480 | tf_op jit(solution)/shard_map/ppermute | solution.py:823
  271.1 233.6 %reduce-scatter.3.cloned.1.call-start = ((), (), s32[]{:S(2)}) async-start(), calls=%async_computation.2 | async-start | bytes 3833856 | tf_op jit(solution)/shard_map/reduce_scatter | solution.py:886
  276.8 15.5 %collective-permute-start.29 = (bf16[192,1024]{1,0:T(8,128)(2,1)}, bf16[192,1024]{1,0:T(8,128)(2,1)S(1)}, u32[]{:S(2)}, u32[]{:S(2)}) collective-permute-start(bf16[192,1024]{1,0:T(8,128)(2,1)} %collective-permute-done.28), channel_id=1, source_target_pairs={{0,1},{1,0},{2,3},{3,2},{4,5},{5,4},{6,7},{7,6},{8,9},{9,8},{10,11... | collective-permute-start | bytes 1179656 | tf_op jit(solution)/shard_map/ppermute | solution.py:823
  291.3 16.4 %collective-permute-start.13 = (bf16[384,768]{1,0:T(8,128)(2,1)S(1)}, bf16[384,768]{1,0:T(8,128)(2,1)}, u32[]{:S(2)}, u32[]{:S(2)}) collective-permute-start(bf16[384,768]{1,0:T(8,128)(2,1)S(1)} %get-tuple-element.191), channel_id=1, source_target_pairs={{0,2},{1,3},{2,0},{3,1},{4,6},{5,7},{6,4},{7,5},{8,10},{9,11},{10,... | collective-permute-start | bytes 1769480 | tf_op jit(solution)/shard_map/ppermute | solution.py:823
  292.2 15.5 %collective-permute-start.12 = (bf16[384,768]{1,0:T(8,128)(2,1)S(1)}, bf16[384,768]{1,0:T(8,128)(2,1)S(1)}, u32[]{:S(2)}, u32[]{:S(2)}) collective-permute-start(bf16[384,768]{1,0:T(8,128)(2,1)S(1)} %get-tuple-element.191), channel_id=1, source_target_pairs={{0,1},{1,0},{2,3},{3,2},{4,5},{5,4},{6,7},{7,6},{8,9},{9,8},{10,11... | collective-permute-start | bytes 1769480 | tf_op jit(solution)/shard_map/ppermute | solution.py:823
  298.4 15.1 %collective-permute-start.32 = (bf16[192,1024]{1,0:T(8,128)(2,1)S(1)}, bf16[192,1024]{1,0:T(8,128)(2,1)S(1)}, u32[]{:S(2)}, u32[]{:S(2)}) collective-permute-start(bf16[192,1024]{1,0:T(8,128)(2,1)S(1)} %add_convert_fusion.4), channel_id=1, source_target_pairs={{0,2},{1,3},{2,0},{3,1},{4,6},{5,7},{6,4},{7,5},{8,10},{9,11},{10,... | collective-permute-start | bytes 1179656 | tf_op jit(solution)/shard_map/ppermute | solution.py:823
  307.7 15.8 %collective-permute-start.14 = (bf16[384,768]{1,0:T(8,128)(2,1)}, bf16[384,768]{1,0:T(8,128)(2,1)}, u32[]{:S(2)}, u32[]{:S(2)}) collective-permute-start(bf16[384,768]{1,0:T(8,128)(2,1)} %collective-permute-done.13), channel_id=1, source_target_pairs={{0,1},{1,0},{2,3},{3,2},{4,5},{5,4},{6,7},{7,6},{8,9},{9,8},{10,11... | collective-permute-start | bytes 1769480 | tf_op jit(solution)/shard_map/ppermute | solution.py:823
  321.2 28.0 %collective-permute-start.34 = (bf16[192,1024]{1,0:T(8,128)(2,1)}, bf16[192,1024]{1,0:T(8,128)(2,1)}, u32[]{:S(2)}, u32[]{:S(2)}) collective-permute-start(bf16[192,1024]{1,0:T(8,128)(2,1)} %get-tuple-element.182), channel_id=1, source_target_pairs={{0,2},{1,3},{2,0},{3,1},{4,6},{5,7},{6,4},{7,5},{8,10},{9,11},{10,... | collective-permute-start | bytes 1179656 | tf_op jit(solution)/shard_map/ppermute | solution.py:823
  322.3 43.1 %collective-permute-start.33 = (bf16[192,1024]{1,0:T(8,128)(2,1)}, bf16[192,1024]{1,0:T(8,128)(2,1)}, u32[]{:S(2)}, u32[]{:S(2)}) collective-permute-start(bf16[192,1024]{1,0:T(8,128)(2,1)} %get-tuple-element.182), channel_id=1, source_target_pairs={{0,1},{1,0},{2,3},{3,2},{4,5},{5,4},{6,7},{7,6},{8,9},{9,8},{10,11... | collective-permute-start | bytes 1179656 | tf_op jit(solution)/shard_map/ppermute | solution.py:823
  344.3 16.1 %collective-permute-start.17 = (bf16[384,768]{1,0:T(8,128)(2,1)}, bf16[384,768]{1,0:T(8,128)(2,1)}, u32[]{:S(2)}, u32[]{:S(2)}) collective-permute-start(bf16[384,768]{1,0:T(8,128)(2,1)} %add_convert_fusion.1), channel_id=1, source_target_pairs={{0,2},{1,3},{2,0},{3,1},{4,6},{5,7},{6,4},{7,5},{8,10},{9,11},{10,... | collective-permute-start | bytes 1769480 | tf_op jit(solution)/shard_map/ppermute | solution.py:823
  349.3 17.3 %collective-permute-start.35 = (bf16[192,1024]{1,0:T(8,128)(2,1)}, bf16[192,1024]{1,0:T(8,128)(2,1)S(1)}, u32[]{:S(2)}, u32[]{:S(2)}) collective-permute-start(bf16[192,1024]{1,0:T(8,128)(2,1)} %collective-permute-done.34), channel_id=1, source_target_pairs={{0,1},{1,0},{2,3},{3,2},{4,5},{5,4},{6,7},{7,6},{8,9},{9,8},{10,11... | collective-permute-start | bytes 1179656 | tf_op jit(solution)/shard_map/ppermute | solution.py:823
  364.4 15.6 %collective-permute-start.19 = (bf16[384,768]{1,0:T(8,128)(2,1)}, bf16[384,768]{1,0:T(8,128)(2,1)}, u32[]{:S(2)}, u32[]{:S(2)}) collective-permute-start(bf16[384,768]{1,0:T(8,128)(2,1)} %get-tuple-element.188), channel_id=1, source_target_pairs={{0,2},{1,3},{2,0},{3,1},{4,6},{5,7},{6,4},{7,5},{8,10},{9,11},{10,... | collective-permute-start | bytes 1769480 | tf_op jit(solution)/shard_map/ppermute | solution.py:823
  408.3 28.7 %collective-permute-start.44 = (bf16[2,2,480,256]{3,2,1,0:T(8,128)(2,1)S(1)}, bf16[2,2,480,256]{3,2,1,0:T(8,128)(2,1)S(1)}, u32[]{:S(2)}, u32[]{:S(2)}) collective-permute-start(bf16[2,2,480,256]{3,2,1,0:T(8,128)(2,1)S(1)} %fusion.14), channel_id=1, source_target_pairs={{0,4},{4,0},{8,12},{12,8},{16,20},{20,16},{24,28},{28,24},{1,5},{5... | collective-permute-start | bytes 2949128 | tf_op jit(solution)/shard_map/ppermute | solution.py:823
  410.3 28.8 %collective-permute-start.36 = (bf16[384,768]{1,0:T(8,128)(2,1)S(1)}, bf16[384,768]{1,0:T(8,128)(2,1)S(1)}, u32[]{:S(2)}, u32[]{:S(2)}) collective-permute-start(bf16[384,768]{1,0:T(8,128)(2,1)S(1)} %select_convert_fusion.1), channel_id=1, source_target_pairs={{0,1},{1,0},{2,3},{3,2},{4,5},{5,4},{6,7},{7,6},{8,9},{9,8},{10,11... | collective-permute-start | bytes 1769480 | tf_op jit(solution)/shard_map/ppermute | solution.py:823
  413.0 42.0 %collective-permute-start.49 = (bf16[2,2,640,256]{3,2,1,0:T(8,128)(2,1)S(1)}, bf16[2,2,640,256]{3,2,1,0:T(8,128)(2,1)S(1)}, u32[]{:S(2)}, u32[]{:S(2)}) collective-permute-start(bf16[2,2,640,256]{3,2,1,0:T(8,128)(2,1)S(1)} %fusion.2), channel_id=1, source_target_pairs={{0,8},{4,12},{8,0},{12,4},{16,24},{20,28},{24,16},{28,20},{1,9},{5... | collective-permute-start | bytes 3932168 | tf_op jit(solution)/shard_map/ppermute | solution.py:823
  414.9 24.2 %collective-permute-start.38 = (bf16[384,768]{1,0:T(8,128)(2,1)S(1)}, bf16[384,768]{1,0:T(8,128)(2,1)S(1)}, u32[]{:S(2)}, u32[]{:S(2)}) collective-permute-start(bf16[384,768]{1,0:T(8,128)(2,1)S(1)} %add_convert_fusion), channel_id=1, source_target_pairs={{0,2},{1,3},{2,0},{3,1},{4,6},{5,7},{6,4},{7,5},{8,10},{9,11},{10,... | collective-permute-start | bytes 1769480 | tf_op jit(solution)/shard_map/ppermute | solution.py:823
  437.5 27.9 %collective-permute-start.45 = (bf16[2,480,256]{2,1,0:T(8,128)(2,1)S(1)}, bf16[2,480,256]{2,1,0:T(8,128)(2,1)S(1)}, u32[]{:S(2)}, u32[]{:S(2)}) collective-permute-start(bf16[2,480,256]{2,1,0:T(8,128)(2,1)S(1)} %fusion.32), channel_id=1, source_target_pairs={{0,8},{4,12},{8,0},{12,4},{16,24},{20,28},{24,16},{28,20},{1,9},{5... | collective-permute-start | bytes 1474568 | tf_op jit(solution)/shard_map/ppermute | solution.py:823
  468.1 16.5 %collective-permute-start.50 = (bf16[2,640,256]{2,1,0:T(8,128)(2,1)S(1)}, bf16[2,640,256]{2,1,0:T(8,128)(2,1)S(1)}, u32[]{:S(2)}, u32[]{:S(2)}) collective-permute-start(bf16[2,640,256]{2,1,0:T(8,128)(2,1)S(1)} %fusion.21), channel_id=1, source_target_pairs={{0,4},{4,0},{8,12},{12,8},{16,20},{20,16},{24,28},{28,24},{1,5},{5... | collective-permute-start | bytes 1966088 | tf_op jit(solution)/shard_map/ppermute | solution.py:823
  484.9 16.6 %collective-permute-start.51 = (bf16[640,256]{1,0:T(8,128)(2,1)S(1)}, bf16[640,256]{1,0:T(8,128)(2,1)S(1)}, u32[]{:S(2)}, u32[]{:S(2)}) collective-permute-start(bf16[640,256]{1,0:T(8,128)(2,1)S(1)} %select_bitcast_fusion), channel_id=1, source_target_pairs={{0,16},{4,20},{8,24},{12,28},{16,0},{20,4},{24,8},{28,12},{1,17},{... | collective-permute-start | bytes 983048 | tf_op jit(solution)/shard_map/ppermute | solution.py:823
  (137 other events, 792.1 us)
Sparse Core Ops, SparseCore 0:
  271.2 76.7 reduce-scatter.4
  352.0 84.2 reduce-scatter.2

commit v3 on v2

v3 whole, which is shorter than its diff:
```python
import functools

import jax
import jax.numpy as jnp
from jax import lax
from jax.experimental import pallas as pl
from jax.experimental.pallas import tpu as pltpu
from jax.sharding import PartitionSpec as P

CO_HEADS = 8
TEXT_HEADS = 12
IMAGE_HEADS = 8
CAP_LEN = 64
ROW_LEN = 128
PER_ROW = 4

epsilon = 1e-05
BF = jnp.bfloat16
F32 = jnp.float32
VMEM_LIMIT = 48 * 1024 * 1024


def product(former, latter):
    return jnp.dot(former, latter, preferred_element_type=F32)


def product_tn(former, latter):
    return lax.dot_general(former, latter, (((0,), (0,)), ((), ())), preferred_element_type=F32)


def product_nt(former, latter):
    return lax.dot_general(former, latter, (((1,), (1,)), ((), ())), preferred_element_type=F32)


def layer_norm(values, norm_gain, norm_shift):
    centre = values - jnp.mean(values, axis=-1, keepdims=True)
    spread = jnp.mean(centre * centre, axis=-1, keepdims=True)
    return centre * lax.rsqrt(spread + epsilon) * norm_gain + norm_shift


def norm_back(values, norm_gain, gradient):
    centre = values - jnp.mean(values, axis=-1, keepdims=True)
    spread = jnp.mean(centre * centre, axis=-1, keepdims=True)
    inverse = lax.rsqrt(spread + epsilon)
    unit = centre * inverse
    scaled = gradient * norm_gain
    back = inverse * (
        scaled
        - jnp.mean(scaled, axis=-1, keepdims=True)
        - unit * jnp.mean(scaled * unit, axis=-1, keepdims=True)
    )
    return back, jnp.sum(gradient * unit, axis=0), jnp.sum(gradient, axis=0)


GELU_A = 0.7978845608028654
GELU_B = 0.044715


def gelu_tanh(values):
    return 0.5 * values * (1.0 + jnp.tanh(GELU_A * (values + GELU_B * values * values * values)))


def gelu_slope(values):
    bent = jnp.tanh(GELU_A * (values + GELU_B * values * values * values))
    return 0.5 * (1.0 + bent) + 0.5 * values * (1.0 - bent * bent) * GELU_A * (
        1.0 + 3.0 * GELU_B * values * values
    )


def softmax_block(scores, mask):
    scores = jnp.where(mask, scores, -1000000000.0)
    exponent = jnp.exp(scores - jnp.max(scores, axis=-1, keepdims=True))
    return (exponent / jnp.sum(exponent, axis=-1, keepdims=True)).astype(BF)


def attend_back(shares, scaling, queries, keys, values, context_grad):
    wide = shares.astype(F32)
    share_grad = product_nt(context_grad, values)
    inner = jnp.sum(share_grad * wide, axis=-1, keepdims=True)
    score_grad = (wide * (share_grad - inner) * scaling).astype(BF)
    return (
        product(score_grad, keys).astype(BF),
        product_tn(score_grad, queries).astype(BF),
        product_tn(shares, context_grad).astype(BF),
    )


def row_ends(region_ref, row):
    ends = [region_ref[row * PER_ROW]]
    for slot in range(1, PER_ROW):
        ends.append(ends[-1] + region_ref[row * PER_ROW + slot])
    return ends


def slot_of(places, ends):
    slot = (places >= ends[0]).astype(jnp.int32)
    for end in ends[1:]:
        slot = slot + (places >= end).astype(jnp.int32)
    return slot


def caption_rows(ref, captions, start, width):
    return jnp.concatenate(
        [ref[caption, :, start : start + width] for caption in captions], axis=0
    )


def co_forward_rows(bench, heads, rows_total):
    text_ref, image_ref = bench.co_t, bench.co_i
    inner = image_ref.shape[1] // 3
    size = inner // heads
    scaling = size ** (-0.5)
    span = PER_ROW * CAP_LEN
    per_step = 2
    order_ref, length_ref = bench.order, bench.lengths
    text_shares, image_shares = bench.cshare_t, bench.cshare_i
    text_out, image_out = bench.rctx_t, bench.ctx_i

    def step(index, carry):
        for member in range(per_step):
            row = index * per_step + member
            captions = [order_ref[row * PER_ROW + slot] for slot in range(PER_ROW)]
            ends = row_ends(bench.regions, row)
            token_slot = lax.broadcasted_iota(jnp.int32, (span, ROW_LEN), 0) // CAP_LEN
            to_image = token_slot == slot_of(
                lax.broadcasted_iota(jnp.int32, (span, ROW_LEN), 1), ends
            )
            spots = lax.broadcasted_iota(jnp.int32, (ROW_LEN, span), 1)
            length = jnp.full((ROW_LEN, span), length_ref[captions[0]], jnp.int32)
            for slot in range(1, PER_ROW):
                length = jnp.where(spots >= slot * CAP_LEN, length_ref[captions[slot]], length)
            to_text = (
                slot_of(lax.broadcasted_iota(jnp.int32, (ROW_LEN, span), 0), ends)
                == spots // CAP_LEN
            ) & (spots % CAP_LEN < length)
            rows = pl.ds(pl.multiple_of(row * ROW_LEN, ROW_LEN), ROW_LEN)
            texts = pl.ds(row * PER_ROW, PER_ROW)
            for head in range(heads):
                text = [
                    caption_rows(text_ref, captions, part * inner + head * size, size)
                    for part in range(3)
                ]
                image = [
                    image_ref[rows, part * inner + head * size : part * inner + (head + 1) * size]
                    for part in range(3)
                ]
                lanes = slice(head * size, (head + 1) * size)
                shares = softmax_block(product_nt(text[0], image[1]) * scaling, to_image)
                text_shares[row, head] = shares
                text_out[texts, :, lanes] = (
                    product(shares, image[2]).astype(BF).reshape(PER_ROW, CAP_LEN, size)
                )
                shares = softmax_block(product_nt(image[0], text[1]) * scaling, to_text)
                image_shares[row, head] = shares
                image_out[rows, lanes] = product(shares, text[2]).astype(BF)
        return carry

    lax.fori_loop(0, rows_total // per_step, step, 0)


def co_backward_rows(bench, heads, rows_total):
    text_ref, image_ref = bench.co_t, bench.co_i
    inner = image_ref.shape[1] // 3
    size = inner // heads
    scaling = size ** (-0.5)
    span = PER_ROW * CAP_LEN
    per_step = 2
    order_ref = bench.order
    text_shares, image_shares = bench.cshare_t, bench.cshare_i
    text_grad, image_grad = bench.cg_t, bench.cg_i
    text_out, image_out = bench.rgrad_t, bench.grad_i

    def step(index, carry):
        for member in range(per_step):
            row = index * per_step + member
            captions = [order_ref[row * PER_ROW + slot] for slot in range(PER_ROW)]
            rows = pl.ds(pl.multiple_of(row * ROW_LEN, ROW_LEN), ROW_LEN)
            texts = pl.ds(row * PER_ROW, PER_ROW)
            for head in range(heads):
                text = [
                    caption_rows(text_ref, captions, part * inner + head * size, size)
                    for part in range(3)
                ]
                image = [
                    image_ref[rows, part * inner + head * size : part * inner + (head + 1) * size]
                    for part in range(3)
                ]
                text_q, image_k, image_v = attend_back(
                    text_shares[row, head], scaling, text[0], image[1], image[2],
                    caption_rows(text_grad, captions, head * size, size),
                )
                image_q, text_k, text_v = attend_back(
                    image_shares[row, head], scaling, image[0], text[1], text[2],
                    image_grad[rows, head * size : (head + 1) * size],
                )
                for part, grad in enumerate((text_q, text_k, text_v)):
                    at = part * inner + head * size
                    text_out[texts, :, at : at + size] = grad.reshape(PER_ROW, CAP_LEN, size)
                for part, grad in enumerate((image_q, image_k, image_v)):
                    at = part * inner + head * size
                    image_out[rows, at : at + size] = grad
        return carry

    lax.fori_loop(0, rows_total // per_step, step, 0)


def in_caption_order(bench, source, target):
    for caption in range(source.shape[0]):
        rows = slice(caption * CAP_LEN, (caption + 1) * CAP_LEN)
        target[rows, :] = source[bench.inverse[caption]]


def self_mask_text(length_ref, block):
    shape = (2 * CAP_LEN, 2 * CAP_LEN)
    queries = lax.broadcasted_iota(jnp.int32, shape, 0)
    spots = lax.broadcasted_iota(jnp.int32, shape, 1)
    length = jnp.where(
        spots >= CAP_LEN, length_ref[block * 2 + 1] + CAP_LEN, length_ref[block * 2]
    )
    return (queries // CAP_LEN == spots // CAP_LEN) & (spots < length)


def self_mask_image(region_ref, row):
    ends = row_ends(region_ref, row)
    shape = (ROW_LEN, ROW_LEN)
    return slot_of(lax.broadcasted_iota(jnp.int32, shape, 0), ends) == slot_of(
        lax.broadcasted_iota(jnp.int32, shape, 1), ends
    )


def shape_of(shape, dtype=BF):
    return jax.ShapeDtypeStruct(shape, dtype)


def cost(flops, moved, exps):
    return pl.CostEstimate(flops=int(flops), bytes_accessed=int(moved), transcendentals=int(exps))


MESH = pl.DeviceIdType.MESH
BIG_LIMIT = 60 * 1024 * 1024


class Bench:
    def __init__(self, refs, fetched, flushed, counts):
        self.refs = refs
        self.fetches = {}
        self.flushes = []
        self.flush_index = {name: i for i, name in enumerate(flushed)}
        self.copies = 0
        for index, name in enumerate(fetched):
            copy = pltpu.make_async_copy(
                refs["src " + name], refs[name], refs["fetch_sems"].at[index]
            )
            copy.start()
            self.fetches[name] = copy

    def __getattr__(self, name):
        fetches = self.__dict__["fetches"]
        if name in fetches:
            fetches.pop(name).wait()
        return self.__dict__["refs"][name]

    def flush(self, *names):
        for name in names:
            copy = pltpu.make_async_copy(
                self.refs[name],
                self.refs["dst " + name],
                self.refs["flush_sems"].at[self.flush_index.pop(name)],
            )
            copy.start()
            self.flushes.append(copy)

    def remote(self, source, target, peer):
        index = self.copies
        assert index < self.refs["send_sems"].shape[0]
        self.copies += 1
        return pltpu.make_async_remote_copy(
            src_ref=source,
            dst_ref=target,
            send_sem=self.refs["send_sems"].at[index],
            recv_sem=self.refs["recv_sems"].at[index],
            device_id=peer,
            device_id_type=MESH,
        )

    def close(self):
        for name in list(self.flush_index):
            self.flush(name)
        for copy in self.flushes:
            copy.wait()


def exchange_kernel(body, name, collective, peers, inputs, outputs, scratch, copies, work):
    fetched = [key for key, (_, kind) in inputs.items() if kind == "hbm"]
    flushed = [key for key, (_, _, kind) in outputs.items() if kind == "hbm"]
    spaces = {"hbm": pl.ANY, "vmem": pltpu.VMEM, "smem": pltpu.SMEM}
    names = [("src " + key if kind == "hbm" else key) for key, (_, kind) in inputs.items()]
    names += [("dst " + key if kind == "hbm" else key) for key, (_, _, kind) in outputs.items()]
    shapes = []
    for key in fetched:
        names.append(key)
        shapes.append(pltpu.VMEM(inputs[key][0].shape, inputs[key][0].dtype))
    for key in flushed:
        names.append(key)
        shapes.append(pltpu.VMEM(outputs[key][0], outputs[key][1]))
    for key, (shape, dtype) in scratch.items():
        names.append(key)
        shapes.append(pltpu.VMEM(shape, dtype))
    for key, count in (
        ("fetch_sems", len(fetched)), ("flush_sems", len(flushed)),
        ("send_sems", copies), ("recv_sems", copies),
    ):
        names.append(key)
        shapes.append(pltpu.SemaphoreType.DMA((max(count, 1),)))

    def kernel(*refs):
        bench = Bench(dict(zip(names, refs)), fetched, flushed, copies)
        barrier = pltpu.get_barrier_semaphore()
        partners = peers()
        for partner in partners:
            pl.semaphore_signal(barrier, inc=1, device_id=partner, device_id_type=MESH)
        pl.semaphore_wait(barrier, len(partners))
        body(bench)
        bench.close()

    flops, moved, exps = work
    results = pl.pallas_call(
        kernel,
        in_specs=[pl.BlockSpec(memory_space=spaces[kind]) for _, kind in inputs.values()],
        out_specs=[pl.BlockSpec(memory_space=spaces[kind]) for _, _, kind in outputs.values()],
        out_shape=[shape_of(shape, dtype) for shape, dtype, _ in outputs.values()],
        scratch_shapes=shapes,
        compiler_params=pltpu.CompilerParams(
            collective_id=collective, has_side_effects=True, vmem_limit_bytes=BIG_LIMIT
        ),
        cost_estimate=cost(flops, moved, exps),
        name=name,
    )(*[array for array, _ in inputs.values()])
    return dict(zip(outputs, results))


def group_peers():
    spot = lax.axis_index("mp")
    core = lax.rem(spot, 2)
    chip = lax.div(spot, 2)
    return core, {"mp": spot + 1 - 2 * core}, {"mp": spot + 2 - 4 * chip}


class Gather:
    def __init__(self, bench, rows):
        self.bench = bench
        self.rows = rows
        self.core, self.core_peer, self.chip_peer = group_peers()
        self.other = 1 - self.core

    def place(self, half, core):
        step = self.rows & -self.rows
        return pl.ds(pl.multiple_of((2 * half + core) * self.rows, step), self.rows)

    def gather(self, full):
        own = full.at[self.place(0, self.core)]
        far = full.at[self.place(1, self.core)]
        self.across = self.bench.remote(own, far, self.chip_peer)
        self.near = self.bench.remote(own, own, self.core_peer)
        self.relay = self.bench.remote(far, far, self.core_peer)
        self.across.start()
        self.near.start()

    def arrive(self, half, project):
        if half == 0:
            project(0, self.core)
            self.near.wait_recv()
            project(0, self.other)
        else:
            self.across.wait_recv()
            self.relay.start()
            project(1, self.core)
            self.relay.wait_recv()
            project(1, self.other)

    def finish_gather(self):
        self.across.wait_send()
        self.near.wait_send()
        self.relay.wait_send()


class Stream(Gather):
    def __init__(self, bench, tag, rows):
        super().__init__(bench, rows)
        for key in ("give", "got", "send", "recv", "acc"):
            setattr(self, key, getattr(bench, tag + "_" + key))

    def open_sum(self):
        self.hand = [
            self.bench.remote(self.give.at[half], self.got.at[half], self.core_peer)
            for half in (0, 1)
        ]
        self.post = self.bench.remote(self.send, self.recv, self.chip_peer)

    def partial(self, half, output):
        self.give[half] = output(half, self.other).astype(BF)
        self.hand[half].start()
        self.acc[half] = output(half, self.core)
        if half == 1:
            self.hand[1].wait_recv()
            self.send[...] = (self.acc[1] + self.got[1].astype(F32)).astype(BF)
            self.post.start()

    def settle(self, gathered=True):
        self.hand[0].wait_recv()
        self.post.wait_recv()
        self.hand[0].wait_send()
        self.hand[1].wait_send()
        self.post.wait_send()
        if gathered:
            self.finish_gather()

    def piece(self, rows):
        return self.acc[0, rows] + self.got[0, rows].astype(F32) + self.recv[rows].astype(F32)


CHUNK = 32


def chunks(count, step, start):
    def once(index, carry):
        return step(pl.ds(pl.multiple_of(index * CHUNK, CHUNK), CHUNK), carry)

    return lax.fori_loop(0, count // CHUNK, once, start)


def folded(values):
    return jnp.sum(values.reshape(CHUNK // 8, 8, values.shape[-1]), axis=0)


def stream_scratch(tag, rows, width):
    return {
        tag + "_give": ((2, rows, width), BF),
        tag + "_got": ((2, rows, width), BF),
        tag + "_send": ((rows, width), BF),
        tag + "_recv": ((rows, width), BF),
        tag + "_acc": ((2, rows, width), F32),
    }


def at_offset(ref, offset, rows):
    return ref.at[pl.ds(pl.multiple_of(offset + rows.start, CHUNK), rows.size)]


def attend_many(parts_ref, share_ref, context_ref, base, first_block, blocks, heads, masker):
    inner = parts_ref.shape[1] // 3
    size = inner // heads
    scaling = size ** (-0.5)
    rows = [
        pl.ds(pl.multiple_of(base + block * ROW_LEN, CHUNK), ROW_LEN) for block in range(blocks)
    ]
    masks = [masker(first_block + block) for block in range(blocks)]
    scores = []
    for block in range(blocks):
        for head in range(heads):
            queries = parts_ref[rows[block], head * size : (head + 1) * size]
            keys = parts_ref[rows[block], inner + head * size : inner + (head + 1) * size]
            scores.append(jnp.where(masks[block], product_nt(queries, keys) * scaling, -1e9))
    scores = jnp.concatenate(scores, axis=0)
    exponent = jnp.exp(scores - jnp.max(scores, axis=-1, keepdims=True))
    shares = (exponent / jnp.sum(exponent, axis=-1, keepdims=True)).astype(BF)
    for block in range(blocks):
        contexts = []
        for head in range(heads):
            at = (block * heads + head) * ROW_LEN
            piece = shares[at : at + ROW_LEN]
            share_ref[first_block + block, head] = piece
            values = parts_ref[rows[block], 2 * inner + head * size : 2 * inner + (head + 1) * size]
            contexts.append(product(piece, values).astype(BF))
        context_ref[rows[block], :] = jnp.concatenate(contexts, axis=1)


def norm_chunk(values, gain, shift):
    centre = values - jnp.mean(values, axis=-1, keepdims=True)
    spread = jnp.mean(centre * centre, axis=-1, keepdims=True)
    return centre * lax.rsqrt(spread + epsilon) * gain + shift


def forward_kernel(ctx_t, ctx_i, text_in, image_in, weights, norms, text_g, image_g, lengths, regions,
                   text_local, image_local):
    (co_text_out, co_image_out, text_up, text_down, image_up, image_down,
     w_self_text, text_self_out, w_self_image, image_self_out) = weights
    n_t, d_t = text_in.shape
    n_i, d_i = image_in.shape
    ff_t, ff_i = text_up.shape[1], image_up.shape[1]
    in_t, in_i = text_self_out.shape[0], image_self_out.shape[0]
    inputs = {
        "lengths": (lengths, "smem"), "regions": (regions, "smem"),
        "gains_t": (norms[0], "vmem"), "shifts_t": (norms[1], "vmem"),
        "gains_i": (norms[2], "vmem"), "shifts_i": (norms[3], "vmem"),
        "ctx_i": (ctx_i, "hbm"), "w_co_i": (co_image_out, "hbm"),
        "ctx_t": (ctx_t, "hbm"), "w_co_t": (co_text_out, "hbm"),
        "x_i": (image_in, "hbm"), "x_t": (text_in, "hbm"),
        "up_i": (image_up, "hbm"), "down_i": (image_down, "hbm"),
        "up_t": (text_up, "hbm"), "down_t": (text_down, "hbm"),
        "qkv_i": (w_self_image, "hbm"), "so_i": (image_self_out, "hbm"),
        "qkv_t": (w_self_text, "hbm"), "so_t": (text_self_out, "hbm"),
        "g_i": (image_g, "hbm"), "g_t": (text_g, "hbm"),
    }
    outputs = {}
    scratch = {}
    for tag, n, d, ff, inner, heads in (
        ("t", n_t, d_t, ff_t, in_t, text_local), ("i", n_i, d_i, ff_i, in_i, image_local),
    ):
        outputs.update({
            "zero_" + tag: ((n, d), F32, "hbm"),
            "mid_" + tag: ((n, d), F32, "hbm"),
            "mlp_" + tag: ((4 * n, d), BF, "hbm"),
            "act_" + tag: ((4 * n, ff), BF, "hbm"),
            "slope_" + tag: ((4 * n, ff), BF, "hbm"),
            "self_" + tag: ((4 * n, d), BF, "hbm"),
            "parts_" + tag: ((4 * n, 3 * inner), BF, "hbm"),
            "share_" + tag: ((4 * n // ROW_LEN, heads, ROW_LEN, ROW_LEN), BF, "hbm"),
            "ctx2_" + tag: ((4 * n, inner), BF, "hbm"),
            "late_" + tag: ((n, d), F32, "hbm"),
            "result_" + tag: ((n, d), BF, "hbm"),
            "gain_" + tag: ((8, d), F32, "vmem"),
            "shift_" + tag: ((8, d), F32, "vmem"),
        })
        scratch.update(stream_scratch(tag, n, d))
        scratch["first_" + tag] = ((n, d), F32)

    def body(bench):
        streams = {tag: Stream(bench, tag, n) for tag, n in (("i", n_i), ("t", n_t))}
        get = lambda key, tag: getattr(bench, key + "_" + tag)

        for tag, stream in streams.items():
            context, weight = get("ctx", tag), get("w_co", tag)
            output = lambda half, core: product(context[stream.place(half, core)], weight[...])
            stream.open_sum()
            stream.partial(1, output)
            stream.partial(0, output)

        def settle(tag, stage, source, kept, resid, full):
            stream = streams[tag]
            stream.settle(gathered=stage > 0)
            gain = get("gains", tag)[stage : stage + 1]
            shift = get("shifts", tag)[stage : stage + 1]
            base = stream.core * stream.rows

            def step(rows, carry):
                values = source[rows].astype(F32) + stream.piece(rows)
                kept[rows] = values
                normed = norm_chunk(values, gain, shift)
                resid[rows] = normed
                at_offset(full, base, rows)[...] = normed.astype(BF)
                return carry

            chunks(stream.rows, step, 0)
            bench.flush({"zero": "zero_", "mid": "mid_"}["zero" if stage == 0 else "mid"] + tag)
            stream.gather(full)

        for tag in streams:
            settle(tag, 0, get("x", tag), get("zero", tag), get("first", tag), get("mlp", tag))

        def feeds(tag):
            stream = streams[tag]
            full, up, down = get("mlp", tag), get("up", tag), get("down", tag)
            act, slope = get("act", tag), get("slope", tag)

            def project(half, core):
                place = stream.place(half, core)
                pre = product(full[place], up[...])
                cube = GELU_A * (pre + GELU_B * pre * pre * pre)
                bent = jnp.tanh(cube)
                act[place] = (0.5 * pre * (1.0 + bent)).astype(BF)
                slope[place] = (
                    0.5 * (1.0 + bent)
                    + 0.5 * pre * (1.0 - bent * bent) * GELU_A * (1.0 + 3.0 * GELU_B * pre * pre)
                ).astype(BF)

            def output(half, core):
                return product(act[stream.place(half, core)], down[...])

            return project, output

        def layer(work):
            for half in (0, 1):
                for tag, stream in streams.items():
                    hooks = work[tag]
                    if half == 0:
                        stream.open_sum()
                    stream.arrive(half, hooks[0])
                    if len(hooks) > 2:
                        hooks[2](half)
                    stream.partial(half, hooks[1])

        layer({tag: feeds(tag) for tag in streams})
        for tag in streams:
            settle(tag, 1, get("first", tag), get("mid", tag), get("first", tag), get("self", tag))
            bench.flush("mlp_" + tag, "act_" + tag, "slope_" + tag)

        def attends(tag):
            stream = streams[tag]
            full, qkv, out = get("self", tag), get("qkv", tag), get("so", tag)
            parts, share, context = get("parts", tag), get("share", tag), get("ctx2", tag)

            def output(half, core):
                return product(context[stream.place(half, core)], out[...])

            if tag == "t":

                def project(half, core):
                    place = stream.place(half, core)
                    project_three(full[place], qkv, parts, place)
                    quad = 2 * half + core
                    attend_many(
                        parts, share, context, quad * n_t, quad * (n_t // ROW_LEN),
                        n_t // ROW_LEN, text_local,
                        functools.partial(self_mask_text, bench.lengths),
                    )

                return project, output

            def project_image(half, core):
                place = stream.place(half, core)
                project_three(full[place], qkv, parts, place)

            def middle(half):
                blocks = 2 * n_i // ROW_LEN
                attend_many(
                    parts, share, context, 2 * half * n_i, half * blocks, blocks, image_local,
                    functools.partial(self_mask_image, bench.regions),
                )

            return project_image, output, middle

        layer({tag: attends(tag) for tag in streams})
        for tag, stream in streams.items():
            stream.settle()
            bench.flush("self_" + tag, "parts_" + tag, "share_" + tag, "ctx2_" + tag)
            gain, shift = get("gains", tag)[2:3], get("shifts", tag)[2:3]
            second, result, late, grad = (
                get("first", tag), get("result", tag), get("late", tag), get("g", tag)
            )
            width = second.shape[1]

            def step(rows, carry):
                values = second[rows] + stream.piece(rows)
                back, normed, gains, shifts = norm_pull(values, gain, shift, grad[rows].astype(F32))
                result[rows] = normed.astype(BF)
                late[rows] = back
                return carry[0] + gains, carry[1] + shifts

            start = jnp.zeros((8, width), F32)
            gains, shifts = chunks(stream.rows, step, (start, start))
            get("gain", tag)[...] = gains
            get("shift", tag)[...] = shifts
            bench.flush("result_" + tag, "late_" + tag)

    return exchange_kernel(
        body, "forward_tail", 1, lambda: list(group_peers()[1:]), inputs, outputs, scratch, 32,
        (15e9, 40e6, 1e6),
    )


def norm_pull(values, gain, shift, gradient):
    centre = values - jnp.mean(values, axis=-1, keepdims=True)
    spread = jnp.mean(centre * centre, axis=-1, keepdims=True)
    inverse = lax.rsqrt(spread + epsilon)
    unit = centre * inverse
    scaled = gradient * gain
    back = inverse * (
        scaled
        - jnp.mean(scaled, axis=-1, keepdims=True)
        - unit * jnp.mean(scaled * unit, axis=-1, keepdims=True)
    )
    return back, unit * gain + shift, folded(gradient * unit), folded(gradient)


def attend_back_many(parts_ref, share_ref, grads, out_ref, base, first_block, blocks, heads):
    inner = parts_ref.shape[1] // 3
    size = inner // heads
    scaling = size ** (-0.5)
    rows = [
        pl.ds(pl.multiple_of(base + block * ROW_LEN, CHUNK), ROW_LEN) for block in range(blocks)
    ]
    context_grads = [grads(block) for block in range(blocks)]
    pairs = [(block, head) for block in range(blocks) for head in range(heads)]

    def piece(part, block, head):
        at = part * inner + head * size
        return parts_ref[rows[block], at : at + size]

    def grad_of(block, head):
        return context_grads[block][:, head * size : (head + 1) * size]

    narrow = [share_ref[first_block + block, head] for block, head in pairs]
    shares = jnp.concatenate(narrow, axis=0).astype(F32)
    share_grad = jnp.concatenate(
        [product_nt(grad_of(*pair), piece(2, *pair)) for pair in pairs], axis=0
    )
    total = jnp.sum(share_grad * shares, axis=-1, keepdims=True)
    score_grad = (shares * (share_grad - total) * scaling).astype(BF)
    for block in range(blocks):
        pieces = [[], [], []]
        for head in range(heads):
            index = block * heads + head
            scores = score_grad[index * ROW_LEN : (index + 1) * ROW_LEN]
            pieces[0].append(product(scores, piece(1, block, head)).astype(BF))
            pieces[1].append(product_tn(scores, piece(0, block, head)).astype(BF))
            pieces[2].append(product_tn(narrow[index], grad_of(block, head)).astype(BF))
        out_ref[rows[block], :] = jnp.concatenate(pieces[0] + pieces[1] + pieces[2], axis=1)


class Split:
    def __init__(self, group_count, rows, order):
        self.bits = group_count.bit_length() - 1
        ready = group_count == 1 << self.bits and (rows // group_count) % 32 == 0
        self.fast = ready and group_count > 1
        self.blocks = group_count if self.fast else 1
        self.part = rows // self.blocks
        self.order = order(self.bits) if self.fast else []

    def position(self, block):
        spot = 0
        for bit in self.order:
            spot = 2 * spot + ((block >> bit) & 1)
        return spot

    def shape(self, columns):
        return (self.blocks, self.part, columns)

    def spare(self, columns):
        return (max(self.blocks - 1, 1), self.part, columns)


def dp_peer(bit):
    place = lax.axis_index("dp")
    value = lax.rem(lax.div(place, 1 << bit), 2)
    return value, {"dp": place + (1 << bit) * (1 - 2 * value)}


def dp_peers(*splits):
    bits = sorted({bit for split in splits for bit in split.order})
    return [dp_peer(bit)[1] for bit in bits]


class GroupSum:
    def __init__(self, bench, split, stack, spare, first=0, last=None):
        self.bench, self.split, self.stack, self.spare = bench, split, stack, spare
        self.base = 0
        self.size = split.blocks
        self.at = 0
        self.left = list(split.order)[first:last]
        for bit in split.order[:first]:
            self.size //= 2
            self.base = self.base + dp_peer(bit)[0] * self.size

    def start(self):
        if not self.left:
            return
        bit = self.left.pop(0)
        self.size //= 2
        value, peer = dp_peer(bit)
        given = self.base + (1 - value) * self.size
        self.base = self.base + value * self.size
        self.copy = self.bench.remote(
            self.stack.at[pl.ds(given, self.size)],
            self.spare.at[pl.ds(self.at, self.size)],
            peer,
        )
        self.copy.start()
        self.pending = True

    def advance(self):
        if not getattr(self, "pending", False):
            return
        self.copy.wait_recv()
        self.copy.wait_send()
        self.pending = False

        def add(index, carry):
            mine = self.base + index
            self.stack[mine] = (
                self.stack[mine].astype(F32) + self.spare[self.at + index].astype(F32)
            ).astype(BF)
            return carry

        lax.fori_loop(0, self.size, add, 0)
        self.at += self.size
        self.start()

    def drain(self):
        while getattr(self, "pending", False):
            self.advance()

    def finish(self, out):
        self.drain()
        out[...] = self.stack[self.base]


def weight_grad(split, stack, column, left, right):
    rows, width = left.shape[1], right.shape[1]
    tile = rows // 2
    for start in (0, tile):
        value = product_tn(left[:, start : start + tile], right[...]).astype(BF)
        if split.blocks == 1:
            stack[0, start : start + tile, column : column + width] = value
            continue
        for index in range(tile // split.part):
            spot = split.position(start // split.part + index)
            stack[spot, :, column : column + width] = value[
                index * split.part : (index + 1) * split.part
            ]


def project_three(rows, weights, target, place):
    width = weights.shape[2]
    for part in range(3):
        target[place, part * width : (part + 1) * width] = product(rows, weights[part]).astype(BF)


def back_three(grads, place, weights):
    width = weights.shape[2]
    return (
        product_nt(grads[place, :width], weights[0])
        + product_nt(grads[place, width : 2 * width], weights[1])
        + product_nt(grads[place, 2 * width :], weights[2])
    )


def run_layer(streams, work):
    for half in (0, 1):
        for tag, stream in streams.items():
            hooks = work[tag]
            if half == 0:
                stream.open_sum()
            stream.arrive(half, hooks[0])
            if len(hooks) > 2:
                hooks[2](half)
            stream.partial(half, hooks[1])


def spread(stream, source, full):
    base = stream.core * stream.rows

    def step(rows, carry):
        at_offset(full, base, rows)[...] = source[rows].astype(BF)
        return carry

    chunks(stream.rows, step, 0)
    stream.gather(full)


def settle_back(stream, resid, values, gain, target, gain_out, shift_out, full=None):
    base = stream.core * stream.rows

    def step(rows, carry):
        gradient = resid[rows] + stream.piece(rows)
        back, _, gains, shifts = norm_pull(values[rows], gain, 0.0, gradient)
        target[rows] = back
        if full is not None:
            at_offset(full, base, rows)[...] = back.astype(BF)
        return carry[0] + gains, carry[1] + shifts

    start = jnp.zeros((8, resid.shape[1]), F32)
    gains, shifts = chunks(stream.rows, step, (start, start))
    gain_out[...] = gains
    shift_out[...] = shifts


def self_back_kernel(late, mid, tokens, parts, share, context, qkv, out, gains, splits):
    inputs, outputs, scratch = {}, {}, {}
    for index, tag in ((1, "i"), (0, "t")):
        n, d = late[index].shape
        width = parts[index].shape[1]
        inputs.update({
            "gains_" + tag: (gains[index], "vmem"),
            "late_" + tag: (late[index], "hbm"),
            "so_" + tag: (out[index], "hbm"),
            "parts_" + tag: (parts[index], "hbm"),
            "share_" + tag: (share[index], "hbm"),
            "qkv_" + tag: (qkv[index], "hbm"),
            "self_" + tag: (tokens[index], "hbm"),
            "ctx2_" + tag: (context[index], "hbm"),
            "mid_" + tag: (mid[index], "hbm"),
        })
        outputs.update({
            "back_" + tag: ((n, d), F32, "hbm"),
            "stack_" + tag: (splits[index].shape(width + width // 3), BF, "hbm"),
            "gain_" + tag: ((8, d), F32, "vmem"),
            "shift_" + tag: ((8, d), F32, "vmem"),
        })
        scratch.update(stream_scratch(tag, n, d))
        scratch["full_" + tag] = ((4 * n, d), BF)
        scratch["grad_" + tag] = ((4 * n, width), BF)
    n_t, n_i = late[0].shape[0], late[1].shape[0]
    scratch["cg_i"] = ((4 * n_i, parts[1].shape[1] // 3), BF)
    heads = {"t": share[0].shape[1], "i": share[1].shape[1]}

    def body(bench):
        streams = {tag: Stream(bench, tag, n) for tag, n in (("i", n_i), ("t", n_t))}
        get = lambda key, tag: getattr(bench, key + "_" + tag)
        for tag, stream in streams.items():
            spread(stream, get("late", tag), get("full", tag))

        def hooks(tag):
            stream = streams[tag]
            full, out_w, qkv_w = get("full", tag), get("so", tag), get("qkv", tag)
            parts_ref, share_ref, grad = get("parts", tag), get("share", tag), get("grad", tag)

            def output(half, core):
                return back_three(grad, stream.place(half, core), qkv_w)

            if tag == "t":

                def project(half, core):
                    context_grad = product_nt(full[stream.place(half, core)], out_w[...]).astype(BF)
                    quad = 2 * half + core
                    blocks = n_t // ROW_LEN
                    attend_back_many(
                        parts_ref, share_ref,
                        lambda block: context_grad[block * ROW_LEN : (block + 1) * ROW_LEN],
                        grad, quad * n_t, quad * blocks, blocks, heads[tag],
                    )

                return project, output
            context_grads = bench.cg_i

            def project_image(half, core):
                place = stream.place(half, core)
                context_grads[place] = product_nt(full[place], out_w[...]).astype(BF)

            def middle(half):
                blocks = 2 * n_i // ROW_LEN
                base = 2 * half * n_i
                attend_back_many(
                    parts_ref, share_ref,
                    lambda block: context_grads[
                        base + block * ROW_LEN : base + (block + 1) * ROW_LEN
                    ],
                    grad, base, half * blocks, blocks, heads[tag],
                )

            return project_image, output, middle

        run_layer(streams, {tag: hooks(tag) for tag in streams})
        for index, tag in ((1, "i"), (0, "t")):
            stack, grad = get("stack", tag), get("grad", tag)
            weight_grad(splits[index], stack, 0, get("self", tag), grad)
            weight_grad(splits[index], stack, grad.shape[1], get("full", tag), get("ctx2", tag))
            bench.flush("stack_" + tag)
            stream = streams[tag]
            stream.settle()
            settle_back(
                stream, get("late", tag), get("mid", tag), get("gains", tag)[1:2],
                get("back", tag), get("gain", tag), get("shift", tag),
            )
            bench.flush("back_" + tag)

    return exchange_kernel(
        body, "self_back", 2, lambda: list(group_peers()[1:]), inputs, outputs, scratch, 16,
        (12e9, 40e6, 1e6),
    )


def feed_back_kernel(mid_grad, zero, tokens, act, slope, up, down, context, co_out, gains, stacks,
                     splits):
    inputs, outputs, scratch = {}, {}, {}
    for index, tag in ((1, "i"), (0, "t")):
        n, d = mid_grad[index].shape
        ff = act[index].shape[1]
        inner = context[index].shape[1]
        split = splits[index]
        columns = stacks[index].shape[2]
        inputs.update({
            "gains_" + tag: (gains[index], "vmem"),
            "mg_" + tag: (mid_grad[index], "hbm"),
            "stack_" + tag: (stacks[index], "hbm"),
            "down_" + tag: (down[index], "hbm"),
            "slope_" + tag: (slope[index], "hbm"),
            "up_" + tag: (up[index], "hbm"),
            "mlp_" + tag: (tokens[index], "hbm"),
            "act_" + tag: (act[index], "hbm"),
            "zero_" + tag: (zero[index], "hbm"),
            "co_" + tag: (co_out[index], "hbm"),
            "ctx_" + tag: (context[index], "hbm"),
        })
        outputs.update({
            "back_" + tag: ((n, d), F32, "hbm"),
            "cg_" + tag: ((4 * n, inner), BF, "hbm"),
            "out_grad_" + tag: (split.shape(inner), BF, "hbm"),
            "gain_" + tag: ((8, d), F32, "vmem"),
            "shift_" + tag: ((8, d), F32, "vmem"),
            "self_sum_" + tag: ((split.part, columns), BF, "hbm"),
            "fstack_" + tag: (split.shape(2 * ff), BF, "hbm"),
        })
        scratch.update(stream_scratch(tag, n, d))
        scratch["spare_" + tag] = (split.spare(columns), BF)
        scratch["fspare_" + tag] = (split.spare(2 * ff), BF)
        scratch["full_" + tag] = ((4 * n, d), BF)
        scratch["full2_" + tag] = ((4 * n, d), BF)
        scratch["pre_" + tag] = ((4 * n, ff), BF)
    n_t, n_i = mid_grad[0].shape[0], mid_grad[1].shape[0]

    def body(bench):
        streams = {tag: Stream(bench, tag, n) for tag, n in (("i", n_i), ("t", n_t))}
        get = lambda key, tag: getattr(bench, key + "_" + tag)
        for tag, stream in streams.items():
            spread(stream, get("mg", tag), get("full", tag))
        self_sums = {
            tag: GroupSum(bench, splits[index], get("stack", tag), get("spare", tag))
            for index, tag in ((1, "i"), (0, "t"))
        }
        for total in self_sums.values():
            total.start()

        def hooks(tag):
            stream = streams[tag]
            full, up_w, down_w = get("full", tag), get("up", tag), get("down", tag)
            slope_ref, pre = get("slope", tag), get("pre", tag)

            def project(half, core):
                place = stream.place(half, core)
                grad = product_nt(full[place], down_w[...])
                pre[place] = (grad * slope_ref[place].astype(F32)).astype(BF)

            def output(half, core):
                return product_nt(pre[stream.place(half, core)], up_w[...])

            return project, output

        run_layer(streams, {tag: hooks(tag) for tag in streams})
        for total in self_sums.values():
            total.advance()
        feed_sums = {}
        for index, tag in ((1, "i"), (0, "t")):
            stack, pre = get("fstack", tag), get("pre", tag)
            weight_grad(splits[index], stack, 0, get("mlp", tag), pre)
            weight_grad(splits[index], stack, pre.shape[1], get("full", tag), get("act", tag))
            feed_sums[tag] = GroupSum(bench, splits[index], stack, get("fspare", tag), 0, 1)
            feed_sums[tag].start()
            stream = streams[tag]
            stream.settle()
            settle_back(
                stream, get("mg", tag), get("zero", tag), get("gains", tag)[0:1],
                get("back", tag), get("gain", tag), get("shift", tag), get("full2", tag),
            )
            bench.flush("back_" + tag)
            stream.gather(get("full2", tag))
        for total in self_sums.values():
            total.advance()
        for half in (0, 1):
            for tag, stream in streams.items():
                full, weight, target = get("full2", tag), get("co", tag), get("cg", tag)

                def project(half, core):
                    place = stream.place(half, core)
                    target[place] = product_nt(full[place], weight[...]).astype(BF)

                stream.arrive(half, project)
        for index, tag in ((1, "i"), (0, "t")):
            bench.flush("cg_" + tag)
            weight_grad(
                splits[index], get("out_grad", tag), 0, get("full2", tag), get("ctx", tag)
            )
            bench.flush("out_grad_" + tag)
            streams[tag].finish_gather()
        for tag in streams:
            self_sums[tag].finish(get("self_sum", tag))
            bench.flush("self_sum_" + tag)
        for tag in streams:
            feed_sums[tag].drain()
            bench.flush("fstack_" + tag)

    return exchange_kernel(
        body, "feed_back", 3, lambda: list(group_peers()[1:]) + dp_peers(*splits), inputs, outputs,
        scratch, 40, (12e9, 60e6, 1e6),
    )


def co_front_kernel(shards, weights, order, inverse, regions, lengths, heads):
    inputs = {
        "order": (order, "smem"), "inverse": (inverse, "smem"),
        "regions": (regions, "smem"), "lengths": (lengths, "smem"),
    }
    outputs, scratch = {}, {}
    for index, tag in ((0, "t"), (1, "i")):
        n, d = shards[index].shape
        width = weights[index].shape[2]
        inputs.update({"x_" + tag: (shards[index], "hbm"), "w_" + tag: (weights[index], "hbm")})
        outputs.update({
            "all_" + tag: ((4 * n, d), BF, "hbm"),
            "co_" + tag: ((4 * n, 3 * width), BF, "hbm"),
            "ctx_" + tag: ((4 * n, width), BF, "hbm"),
        })
    n_t, n_i = shards[0].shape[0], shards[1].shape[0]
    held, width = n_t // CAP_LEN, weights[0].shape[2]
    outputs["co_t"] = ((4 * held, CAP_LEN, 3 * width), BF, "hbm")
    rows = 4 * n_i // ROW_LEN
    span = PER_ROW * CAP_LEN
    outputs["cshare_t"] = ((rows, heads, span, ROW_LEN), BF, "hbm")
    outputs["cshare_i"] = ((rows, heads, ROW_LEN, span), BF, "hbm")
    scratch["rctx_t"] = ((4 * held, CAP_LEN, width), BF)

    def body(bench):
        streams = {tag: Gather(bench, n) for tag, n in (("t", n_t), ("i", n_i))}
        get = lambda key, tag: getattr(bench, key + "_" + tag)
        for tag, stream in streams.items():
            full = get("all", tag)
            full[stream.place(0, stream.core)] = get("x", tag)[...]
            stream.gather(full)
        for half in (0, 1):
            for tag, stream in streams.items():
                full, weight, target = get("all", tag), get("w", tag), get("co", tag)

                def project(half, core):
                    place = stream.place(half, core)
                    if tag == "i":
                        project_three(full[place], weight, target, place)
                        return
                    captions = pl.ds((2 * half + core) * held, held)
                    for part in range(3):
                        target[captions, :, part * width : (part + 1) * width] = (
                            product(full[place], weight[part])
                            .astype(BF)
                            .reshape(held, CAP_LEN, width)
                        )

                stream.arrive(half, project)
        for tag in streams:
            bench.flush("all_" + tag, "co_" + tag)
        co_forward_rows(bench, heads, rows)
        in_caption_order(bench, bench.rctx_t, bench.ctx_t)
        for stream in streams.values():
            stream.finish_gather()

    return exchange_kernel(
        body, "co_front", 5, lambda: list(group_peers()[1:]), inputs, outputs, scratch, 6,
        (4e9, 20e6, 1e6),
    )


class Total:
    def __init__(self, bench, held, landing, group_count):
        self.bench, self.held, self.landing = bench, held, landing
        self.peers = list(group_peers()[1:]) + [
            dp_peer(bit)[1] for bit in range(group_count.bit_length() - 1)
        ]
        self.step = 0
        self.start()

    def start(self):
        if self.step < len(self.peers):
            self.copy = self.bench.remote(
                self.held.at[self.step], self.landing.at[self.step], self.peers[self.step]
            )
            self.copy.start()

    def advance(self):
        if self.step < len(self.peers):
            self.copy.wait()
            self.held[self.step + 1] = self.held[self.step] + self.landing[self.step]
            self.step += 1
            self.start()

    def finish(self, out):
        while self.step < len(self.peers):
            self.advance()
        out[...] = self.held[self.step]


def co_back_kernel(zero_grad, context_grads, tokens, projected, shares, weights, out_grads,
                   feed_stacks, norms, order, inverse, splits, heads, group_count):
    inputs = {"order": (order, "smem"), "inverse": (inverse, "smem")}
    outputs, scratch = {}, {}
    steps = 2 + group_count.bit_length() - 1
    for index, tag in ((1, "i"), (0, "t")):
        n, d = zero_grad[index].shape
        width = projected[index].shape[-1]
        inner = out_grads[index].shape[2]
        split = splits[index]
        feeds = feed_stacks[index].shape[2]
        inputs.update({"norm%d_%s" % (k, tag): (v, "vmem") for k, v in enumerate(norms[index])})
        inputs.update({
            "co_" + tag: (projected[index], "hbm"),
            "cg_" + tag: (context_grads[index], "hbm"),
            "cshare_" + tag: (shares[index], "hbm"),
            "fstack_" + tag: (feed_stacks[index], "hbm"),
            "ostack_" + tag: (out_grads[index], "hbm"),
            "x_" + tag: (tokens[index], "hbm"),
            "w_" + tag: (weights[index], "hbm"),
            "zg_" + tag: (zero_grad[index], "hbm"),
        })
        outputs.update({
            "in_grad_" + tag: ((n, d), F32, "hbm"),
            "feed_sum_" + tag: ((split.part, feeds), BF, "hbm"),
            "out_sum_" + tag: ((split.part, inner), BF, "hbm"),
            "qkv_sum_" + tag: ((split.part, width), BF, "hbm"),
            "norm_" + tag: ((8, d), F32, "vmem"),
        })
        scratch.update(stream_scratch(tag, n, d))
        scratch["grad_" + tag] = ((4 * n, width), BF)
        scratch["stack_" + tag] = (split.shape(width), BF)
        scratch["spare_" + tag] = (split.spare(width), BF)
        scratch["fspare_" + tag] = (split.spare(feeds), BF)
        scratch["ospare_" + tag] = (split.spare(inner), BF)
        scratch["held_" + tag] = ((steps + 1, 8, d), F32)
        scratch["landing_" + tag] = ((steps, 8, d), F32)
    n_t, n_i = zero_grad[0].shape[0], zero_grad[1].shape[0]
    scratch["rgrad_t"] = (projected[0].shape, BF)

    def body(bench):
        streams = {tag: Stream(bench, tag, n) for tag, n in (("i", n_i), ("t", n_t))}
        get = lambda key, tag: getattr(bench, key + "_" + tag)
        totals, early, late = [], [], {}
        for index, tag in ((1, "i"), (0, "t")):
            held = get("held", tag)
            vectors = [
                jnp.sum(get("norm%d" % k, tag)[...], axis=0, keepdims=True) for k in range(6)
            ]
            held[0] = jnp.concatenate(vectors + [jnp.zeros_like(vectors[0])] * 2, axis=0)
            totals.append(Total(bench, held, get("landing", tag), group_count))
            early.append(
                GroupSum(bench, splits[index], get("fstack", tag), get("fspare", tag), 1)
            )
            early.append(GroupSum(bench, splits[index], get("ostack", tag), get("ospare", tag)))
        for total in early:
            total.start()
        co_backward_rows(bench, heads, 4 * n_i // ROW_LEN)
        in_caption_order(bench, bench.rgrad_t, bench.grad_t)
        for total in totals:
            total.advance()
        for index, tag in ((1, "i"), (0, "t")):
            stack = get("stack", tag)
            weight_grad(splits[index], stack, 0, get("x", tag), get("grad", tag))
            late[tag] = GroupSum(bench, splits[index], stack, get("spare", tag))
            late[tag].start()
            stream = streams[tag]
            grad, weight = get("grad", tag), get("w", tag)
            output = lambda half, core: back_three(grad, stream.place(half, core), weight)
            stream.open_sum()
            stream.partial(1, output)
            stream.partial(0, output)
            for total in totals + early:
                total.advance()
        for total in totals:
            total.advance()
        for tag, stream in streams.items():
            late[tag].advance()
            resid, target = get("zg", tag), get("in_grad", tag)
            stream.settle(gathered=False)

            def step(rows, carry):
                target[rows] = resid[rows] + stream.piece(rows)
                return carry

            chunks(stream.rows, step, 0)
            bench.flush("in_grad_" + tag)
            for total in totals:
                total.advance()
        for tag, total in zip(("i", "t"), totals):
            total.finish(get("norm", tag))
        for tag in ("i", "t"):
            late[tag].advance()
        for tag, total in zip(("feed_sum_i", "out_sum_i", "feed_sum_t", "out_sum_t"), early):
            total.finish(getattr(bench, tag))
            bench.flush(tag)
        for tag in ("t", "i"):
            late[tag].finish(get("qkv_sum", tag))
            bench.flush("qkv_sum_" + tag)

    return exchange_kernel(
        body, "co_back", 4,
        lambda: list(group_peers()[1:])
        + [dp_peer(bit)[1] for bit in range(group_count.bit_length() - 1)],
        inputs, outputs, scratch, 16 + 2 * steps + 20, (8e9, 50e6, 1e6),
    )


def finish_kernel(sums):
    flat = []
    shapes = []
    for qkv, out, own, feed, in_grad in sums:
        part = qkv.shape[0]
        inner = own.shape[1] // 4
        flat += [qkv, out, own, feed, in_grad]
        shapes += [
            shape_of((3, part, qkv.shape[1] // 3), F32),
            shape_of((out.shape[1], part), F32),
            shape_of((3, part, inner), F32),
            shape_of((inner, part), F32),
            shape_of((part, feed.shape[1] // 2), F32),
            shape_of((feed.shape[1] // 2, part), F32),
            shape_of(in_grad.shape, F32),
        ]

    def kernel(*refs):
        for stream in range(2):
            qkv, out, own, feed, in_grad = refs[5 * stream : 5 * stream + 5]
            results = refs[10 + 7 * stream : 17 + 7 * stream]
            width = qkv.shape[1] // 3
            inner = own.shape[1] // 4
            for part in range(3):
                results[0][part] = qkv[:, part * width : (part + 1) * width].astype(F32)
                results[2][part] = own[:, part * inner : (part + 1) * inner].astype(F32)
            results[1][...] = out[...].astype(F32).T
            results[3][...] = own[:, 3 * inner :].astype(F32).T
            ff = feed.shape[1] // 2
            results[4][...] = feed[:, :ff].astype(F32)
            results[5][...] = feed[:, ff:].astype(F32).T
            results[6][...] = in_grad[...]

    return pl.pallas_call(
        kernel,
        in_specs=[pl.BlockSpec(memory_space=pltpu.VMEM)] * len(flat),
        out_specs=[pl.BlockSpec(memory_space=pltpu.VMEM)] * len(shapes),
        out_shape=shapes,
        compiler_params=pltpu.CompilerParams(vmem_limit_bytes=32 * 1024 * 1024),
        name="finish",
    )(*flat)


def apart(grad):
    rows, columns = grad.shape
    return jnp.transpose(grad.reshape(rows, 3, columns // 3), (1, 0, 2))


def finish_plain(qkv, out, own, feed, in_grad):
    qkv, out, own, feed = [value.astype(F32) for value in (qkv, out, own, feed)]
    inner, ff = own.shape[1] // 4, feed.shape[1] // 2
    return (
        apart(qkv), out.T, apart(own[:, : 3 * inner]), own[:, 3 * inner :].T,
        feed[:, :ff], feed[:, ff:].T, in_grad,
    )


def per_device(
    text_in,
    image_in,
    caption_lengths,
    region_lengths,
    image_caption,
    co_text_qkv,
    co_image_qkv,
    co_text_out,
    co_image_out,
    text_up,
    text_down,
    image_up,
    image_down,
    text_self_qkv,
    text_self_out,
    image_self_qkv,
    image_self_out,
    text_gains,
    text_shifts,
    image_gains,
    image_shifts,
    text_grad_out,
    image_grad_out,
):
    captions = image_caption.shape[1]
    part_count = lax.axis_size("mp")
    group_count = lax.axis_size("dp")
    spot = lax.axis_index("mp")
    core = spot % 2
    chip = spot // 2
    co_local = CO_HEADS // part_count
    text_local = TEXT_HEADS // part_count
    image_local = IMAGE_HEADS // part_count

    half = captions // 2
    turned = chip == 1
    flip = lambda values: jnp.where(turned, jnp.roll(values, half), values)
    lengths = flip(caption_lengths)
    regions = flip(region_lengths.reshape(-1))
    order = flip(image_caption[0])
    order = jnp.where(turned, (order + half) % captions, order)

    labels = jnp.arange(captions, dtype=jnp.int32)
    inverse = jnp.sum(
        labels[None, :] * (order[None, :] == labels[:, None]).astype(jnp.int32), axis=1
    )

    front = co_front_kernel(
        (text_in, image_in), (co_text_qkv, co_image_qkv), order, inverse, regions, lengths,
        co_local,
    )
    text_ctx, image_ctx = front["ctx_t"], front["ctx_i"]
    ahead = forward_kernel(
        text_ctx, image_ctx, text_in, image_in,
        (co_text_out, co_image_out, text_up, text_down, image_up, image_down,
         text_self_qkv, text_self_out, image_self_qkv, image_self_out),
        (text_gains, text_shifts, image_gains, image_shifts),
        text_grad_out, image_grad_out, lengths, regions, text_local, image_local,
    )
    splits = (
        Split(group_count, text_in.shape[1], lambda bits: list(range(bits))),
        Split(group_count, image_in.shape[1], lambda bits: ([1, 0] + list(range(2, bits)))[:bits]),
    )
    gains = (text_gains, image_gains)
    first_back = self_back_kernel(
        (ahead["late_t"], ahead["late_i"]), (ahead["mid_t"], ahead["mid_i"]),
        (ahead["self_t"], ahead["self_i"]), (ahead["parts_t"], ahead["parts_i"]),
        (ahead["share_t"], ahead["share_i"]), (ahead["ctx2_t"], ahead["ctx2_i"]),
        (text_self_qkv, image_self_qkv), (text_self_out, image_self_out), gains, splits,
    )
    second_back = feed_back_kernel(
        (first_back["back_t"], first_back["back_i"]), (ahead["zero_t"], ahead["zero_i"]),
        (ahead["mlp_t"], ahead["mlp_i"]), (ahead["act_t"], ahead["act_i"]),
        (ahead["slope_t"], ahead["slope_i"]), (text_up, image_up), (text_down, image_down),
        (text_ctx, image_ctx), (co_text_out, co_image_out), gains,
        (first_back["stack_t"], first_back["stack_i"]), splits,
    )

    norms = [
        [stage[key + tag] for key in ("gain_", "shift_") for stage in (second_back, first_back, ahead)]
        for tag in "ti"
    ]
    last_back = co_back_kernel(
        (second_back["back_t"], second_back["back_i"]),
        (second_back["cg_t"].reshape(captions, CAP_LEN, -1), second_back["cg_i"]),
        (front["all_t"], front["all_i"]), (front["co_t"], front["co_i"]),
        (front["cshare_t"], front["cshare_i"]), (co_text_qkv, co_image_qkv),
        (second_back["out_grad_t"], second_back["out_grad_i"]),
        (second_back["fstack_t"], second_back["fstack_i"]),
        norms, order, inverse, splits, co_local, group_count,
    )

    def over_groups(summed, split):
        if not split.fast:
            summed = lax.psum_scatter(summed, "dp", scatter_dimension=0, tiled=True)
        return summed

    sums = [
        [
            over_groups(last_back["qkv_sum_" + tag], split),
            over_groups(last_back["out_sum_" + tag], split),
            over_groups(second_back["self_sum_" + tag], split),
            over_groups(last_back["feed_sum_" + tag], split),
            last_back["in_grad_" + tag],
        ]
        for tag, split in zip("ti", splits)
    ]
    if all(split.fast for split in splits):
        finished = finish_kernel(sums)
        text_grads, image_grads = finished[:7], finished[7:]
    else:
        text_grads, image_grads = [finish_plain(*stream) for stream in sums]

    def norm_part(total):
        columns = total.shape[1] // (group_count * part_count)
        place = lax.axis_index("dp") * part_count + spot
        mine = lax.dynamic_slice_in_dim(total, place * columns, columns, axis=1)
        return mine[:3], mine[3:6]

    text_gain_grad, text_shift_grad = norm_part(last_back["norm_t"])
    image_gain_grad, image_shift_grad = norm_part(last_back["norm_i"])
    return (
        ahead["result_t"],
        ahead["result_i"],
        text_grads[6],
        image_grads[6],
        text_grads[0],
        image_grads[0],
        text_grads[1],
        image_grads[1],
        text_grads[4],
        text_grads[5],
        image_grads[4],
        image_grads[5],
        text_grads[2],
        text_grads[3],
        image_grads[2],
        image_grads[3],
        text_gain_grad,
        text_shift_grad,
        image_gain_grad,
        image_shift_grad,
    )


def solution(mesh):
    tokens = P(("dp", "mp"), None)
    stack_in = P(None, None, "mp")
    rows_in = P("mp", None)
    columns_in = P(None, "mp")
    in_specs = (
        tokens, tokens, P("dp"), P("dp", None), P("dp", None),
        stack_in, stack_in, rows_in, rows_in,
        columns_in, rows_in, columns_in, rows_in,
        stack_in, rows_in, stack_in, rows_in,
        P(), P(), P(), P(),
        tokens, tokens,
    )
    stack_out = P(None, "dp", "mp")
    rows_out = P("mp", "dp")
    columns_out = P("dp", "mp")
    norm_out = P(None, ("dp", "mp"))
    out_specs = (
        tokens, tokens, tokens, tokens,
        stack_out, stack_out, rows_out, rows_out,
        columns_out, rows_out, columns_out, rows_out,
        stack_out, rows_out, stack_out, rows_out,
        norm_out, norm_out, norm_out, norm_out,
    )
    return jax.shard_map(
        per_device, mesh=mesh, in_specs=in_specs, out_specs=out_specs, check_vma=False
    )
```

time: 527 us -> 395 us (0.75)
  Pallas kernels: 152 us -> 364 us
  waiting for transfers between devices: 116 us -> 0 us
  other arithmetic: 84.5 us -> 3.87 us
  local copies, waits for them, and re-layouts: 68.3 us -> 19.6 us
  matrix products: 48.5 us -> 0 us
  starting transfers between devices: 32.9 us -> 0 us
  between operations: 16.2 us -> 0.94 us
    pallas_call x1 -> x5, Pallas kernels: 118 us -> 362 us  [exchange_kernel(): pl.pallas_call(kernel, in_specs=[pl.BlockSpec(memory_space=spaces[kind])...]
    ppermute x52 -> x0, waiting for transfers between devices: 116 us -> none  [swap(): lax.ppermute(values, axis, [(i, i ^ flip) for i in range(lax.axis_size(ax...]
    dot_general x32 -> x0, matrix products: 48.5 us -> none  [the longest x18 23.5 us: product_nt(): lax.dot_general(former, latter, (((1,), (1,)), ((), ())), preferred_eleme...]
    ppermute x52 -> x0, starting transfers between devices: 32.6 us -> none  [swap(): lax.ppermute(values, axis, [(i, i ^ flip) for i in range(lax.axis_size(ax...]
    pallas_call x4 -> x1, Pallas kernels: 33.7 us -> 2.25 us  [finish_kernel(): pl.pallas_call(kernel, in_specs=[pl.BlockSpec(memory_space=pltpu.VMEM)] *...]
    unnamed x268 -> x30, local copies, waits for them, and re-layouts: 41.3 us -> 14 us
    convert_element_type x32 -> x0, other arithmetic: 23 us -> none  [the longest x6 6.02 us: scatter_sum(): sent = swap(over_cores(right).astype(BF), 'mp', 2)]
    reduce_sum x16 -> x1, other arithmetic: 22.4 us -> 0.63 us  [per_device(): jnp.sum(labels[None, :] * (order[None, :] == labels[:, None]).astype(jnp....]
  transfers between devices with their start and end apart: 54 -> 0, of which waited for: 15 -> 0; matrix products, arithmetic and copies ran while one was open for 34% -> 0% of each run, Pallas kernels for 5% -> 0%
where the time goes in v3:
time: 395 us; the launch traced here: 389 us
  Pallas kernels  364 us (92%)
  local copies, waits for them, and re-layouts  19.6 us (5%)
    pallas_call x5, Pallas kernels, exchange_kernel(): pl.pallas_call(kernel, in_specs=[pl.BlockSpec(memory_space=spaces[kind])...  362 us
    unnamed x30, local copies, waits for them, and re-layouts  14 us

profile of v3, /device:TPU:0, one launch (start us, length us, event | category | flops | bytes accessed | tf_op | source)
XLA Modules:
  0.0 388.6 jit_solution(6230020563568672588)
XLA Ops:
  0.7 0.8 fusion.5
  1.5 1.2 broadcast_select_fusion.5.refs_3_.refs_0_
  2.7 0.8 fusion.4
  3.5 0.7 fusion
  4.3 0.6 select_reduce_fusion.refs_1_
  4.9 0.8 copy.59
  5.7 0.8 fusion.3
  6.6 0.1 copy.57
  6.9 1.3 broadcast_select_fusion.2
  8.2 2.3 copy.60.refs_18_.refs_14_
  10.5 31.4 %co_front.1 = (bf16[1536,768]{1,0:T(8,128)(2,1)}, bf16[24,64,768]{2,1,0:T(8,128)(2,1)}, bf16[1536,256]{1,0:T(8,128)(2,1)}, bf16[768,1024]{1,0:T(8,128)(2,1)}, bf...) custom-call(s32[24]{0:T(128)} %get-tuple-element.252.refs_0_, ...), custom_call_target="tpu_custom_call" | custom-call | flops 4000000000 | bytes 20000000 | tf_op jit(solution)/shard_map/co_front/pallas_call | solution.py:327
  41.9 117.6 %forward_tail.1 = (f32[384,768]{1,0:T(8,128)}, f32[384,768]{1,0:T(8,128)}, bf16[1536,768]{1,0:T(8,128)(2,1)}, bf16[1536,768]{1,0:T(8,128)(2,1)}, bf16[1536,768]{...) custom-call(s32[24]{0:T(128)} %broadcast_select_fusion.5.refs_3_.ref, ...), custom_call_target="tpu_custom_call" | custom-call | flops 15000000512 | bytes 40000000 | tf_op jit(solution)/shard_map/forward_tail/pallas_call | solution.py:327
  159.5 51.3 %self_back.1 = (f32[192,1024]{1,0:T(8,128)}, bf16[8,128,1024]{2,1,0:T(8,128)(2,1)}, f32[8,1024]{1,0:T(8,128)}, f32[8,1024]{1,0:T(8,128)}, f32[384,768]{1,0:T(8,1...) custom-call(f32[3,1024]{1,0:T(4,128)} %refs_0_.3, f32[192,1024]{1,0:T(8,128)} %get-tuple-element.104.refs_1_, ...), custom_call_target="tpu_custom_call" | custom-call | flops 12000000000 | bytes 40000000 | tf_op jit(solution)/shard_map/self_back/pallas_call | solution.py:327
  210.8 75.0 %feed_back.1 = (f32[192,1024]{1,0:T(8,128)}, bf16[768,256]{1,0:T(8,128)(2,1)}, bf16[8,128,256]{2,1,0:T(8,128)(2,1)}, f32[8,1024]{1,0:T(8,128)}, f32[8,1024]{1,0:...) custom-call(f32[3,1024]{1,0:T(4,128)} %refs_0_.3, ...), custom_call_target="tpu_custom_call" | custom-call | flops 12000000000 | bytes 60000000 | tf_op jit(solution)/shard_map/feed_back/pallas_call | solution.py:327
  285.9 86.7 %co_back.1 = (f32[192,1024]{1,0:T(8,128)}, bf16[128,512]{1,0:T(8,128)(2,1)}, bf16[128,256]{1,0:T(8,128)(2,1)}, bf16[128,768]{1,0:T(8,128)(2,1)}, f32[8,1024]{1,0...) custom-call(s32[24]{0:T(128)} %get-tuple-element.252.refs_0_, ...), custom_call_target="tpu_custom_call" | custom-call | flops 8000000000 | bytes 50000000 | tf_op jit(solution)/shard_map/co_back/pallas_call | solution.py:327
  372.6 0.8 constant_dynamic-slice_fusion.1
  373.3 0.6 fusion.2
  373.9 0.8 constant_dynamic-slice_fusion
  374.7 0.6 fusion.1
  375.3 1.3 copy-done
  376.5 1.1 copy-done.1
  377.7 1.0 copy-done.2
  378.6 0.9 copy-done.4
  379.6 0.9 copy-done.6
  380.5 0.9 copy-done.7
  381.4 0.8 copy-done.8
  382.2 0.8 copy-done.9
  383.0 2.3 finish.1
  385.3 0.7 copy.62
  386.0 0.9 copy.63
  386.9 0.8 copy.66
  387.7 0.7 copy.67
  (20 shorter events, 0.4 us)
Async XLA Ops:
  285.8 89.4 %copy-start.3 = (bf16[128,1024]{1,0:T(8,128)(2,1)S(1)}, bf16[128,1024]{1,0:T(8,128)(2,1)}, u32[]{:S(2)}) copy-start(bf16[128,1024]{1,0:T(8,128)(2,1)} %get-tuple-element.161.refs_7_) | copy-start | bytes 786436
  285.8 89.4 %copy-start.5 = (bf16[96,768]{1,0:T(8,128)(2,1)S(1)}, bf16[96,768]{1,0:T(8,128)(2,1)}, u32[]{:S(2)}) copy-start(bf16[96,768]{1,0:T(8,128)(2,1)} %get-tuple-element.156.refs_2_) | copy-start | bytes 442372
  375.3 1.3 copy-start
  376.5 1.1 copy-start.1
  377.7 1.0 copy-start.2
  378.6 0.9 copy-start.4
  379.6 0.9 copy-start.6
  380.5 0.9 copy-start.7
  381.4 0.8 copy-start.8
  382.2 0.8 copy-start.9
  385.3 1.6 copy-start.10
  385.3 2.4 copy-start.11
